TPU v7x, 32 devices: a whole 2x2x4 slice. The times are simulated.
32 devices in a mesh: seq: 16 (over z, x, core), head: 2 (over y).
Axes of the slice: x: 2, y: 2, z: 4, core: 2. Of those that a mesh axis runs over, the one named last changes fastest.
Arguments:
- tokens: bfloat16 [98304, 256], P(('seq', 'head')), may hold values from -6 to 6
- cotangent: bfloat16 [98304, 256], P(('seq', 'head')), may hold values from -6 to 6
- image_rows: int32 [128], replicated, may hold values from 1 to 32, as said below
- image_fill: int32 [128], replicated, may hold values from 1 to 96
- first_gain: float32 [256], replicated, may hold values from 0.1 to 1.9
- first_shift: float32 [256], replicated, may hold values from -2 to 2
- query_weight: bfloat16 [256, 256], P(None, 'head'), may hold values from -0.375 to 0.375
- key_weight: bfloat16 [256, 256], P(None, 'head'), may hold values from -0.375 to 0.375
- value_weight: bfloat16 [256, 256], P(None, 'head'), may hold values from -0.375 to 0.375
- out_weight: bfloat16 [256, 256], P('head'), may hold values from -2 to 2
- second_gain: float32 [256], replicated, may hold values from 0.1 to 1.9
- second_shift: float32 [256], replicated, may hold values from -2 to 2
- up_weight: bfloat16 [256, 1024], replicated, may hold values from -0.375 to 0.375
- up_bias: float32 [1024], replicated, may hold values from -3 to 3
- down_weight: bfloat16 [1024, 256], replicated, may hold values from -0.375 to 0.375
- down_bias: float32 [256], replicated, may hold values from -2 to 2
Outputs:
- mixed: bfloat16 [98304, 256], P(('seq', 'head'))
- input_grad: bfloat16 [98304, 256], P(('seq', 'head'))
- first_gain_grad: float32 [256], replicated
- first_shift_grad: float32 [256], replicated
- query_grad: float32 [256, 256], P(None, 'head')
- key_grad: float32 [256, 256], P(None, 'head')
- value_grad: float32 [256, 256], P(None, 'head')
- out_grad: float32 [256, 256], P('head')
- second_gain_grad: float32 [256], replicated
- second_shift_grad: float32 [256], replicated
- up_grad: float32 [256, 1024], replicated
- up_bias_grad: float32 [1024], replicated
- down_grad: float32 [1024, 256], replicated
- down_bias_grad: float32 [256], replicated
Inputs may be any that keep to these rules, and one draw needn't show every extreme that they name: `image_rows`: image 1 has exactly 32 rows; the rows sum to 1024; the number of rows before any image but the first is never a multiple of 4.
All inputs are finite; a program needn't handle non-finite values.
Results may differ from a plain program's by a relative error of at most 0.012.
Values may be sent and summed in bfloat16 or wider, within the bound.
No kernel may reach another device: no remote copies, remote signals or barrier semaphores. Data moves between devices by JAX's collectives and lax.ppermute only.
A program may use at most 192 MiB of HBM per device.

v0:
```python
import functools

import jax
import jax.numpy as jnp
from jax import lax
from jax.experimental import pallas as pl
from jax.experimental.pallas import tpu as pltpu
from jax.sharding import PartitionSpec as P

HEAD_DIM = 128
HEADS = 2
WINDOW = 96
BOTH = ("seq", "head")

EPSILON = 1e-05
MASKED = -1000000000.0
LOG2E = 1.4426950408889634
SCALE = HEAD_DIM ** (-0.5)

F32 = jnp.float32
BF16 = jnp.bfloat16
LANES = (((1,), (1,)), ((), ()))
ROWS = (((0,), (0,)), ((), ()))


def dot(a, b):
    return jnp.dot(a, b, preferred_element_type=F32)


def dot_lanes(a, b):
    return lax.dot_general(a, b, LANES, preferred_element_type=F32)


def dot_rows(a, b):
    return lax.dot_general(a, b, ROWS, preferred_element_type=F32)


def standardize(inputs):
    center = inputs - jnp.mean(inputs, axis=1, keepdims=True)
    spread = jnp.mean(center * center, axis=1, keepdims=True)
    inverse = lax.rsqrt(spread + EPSILON)
    return center * inverse, inverse


def normalize_back(weighted, scaled, inverse):
    return inverse * (
        weighted
        - jnp.mean(weighted, axis=1, keepdims=True)
        - scaled * jnp.mean(weighted * scaled, axis=1, keepdims=True)
    )


def gelu_pair(x):
    below = 0.5 * (1.0 + lax.erf(x * 0.7071067811865476))
    bell = jnp.exp2(x * x * (-0.5 * LOG2E))
    return x * below, below + x * bell * 0.3989422804014327


def column_sums(value):
    return jnp.sum(value, axis=0, keepdims=True)


def layer_kernel(
    rows,
    x_ref,
    cot_ref,
    first_ref,
    fill_ref,
    gain1_ref,
    shift1_ref,
    heads_ref,
    gain2_ref,
    shift2_ref,
    up_ref,
    up_bias_ref,
    down_ref,
    down_bias_ref,
    mixed_ref,
    in_grad_ref,
    grads_ref,
    wqkv,
    wout,
    normed,
    xhat,
    inv,
    qbuf,
    kbuf,
    vbuf,
    att,
    probs,
    mid_grad,
    att_grad,
    dq,
    dk,
    dv,
    act,
    hid_grad,
    acc_down,
    acc_up,
    acc_qkv,
    acc_out,
    acc_vec,
):
    D = x_ref.shape[1]
    FF = up_ref.shape[1]
    for part in range(3):
        for h in range(HEADS):
            wqkv[:, part * D + h * HEAD_DIM : part * D + (h + 1) * HEAD_DIM] = heads_ref[
                h, part * D : (part + 1) * D, :
            ]
    for h in range(HEADS):
        for half in range(D // HEAD_DIM):
            wout[h * HEAD_DIM : (h + 1) * HEAD_DIM, half * HEAD_DIM : (half + 1) * HEAD_DIM] = (
                heads_ref[h, 3 * D + half * HEAD_DIM : 3 * D + (half + 1) * HEAD_DIM, :]
            )
    acc_down[...] = jnp.zeros_like(acc_down)
    acc_up[...] = jnp.zeros_like(acc_up)
    acc_qkv[...] = jnp.zeros_like(acc_qkv)
    acc_out[...] = jnp.zeros_like(acc_out)
    acc_vec[...] = jnp.zeros_like(acc_vec)

    rows_a = 17 if (rows + 2) % 17 == 0 else 1
    step_a = rows_a * WINDOW // 3

    def project(i, _):
        here = pl.ds(pl.multiple_of(i * step_a, 16), step_a)
        scaled, inverse = standardize(x_ref[here, :].astype(F32))
        xhat[here, :] = scaled
        inv[here, :] = inverse
        value = (scaled * gain1_ref[...] + shift1_ref[...]).astype(BF16)
        normed[here, :] = value
        qkv = dot(value, wqkv[...]).astype(BF16)
        qbuf[here, :] = qkv[:, :D]
        kbuf[here, :] = qkv[:, D : 2 * D]
        vbuf[here, :] = qkv[:, 2 * D :]
        return 0

    lax.fori_loop(0, (rows + 2) * WINDOW // step_a, project, 0)

    key_id = lax.broadcasted_iota(jnp.int32, (WINDOW, WINDOW), 0)
    query_id = lax.broadcasted_iota(jnp.int32, (WINDOW, WINDOW), 1)
    current = key_id <= query_id
    place = jnp.where(current, key_id, key_id - WINDOW)

    group = 3 if (rows + 1) % 3 == 0 else 1

    def attend(i, _):
        for g in range(group):
            r = i * group + g
            lowest = jnp.where(first_ref[r] > 0, 0, -WINDOW)
            keep = (place >= lowest) & (place < fill_ref[r])
            at = pl.multiple_of(r * WINDOW, 16)
            for h in range(HEADS):
                cols = slice(h * HEAD_DIM, (h + 1) * HEAD_DIM)
                keys = kbuf[pl.ds(at, 2 * WINDOW), cols]
                values = vbuf[pl.ds(at, 2 * WINDOW), cols]
                query = qbuf[pl.ds(at + WINDOW, WINDOW), cols]
                raw = dot_lanes(keys, query)
                scores = jnp.where(current, raw[WINDOW:], raw[:WINDOW]) * (SCALE * LOG2E)
                scores = jnp.where(keep, scores, MASKED * LOG2E)
                lifted = jnp.exp2(scores - jnp.max(scores, axis=0, keepdims=True))
                weights = lifted / jnp.sum(lifted, axis=0, keepdims=True)
                probs[r * HEADS + h] = weights
                both = jnp.concatenate(
                    [jnp.where(current, 0.0, weights), jnp.where(current, weights, 0.0)]
                ).astype(BF16)
                att[pl.ds(at, WINDOW), cols] = dot_rows(both, values).astype(BF16)
        return 0

    lax.fori_loop(0, (rows + 1) // group, attend, 0)

    def feed_forward(at, count, own):
        here = pl.ds(at, count)
        attended = att[here, :]
        cot = cot_ref[here, :]
        cot32 = cot.astype(F32)
        middle = x_ref[pl.ds(at + WINDOW, count), :].astype(F32) + dot(attended, wout[...])
        scaled, inverse = standardize(middle)
        normed_two = (scaled * gain2_ref[...] + shift2_ref[...]).astype(BF16)
        block = 256
        for f in range(FF // block):
            cols = slice(f * block, (f + 1) * block)
            hidden = dot(normed_two, up_ref[:, cols]) + up_bias_ref[:, cols]
            active, slope = gelu_pair(hidden)
            grad = (dot_lanes(cot, down_ref[cols, :]) * slope).astype(BF16)
            hid_grad[:count, cols] = grad
            if own:
                act[:count, cols] = active.astype(BF16)
                acc_vec[8:9, cols] += column_sums(grad.astype(F32))
        if own:
            mixed_ref[here, :] = (
                middle + dot(act[:count], down_ref[...]) + down_bias_ref[...]
            ).astype(BF16)
            acc_down[...] += dot_rows(cot, act[:count])
            acc_up[...] += dot_rows(normed_two, hid_grad[:count])
        g2 = dot_lanes(hid_grad[:count], up_ref[...])
        middle_grad = cot32 + normalize_back(g2 * gain2_ref[...], scaled, inverse)
        mixing_grad = middle_grad.astype(BF16)
        if own:
            mid_grad[here, :] = middle_grad
            acc_vec[2:3, :D] += column_sums(g2 * scaled)
            acc_vec[3:4, :D] += column_sums(g2)
            acc_vec[4:5, :D] += column_sums(cot32)
            acc_out[...] += dot_rows(attended, mixing_grad)
        att_grad[here, :] = dot_lanes(mixing_grad, wout[...]).astype(BF16)

    step_f = 4 * WINDOW if rows % 4 == 0 else WINDOW

    def feed_step(i, _):
        feed_forward(pl.multiple_of(i * step_f, 16), step_f, True)
        return 0

    lax.fori_loop(0, rows * WINDOW // step_f, feed_step, 0)
    feed_forward(rows * WINDOW, WINDOW, False)

    dk[:WINDOW, :] = jnp.zeros((WINDOW, D), F32)
    dv[:WINDOW, :] = jnp.zeros((WINDOW, D), F32)

    def attend_back(i, _):
        for g in range(group):
            r = i * group + g
            at = pl.multiple_of(r * WINDOW, 16)
            for h in range(HEADS):
                cols = slice(h * HEAD_DIM, (h + 1) * HEAD_DIM)
                keys = kbuf[pl.ds(at, 2 * WINDOW), cols]
                values = vbuf[pl.ds(at, 2 * WINDOW), cols]
                query = qbuf[pl.ds(at + WINDOW, WINDOW), cols]
                upstream = att_grad[pl.ds(at, WINDOW), cols]
                weights = probs[r * HEADS + h]
                raw = dot_lanes(values, upstream)
                dweights = jnp.where(current, raw[WINDOW:], raw[:WINDOW])
                inner = jnp.sum(weights * dweights, axis=0, keepdims=True)
                dscores = weights * (dweights - inner)
                both = jnp.concatenate(
                    [jnp.where(current, 0.0, dscores), jnp.where(current, dscores, 0.0)]
                ).astype(BF16)
                both_w = jnp.concatenate(
                    [jnp.where(current, 0.0, weights), jnp.where(current, weights, 0.0)]
                ).astype(BF16)
                key_part = dot(both, query) * SCALE
                value_part = dot(both_w, upstream)
                dk[pl.ds(at, WINDOW), cols] += key_part[:WINDOW]
                dk[pl.ds(at + WINDOW, WINDOW), cols] = key_part[WINDOW:]
                dv[pl.ds(at, WINDOW), cols] += value_part[:WINDOW]
                dv[pl.ds(at + WINDOW, WINDOW), cols] = value_part[WINDOW:]
                dq[pl.ds(at, WINDOW), cols] = (dot_rows(both, keys) * SCALE).astype(BF16)
        return 0

    lax.fori_loop(0, (rows + 1) // group, attend_back, 0)

    def project_back(i, _):
        at = pl.multiple_of(i * step_f, 16)
        here = pl.ds(at, step_f)
        there = pl.ds(at + WINDOW, step_f)
        grads = jnp.concatenate(
            [dq[here, :], dk[there, :].astype(BF16), dv[there, :].astype(BF16)], axis=1
        )
        acc_qkv[...] += dot_rows(normed[there, :], grads)
        g1 = dot_lanes(grads, wqkv[...])
        scaled = xhat[there, :]
        acc_vec[0:1, :D] += column_sums(g1 * scaled)
        acc_vec[1:2, :D] += column_sums(g1)
        in_grad_ref[here, :] = (
            mid_grad[here, :] + normalize_back(g1 * gain1_ref[...], scaled, inv[there, :])
        ).astype(BF16)
        return 0

    lax.fori_loop(0, rows * WINDOW // step_f, project_back, 0)

    for f in range(FF // D):
        cols = slice(f * D, (f + 1) * D)
        grads_ref[f * D : (f + 1) * D, :] = acc_down[:, cols].T.astype(BF16)
        grads_ref[FF + f * D : FF + (f + 1) * D, :] = acc_up[:, cols].astype(BF16)
    base = 2 * FF
    for part in range(3):
        grads_ref[base + part * D : base + (part + 1) * D, :] = acc_qkv[
            :, part * D : (part + 1) * D
        ].astype(BF16)
    grads_ref[base + 3 * D : base + 4 * D, :] = acc_out[...].astype(BF16)
    base = base + 4 * D
    tail = grads_ref.shape[0] - base
    vectors = jnp.concatenate(
        [acc_vec[0:8, :D]] + [acc_vec[8:9, f * D : (f + 1) * D] for f in range(FF // D)]
        + [jnp.zeros((tail - 8 - FF // D, D), F32)]
    )
    grads_ref[base:, :] = vectors.astype(BF16)


def layer(x_ext, cot_ext, first, fill, gain1, shift1, heads, gain2, shift2, up, up_bias, down, down_bias, piece):
    count, D = x_ext.shape
    FF = up.shape[1]
    rows = count // WINDOW - 2
    own = rows * WINDOW
    grad_rows = 2 * FF + 4 * D + 16
    grad_rows = -(-grad_rows // piece) * piece
    vmem = pl.BlockSpec(memory_space=pltpu.VMEM)
    smem = pl.BlockSpec(memory_space=pltpu.SMEM)
    step_f = 4 * WINDOW if rows % 4 == 0 else WINDOW
    return pl.pallas_call(
        functools.partial(layer_kernel, rows),
        out_shape=(
            jax.ShapeDtypeStruct((own, D), BF16),
            jax.ShapeDtypeStruct((own, D), BF16),
            jax.ShapeDtypeStruct((grad_rows, D), BF16),
        ),
        in_specs=[vmem, vmem, smem, smem] + [vmem] * 9,
        out_specs=(vmem, vmem, vmem),
        scratch_shapes=[
            pltpu.VMEM((D, 3 * D), BF16),
            pltpu.VMEM((D, D), BF16),
            pltpu.VMEM((count, D), BF16),
            pltpu.VMEM((count, D), F32),
            pltpu.VMEM((count, 1), F32),
            pltpu.VMEM((count, D), BF16),
            pltpu.VMEM((count, D), BF16),
            pltpu.VMEM((count, D), BF16),
            pltpu.VMEM((count - WINDOW, D), BF16),
            pltpu.VMEM(((rows + 1) * HEADS, WINDOW, WINDOW), F32),
            pltpu.VMEM((own, D), F32),
            pltpu.VMEM((count - WINDOW, D), BF16),
            pltpu.VMEM((count - WINDOW, D), BF16),
            pltpu.VMEM((count, D), F32),
            pltpu.VMEM((count, D), F32),
            pltpu.VMEM((step_f, FF), BF16),
            pltpu.VMEM((step_f, FF), BF16),
            pltpu.VMEM((D, FF), F32),
            pltpu.VMEM((D, FF), F32),
            pltpu.VMEM((D, 3 * D), F32),
            pltpu.VMEM((D, D), F32),
            pltpu.VMEM((16, FF), F32),
        ],
        compiler_params=pltpu.CompilerParams(vmem_limit_bytes=56 * 1024 * 1024),
        name="layer",
    )(x_ext, cot_ext, first, fill, gain1, shift1, heads, gain2, shift2, up, up_bias, down, down_bias)


def row_marks(image_rows, image_fill, first_row, count):
    ends = jnp.cumsum(image_rows, dtype=jnp.int32)
    starts = ends - image_rows
    row = first_row + jnp.arange(count, dtype=jnp.int32)
    opens = jnp.any(starts[None, :] == row[:, None], axis=1) | (row >= ends[-1])
    short = jnp.sum(
        jnp.where(ends[None, :] == row[:, None] + 1, WINDOW - image_fill[None, :], 0),
        axis=1,
        dtype=jnp.int32,
    )
    return opens.astype(jnp.int32), WINDOW - short


def swapped(value, mask):
    count = lax.axis_size("seq") * lax.axis_size("head")
    return lax.ppermute(value, BOTH, [(i, i ^ mask) for i in range(count)])


def stages():
    count = lax.axis_size("seq") * lax.axis_size("head")
    bits = [1 << b for b in range(count.bit_length() - 1)]
    if len(bits) < 3:
        return [bits]
    rest = bits[3:]
    return [[bits[1]], [bits[0], bits[2]]] + [rest[i : i + 2] for i in range(0, len(rest), 2)]


def spans(masks):
    found = [0]
    for mask in masks:
        found = found + [f ^ mask for f in found]
    return found


def all_sum(value):
    place = lax.axis_index("seq") * lax.axis_size("head") + lax.axis_index("head")
    width = value.shape[1]
    codes = []
    for masks in stages():
        code = sum(((place & mask) // mask) << j for j, mask in enumerate(masks))
        codes.append(code)
        parts = value.reshape(1 << len(masks), -1, width)
        total = lax.dynamic_index_in_dim(parts, code, 0, False).astype(F32)
        arrived = [
            swapped(lax.dynamic_index_in_dim(parts, code ^ k, 0, False), mask)
            for k, mask in enumerate(spans(masks))
            if k
        ]
        for part in arrived:
            total = total + part.astype(F32)
        value = total.astype(BF16)
    for masks, code in list(zip(stages(), codes))[::-1]:
        found = [value] + [swapped(value, mask) for k, mask in enumerate(spans(masks)) if k]
        whole = jnp.zeros((len(found),) + value.shape, value.dtype)
        for k, part in enumerate(found):
            whole = lax.dynamic_update_index_in_dim(whole, part, code ^ k, 0)
        value = whole.reshape(-1, width)
    return value


def shards(
    tokens,
    cotangent,
    image_rows,
    image_fill,
    first_gain,
    first_shift,
    query_weight,
    key_weight,
    value_weight,
    out_weight,
    second_gain,
    second_shift,
    up_weight,
    up_bias,
    down_weight,
    down_bias,
):
    own, D = tokens.shape
    FF = up_weight.shape[1]
    devices = lax.axis_size("seq") * lax.axis_size("head")
    head = lax.axis_index("head")
    place = lax.axis_index("seq") * lax.axis_size("head") + head
    rows = own // WINDOW
    mine = jnp.concatenate(
        [query_weight, key_weight, value_weight]
        + [out_weight[:, c : c + HEAD_DIM] for c in range(0, D, HEAD_DIM)]
    )
    other = lax.ppermute(mine, "head", [(0, 1), (1, 0)])
    before = lax.ppermute(tokens[own - WINDOW :], BOTH, [(i, i + 1) for i in range(devices - 1)])
    after = lax.ppermute(
        jnp.concatenate([tokens[:WINDOW], cotangent[:WINDOW]]),
        BOTH,
        [(i + 1, i) for i in range(devices - 1)],
    )
    heads = jnp.stack([jnp.where(head == 0, mine, other), jnp.where(head == 0, other, mine)])
    x_ext = jnp.concatenate([before, tokens, after[:WINDOW]])
    cot_ext = jnp.concatenate([cotangent, after[WINDOW:]])
    opens, fill = row_marks(image_rows, image_fill, place * rows, rows + 1)
    mixed, input_grad, grads = layer(
        x_ext,
        cot_ext,
        opens,
        fill,
        first_gain[None],
        first_shift[None],
        heads,
        second_gain[None],
        second_shift[None],
        up_weight,
        up_bias[None],
        down_weight,
        down_bias[None],
        8 * devices,
    )
    total = all_sum(grads)
    column = head * HEAD_DIM
    base = 2 * FF
    sums = [total[base + p * D : base + (p + 1) * D] for p in range(4)]
    vectors = total[base + 4 * D : base + 4 * D + 16].astype(F32)
    up_grad = jnp.concatenate([total[FF + c : FF + c + D] for c in range(0, FF, D)], axis=1)
    return (
        mixed,
        input_grad,
        vectors[0],
        vectors[1],
        lax.dynamic_slice_in_dim(sums[0], column, HEAD_DIM, 1).astype(F32),
        lax.dynamic_slice_in_dim(sums[1], column, HEAD_DIM, 1).astype(F32),
        lax.dynamic_slice_in_dim(sums[2], column, HEAD_DIM, 1).astype(F32),
        lax.dynamic_slice_in_dim(sums[3], column, HEAD_DIM, 0).astype(F32),
        vectors[2],
        vectors[3],
        up_grad.astype(F32),
        vectors[8 : 8 + FF // D].reshape(FF),
        total[:FF].astype(F32),
        vectors[4],
    )


def solution(mesh):
    stream = P(("seq", "head"), None)
    columns = P(None, "head")
    in_specs = (stream, stream) + (P(),) * 4 + (columns,) * 3 + (P("head", None),) + (P(),) * 6
    out_specs = (
        (stream, stream) + (P(),) * 2 + (columns,) * 3 + (P("head", None),) + (P(),) * 6
    )
    return jax.shard_map(shards, mesh=mesh, in_specs=in_specs, out_specs=out_specs, check_vma=False)
```

profile of v0, /device:TPU:0, one launch (start us, length us, event | category | flops | bytes accessed | tf_op | source)
XLA Modules:
  0.0 129.5 jit_solution(11379112036125988784)
XLA Ops:
  0.6 0.8 constant_dynamic-update-slice_fusion.2
  1.5 0.9 constant_dynamic-update-slice_fusion.1
  2.3 0.9 constant_dynamic-update-slice_fusion
  4.7 3.0 %collective-permute-start.2 = (bf16[1024,128]{1,0:T(8,128)(2,1)S(1)}, bf16[1024,128]{1,0:T(8,128)(2,1)S(1)}, u32[]{:S(2)}, u32[]{:S(2)}) collective-permute-start(bf16[1024,128]{1,0:T(8,128)(2,1)S(1)} %slice_dynamic-update-slice_fusion), channel_id=1, source_target_pairs={{0,1},{1,0},{2,3},{3,2},{4,5},{5,4},{6,7},{7,6},{8,9},{9,8},{10,11... | collective-permute-start | bytes 786440 | tf_op jit(solution)/shard_map/ppermute | solution.py:425
  7.7 0.8 fusion.9
  8.5 0.8 slice.75
  9.3 1.3 collective-permute-start.1
  10.6 4.5 %collective-permute-start = (bf16[96,256]{1,0:T(8,128)(2,1)S(1)}, bf16[96,256]{1,0:T(8,128)(2,1)S(1)}, u32[]{:S(2)}, u32[]{:S(2)}) collective-permute-start(bf16[96,256]{1,0:T(8,128)(2,1)S(1)} %get-tuple-element.30), channel_id=1, source_target_pairs={{0,1},{1,2},{2,3},{3,4},{4,5},{5,6},{6,7},{7,8},{8,9},{9,10},{10,1... | collective-permute-start | bytes 147464 | tf_op jit(solution)/shard_map/ppermute | solution.py:426
  19.0 1.2 or_convert_fusion.first_ref
  20.1 2.8 %pad_maximum_fusion.1.cot_ref = bf16[3168,256]{1,0:T(8,128)(2,1)} fusion(bf16[96,256]{1,0:T(8,128)(2,1)S(1)} %get-tuple-element.40, bf16[3072,256]{1,0:T(8,128)(2,1)} %param.17), kind=kLoop, calls=%fused_computation.3 | loop fusion | flops 3244032 | bytes 3244032 | tf_op jit(solution)/shard_map/concatenate | solution.py:434
  23.0 1.3 pad_maximum_fusion.x_ref
  24.3 0.8 pad_maximum_fusion.2.heads_ref
  25.1 50.8 %layer.1 = (bf16[3072,256]{1,0:T(8,128)(2,1)}, bf16[3072,256]{1,0:T(8,128)(2,1)}, bf16[3328,256]{1,0:T(8,128)(2,1)}) custom-call(bf16[3264,256]{1,0:T(8,128)(2,1)} %pad_maximum_fusion.x_ref, bf16[3168,256]{1,0:T(8,128)(2,1)} %pad_maximum_fusion.1.cot_ref, s32[33]{0:T(128)} %or_convert_fusion.first_ref, s32[33]{0:T(128)} %broadcast_subtract_fusion.1.fill_ref, ...), custom_call_target="tpu_custom_call" | custom-call | tf_op jit(solution)/shard_map/layer/pallas_call | solution.py:299
  75.9 1.3 %dynamic-slice_bitcast_fusion = bf16[1664,256]{1,0:T(8,128)(2,1)S(1)} fusion(bf16[2,1664,256]{2,1,0:T(8,128)(2,1)} %bitcast.79, s32[]{:T(128)S(6)} %select_n.89), kind=kLoop, calls=%fused_computation.6 | loop fusion | bytes 1703940 | tf_op jit(solution)/shard_map/jit(dynamic_index_in_dim)/squeeze | solution.py:381
  77.4 2.3 %collective-permute-done.3 = bf16[1664,256]{1,0:T(8,128)(2,1)S(1)} collective-permute-done((bf16[1664,256]{1,0:T(8,128)(2,1)S(1)}, bf16[1664,256]{1,0:T(8,128)(2,1)S(1)}, u32[]{:S(2)}, u32[]{:S(2)}) %collective-permute-start.3) | collective-permute-done | bytes 852000 | tf_op jit(solution)/shard_map/ppermute | solution.py:352
  80.7 2.0 %collective-permute-start.5 = (bf16[416,256]{1,0:T(8,128)(2,1)S(1)}, bf16[416,256]{1,0:T(8,128)(2,1)S(1)}, u32[]{:S(2)}, u32[]{:S(2)}) collective-permute-start(bf16[416,256]{1,0:T(8,128)(2,1)S(1)} %get-tuple-element.34), channel_id=1, source_target_pairs={{0,4},{1,5},{2,6},{3,7},{4,0},{5,1},{6,2},{7,3},{8,12},{9,13},{10,... | collective-permute-start | bytes 638984 | tf_op jit(solution)/shard_map/ppermute | solution.py:352
  83.5 3.8 %collective-permute-done.4 = bf16[416,256]{1,0:T(8,128)(2,1)S(1)} collective-permute-done((bf16[416,256]{1,0:T(8,128)(2,1)S(1)}, bf16[416,256]{1,0:T(8,128)(2,1)S(1)}, u32[]{:S(2)}, u32[]{:S(2)}) %collective-permute-start.4) | collective-permute-done | bytes 213024 | tf_op jit(solution)/shard_map/ppermute | solution.py:352
  87.3 1.5 %collective-permute-done.5 = bf16[416,256]{1,0:T(8,128)(2,1)S(1)} collective-permute-done((bf16[416,256]{1,0:T(8,128)(2,1)S(1)}, bf16[416,256]{1,0:T(8,128)(2,1)S(1)}, u32[]{:S(2)}, u32[]{:S(2)}) %collective-permute-start.5) | collective-permute-done | bytes 213024 | tf_op jit(solution)/shard_map/ppermute | solution.py:352
  88.8 4.3 %collective-permute-done.6 = bf16[416,256]{1,0:T(8,128)(2,1)S(1)} collective-permute-done((bf16[416,256]{1,0:T(8,128)(2,1)S(1)}, bf16[416,256]{1,0:T(8,128)(2,1)S(1)}, u32[]{:S(2)}, u32[]{:S(2)}) %collective-permute-start.6) | collective-permute-done | bytes 213024 | tf_op jit(solution)/shard_map/ppermute | solution.py:352
  93.2 1.6 %collective-permute-start.7 = (bf16[104,256]{1,0:T(8,128)(2,1)S(1)}, bf16[104,256]{1,0:T(8,128)(2,1)S(1)}, u32[]{:S(2)}, u32[]{:S(2)}) collective-permute-start(bf16[104,256]{1,0:T(8,128)(2,1)S(1)} %get-tuple-element.37), channel_id=1, source_target_pairs={{0,8},{1,9},{2,10},{3,11},{4,12},{5,13},{6,14},{7,15},{8,0},{9,1},... | collective-permute-start | bytes 159752 | tf_op jit(solution)/shard_map/ppermute | solution.py:352
  94.9 2.6 %collective-permute-start.8 = (bf16[104,256]{1,0:T(8,128)(2,1)S(1)}, bf16[104,256]{1,0:T(8,128)(2,1)S(1)}, u32[]{:S(2)}, u32[]{:S(2)}) collective-permute-start(bf16[104,256]{1,0:T(8,128)(2,1)S(1)} %get-tuple-element.39), channel_id=1, source_target_pairs={{0,16},{1,17},{2,18},{3,19},{4,20},{5,21},{6,22},{7,23},{8,24},{9,... | collective-permute-start | bytes 159752 | tf_op jit(solution)/shard_map/ppermute | solution.py:352
  97.9 3.1 %collective-permute-done.8 = bf16[104,256]{1,0:T(8,128)(2,1)S(1)} collective-permute-done((bf16[104,256]{1,0:T(8,128)(2,1)S(1)}, bf16[104,256]{1,0:T(8,128)(2,1)S(1)}, u32[]{:S(2)}, u32[]{:S(2)}) %collective-permute-start.8) | collective-permute-done | bytes 53280 | tf_op jit(solution)/shard_map/ppermute | solution.py:352
  101.0 3.0 %collective-permute-done.9 = bf16[104,256]{1,0:T(8,128)(2,1)S(1)} collective-permute-done((bf16[104,256]{1,0:T(8,128)(2,1)S(1)}, bf16[104,256]{1,0:T(8,128)(2,1)S(1)}, u32[]{:S(2)}, u32[]{:S(2)}) %collective-permute-start.9) | collective-permute-done | bytes 53280 | tf_op jit(solution)/shard_map/ppermute | solution.py:352
  104.8 3.8 %collective-permute-start.12 = (bf16[104,256]{1,0:T(8,128)(2,1)S(1)}, bf16[104,256]{1,0:T(8,128)(2,1)S(1)}, u32[]{:S(2)}, u32[]{:S(2)}) collective-permute-start(bf16[104,256]{1,0:T(8,128)(2,1)S(1)} %get-tuple-element.21), channel_id=1, source_target_pairs={{0,24},{1,25},{2,26},{3,27},{4,28},{5,29},{6,30},{7,31},{8,16},{9,... | collective-permute-start | bytes 159752 | tf_op jit(solution)/shard_map/ppermute | solution.py:352
  109.3 1.9 %collective-permute-done.12 = bf16[104,256]{1,0:T(8,128)(2,1)S(1)} collective-permute-done((bf16[104,256]{1,0:T(8,128)(2,1)S(1)}, bf16[104,256]{1,0:T(8,128)(2,1)S(1)}, u32[]{:S(2)}, u32[]{:S(2)}) %collective-permute-start.12) | collective-permute-done | bytes 53280 | tf_op jit(solution)/shard_map/ppermute | solution.py:352
  112.0 1.4 %collective-permute-start.14 = (bf16[416,256]{1,0:T(8,128)(2,1)S(1)}, bf16[416,256]{1,0:T(8,128)(2,1)S(1)}, u32[]{:S(2)}, u32[]{:S(2)}) collective-permute-start(bf16[416,256]{1,0:T(8,128)(2,1)S(1)} %bitcast.84), channel_id=1, source_target_pairs={{0,4},{1,5},{2,6},{3,7},{4,0},{5,1},{6,2},{7,3},{8,12},{9,13},{10,... | collective-permute-start | bytes 638984 | tf_op jit(solution)/shard_map/ppermute | solution.py:352
  113.4 1.4 %collective-permute-start.15 = (bf16[416,256]{1,0:T(8,128)(2,1)S(1)}, bf16[416,256]{1,0:T(8,128)(2,1)S(1)}, u32[]{:S(2)}, u32[]{:S(2)}) collective-permute-start(bf16[416,256]{1,0:T(8,128)(2,1)S(1)} %bitcast.85), channel_id=1, source_target_pairs={{0,5},{1,4},{2,7},{3,6},{4,1},{5,0},{6,3},{7,2},{8,13},{9,12},{10,... | collective-permute-start | bytes 638984 | tf_op jit(solution)/shard_map/ppermute | solution.py:352
  114.9 2.9 %collective-permute-done.13 = bf16[416,256]{1,0:T(8,128)(2,1)S(1)} collective-permute-done((bf16[416,256]{1,0:T(8,128)(2,1)S(1)}, bf16[416,256]{1,0:T(8,128)(2,1)S(1)}, u32[]{:S(2)}, u32[]{:S(2)}) %collective-permute-start.13) | collective-permute-done | bytes 213024 | tf_op jit(solution)/shard_map/ppermute | solution.py:352
  117.9 3.0 %collective-permute-done.15 = bf16[416,256]{1,0:T(8,128)(2,1)S(1)} collective-permute-done((bf16[416,256]{1,0:T(8,128)(2,1)S(1)}, bf16[416,256]{1,0:T(8,128)(2,1)S(1)}, u32[]{:S(2)}, u32[]{:S(2)}) %collective-permute-start.15) | collective-permute-done | bytes 213024 | tf_op jit(solution)/shard_map/ppermute | solution.py:352
  121.2 2.2 %collective-permute-done.16 = bf16[1664,256]{1,0:T(8,128)(2,1)S(1)} collective-permute-done((bf16[1664,256]{1,0:T(8,128)(2,1)S(1)}, bf16[1664,256]{1,0:T(8,128)(2,1)S(1)}, u32[]{:S(2)}, u32[]{:S(2)}) %collective-permute-start.16) | collective-permute-done | bytes 852000 | tf_op jit(solution)/shard_map/ppermute | solution.py:352
  123.5 1.0 slice_convert_fusion
  128.4 1.1 maximum_convert_fusion
  (60 shorter events, 14.5 us)
Async XLA Ops:
  4.7 19.5 %collective-permute-start.2 = (bf16[1024,128]{1,0:T(8,128)(2,1)S(1)}, bf16[1024,128]{1,0:T(8,128)(2,1)S(1)}, u32[]{:S(2)}, u32[]{:S(2)}) collective-permute-start(bf16[1024,128]{1,0:T(8,128)(2,1)S(1)} %slice_dynamic-update-slice_fusion), channel_id=1, source_target_pairs={{0,1},{1,0},{2,3},{3,2},{4,5},{5,4},{6,7},{7,6},{8,9},{9,8},{10,11... | collective-permute-start | bytes 786440 | tf_op jit(solution)/shard_map/ppermute | solution.py:425
  9.3 10.8 %collective-permute-start.1 = (bf16[192,256]{1,0:T(8,128)(2,1)S(1)}, bf16[192,256]{1,0:T(8,128)(2,1)S(1)}, u32[]{:S(2)}, u32[]{:S(2)}) collective-permute-start(bf16[192,256]{1,0:T(8,128)(2,1)S(1)} %pad_maximum_fusion.3), channel_id=1, source_target_pairs={{1,0},{2,1},{3,2},{4,3},{5,4},{6,5},{7,6},{8,7},{9,8},{10,9},{11,1... | collective-permute-start | bytes 294920 | tf_op jit(solution)/shard_map/ppermute | solution.py:427
  10.6 12.3 %collective-permute-start = (bf16[96,256]{1,0:T(8,128)(2,1)S(1)}, bf16[96,256]{1,0:T(8,128)(2,1)S(1)}, u32[]{:S(2)}, u32[]{:S(2)}) collective-permute-start(bf16[96,256]{1,0:T(8,128)(2,1)S(1)} %get-tuple-element.30), channel_id=1, source_target_pairs={{0,1},{1,2},{2,3},{3,4},{4,5},{5,6},{6,7},{7,8},{8,9},{9,10},{10,1... | collective-permute-start | bytes 147464 | tf_op jit(solution)/shard_map/ppermute | solution.py:426
  20.1 2.8 %copy-start = (bf16[3072,256]{1,0:T(8,128)(2,1)S(1)}, bf16[3072,256]{1,0:T(8,128)(2,1)}, u32[]{:S(2)}) copy-start(bf16[3072,256]{1,0:T(8,128)(2,1)} %param.16) | copy-start | bytes 4718596
  75.9 3.8 %copy-start.1 = (bf16[3328,256]{1,0:T(8,128)(2,1)S(1)}, bf16[3328,256]{1,0:T(8,128)(2,1)}, u32[]{:S(2)}) copy-start(bf16[3328,256]{1,0:T(8,128)(2,1)} %get-tuple-element.19) | copy-start | bytes 5111812
  77.2 2.4 %collective-permute-start.3 = (bf16[1664,256]{1,0:T(8,128)(2,1)S(1)}, bf16[1664,256]{1,0:T(8,128)(2,1)S(1)}, u32[]{:S(2)}, u32[]{:S(2)}) collective-permute-start(bf16[1664,256]{1,0:T(8,128)(2,1)S(1)} %dynamic-slice_bitcast_fusion), channel_id=1, source_target_pairs={{0,2},{1,3},{2,0},{3,1},{4,6},{5,7},{6,4},{7,5},{8,10},{9,11},{10,... | collective-permute-start | bytes 2555912 | tf_op jit(solution)/shard_map/ppermute | solution.py:352
  80.0 7.4 %collective-permute-start.4 = (bf16[416,256]{1,0:T(8,128)(2,1)S(1)}, bf16[416,256]{1,0:T(8,128)(2,1)S(1)}, u32[]{:S(2)}, u32[]{:S(2)}) collective-permute-start(bf16[416,256]{1,0:T(8,128)(2,1)S(1)} %get-tuple-element.32), channel_id=1, source_target_pairs={{0,1},{1,0},{2,3},{3,2},{4,5},{5,4},{6,7},{7,6},{8,9},{9,8},{10,11... | collective-permute-start | bytes 638984 | tf_op jit(solution)/shard_map/ppermute | solution.py:352
  80.7 8.1 %collective-permute-start.5 = (bf16[416,256]{1,0:T(8,128)(2,1)S(1)}, bf16[416,256]{1,0:T(8,128)(2,1)S(1)}, u32[]{:S(2)}, u32[]{:S(2)}) collective-permute-start(bf16[416,256]{1,0:T(8,128)(2,1)S(1)} %get-tuple-element.34), channel_id=1, source_target_pairs={{0,4},{1,5},{2,6},{3,7},{4,0},{5,1},{6,2},{7,3},{8,12},{9,13},{10,... | collective-permute-start | bytes 638984 | tf_op jit(solution)/shard_map/ppermute | solution.py:352
  82.8 10.3 %collective-permute-start.6 = (bf16[416,256]{1,0:T(8,128)(2,1)S(1)}, bf16[416,256]{1,0:T(8,128)(2,1)S(1)}, u32[]{:S(2)}, u32[]{:S(2)}) collective-permute-start(bf16[416,256]{1,0:T(8,128)(2,1)S(1)} %get-tuple-element.33), channel_id=1, source_target_pairs={{0,5},{1,4},{2,7},{3,6},{4,1},{5,0},{6,3},{7,2},{8,13},{9,12},{10,... | collective-permute-start | bytes 638984 | tf_op jit(solution)/shard_map/ppermute | solution.py:352
  93.2 4.7 %collective-permute-start.7 = (bf16[104,256]{1,0:T(8,128)(2,1)S(1)}, bf16[104,256]{1,0:T(8,128)(2,1)S(1)}, u32[]{:S(2)}, u32[]{:S(2)}) collective-permute-start(bf16[104,256]{1,0:T(8,128)(2,1)S(1)} %get-tuple-element.37), channel_id=1, source_target_pairs={{0,8},{1,9},{2,10},{3,11},{4,12},{5,13},{6,14},{7,15},{8,0},{9,1},... | collective-permute-start | bytes 159752 | tf_op jit(solution)/shard_map/ppermute | solution.py:352
  94.9 6.2 %collective-permute-start.8 = (bf16[104,256]{1,0:T(8,128)(2,1)S(1)}, bf16[104,256]{1,0:T(8,128)(2,1)S(1)}, u32[]{:S(2)}, u32[]{:S(2)}) collective-permute-start(bf16[104,256]{1,0:T(8,128)(2,1)S(1)} %get-tuple-element.39), channel_id=1, source_target_pairs={{0,16},{1,17},{2,18},{3,19},{4,20},{5,21},{6,22},{7,23},{8,24},{9,... | collective-permute-start | bytes 159752 | tf_op jit(solution)/shard_map/ppermute | solution.py:352
  97.5 6.6 %collective-permute-start.9 = (bf16[104,256]{1,0:T(8,128)(2,1)S(1)}, bf16[104,256]{1,0:T(8,128)(2,1)S(1)}, u32[]{:S(2)}, u32[]{:S(2)}) collective-permute-start(bf16[104,256]{1,0:T(8,128)(2,1)S(1)} %get-tuple-element.38), channel_id=1, source_target_pairs={{0,24},{1,25},{2,26},{3,27},{4,28},{5,29},{6,30},{7,31},{8,16},{9,... | collective-permute-start | bytes 159752 | tf_op jit(solution)/shard_map/ppermute | solution.py:352
  104.1 4.5 %collective-permute-start.10 = (bf16[104,256]{1,0:T(8,128)(2,1)S(1)}, bf16[104,256]{1,0:T(8,128)(2,1)S(1)}, u32[]{:S(2)}, u32[]{:S(2)}) collective-permute-start(bf16[104,256]{1,0:T(8,128)(2,1)S(1)} %get-tuple-element.21), channel_id=1, source_target_pairs={{0,8},{1,9},{2,10},{3,11},{4,12},{5,13},{6,14},{7,15},{8,0},{9,1},... | collective-permute-start | bytes 159752 | tf_op jit(solution)/shard_map/ppermute | solution.py:352
  104.2 5.1 %collective-permute-start.11 = (bf16[104,256]{1,0:T(8,128)(2,1)S(1)}, bf16[104,256]{1,0:T(8,128)(2,1)S(1)}, u32[]{:S(2)}, u32[]{:S(2)}) collective-permute-start(bf16[104,256]{1,0:T(8,128)(2,1)S(1)} %get-tuple-element.21), channel_id=1, source_target_pairs={{0,16},{1,17},{2,18},{3,19},{4,20},{5,21},{6,22},{7,23},{8,24},{9,... | collective-permute-start | bytes 159752 | tf_op jit(solution)/shard_map/ppermute | solution.py:352
  104.8 6.4 %collective-permute-start.12 = (bf16[104,256]{1,0:T(8,128)(2,1)S(1)}, bf16[104,256]{1,0:T(8,128)(2,1)S(1)}, u32[]{:S(2)}, u32[]{:S(2)}) collective-permute-start(bf16[104,256]{1,0:T(8,128)(2,1)S(1)} %get-tuple-element.21), channel_id=1, source_target_pairs={{0,24},{1,25},{2,26},{3,27},{4,28},{5,29},{6,30},{7,31},{8,16},{9,... | collective-permute-start | bytes 159752 | tf_op jit(solution)/shard_map/ppermute | solution.py:352
  111.2 6.6 %collective-permute-start.13 = (bf16[416,256]{1,0:T(8,128)(2,1)S(1)}, bf16[416,256]{1,0:T(8,128)(2,1)S(1)}, u32[]{:S(2)}, u32[]{:S(2)}) collective-permute-start(bf16[416,256]{1,0:T(8,128)(2,1)S(1)} %bitcast.83), channel_id=1, source_target_pairs={{0,1},{1,0},{2,3},{3,2},{4,5},{5,4},{6,7},{7,6},{8,9},{9,8},{10,11... | collective-permute-start | bytes 638984 | tf_op jit(solution)/shard_map/ppermute | solution.py:352
  112.0 5.8 %collective-permute-start.14 = (bf16[416,256]{1,0:T(8,128)(2,1)S(1)}, bf16[416,256]{1,0:T(8,128)(2,1)S(1)}, u32[]{:S(2)}, u32[]{:S(2)}) collective-permute-start(bf16[416,256]{1,0:T(8,128)(2,1)S(1)} %bitcast.84), channel_id=1, source_target_pairs={{0,4},{1,5},{2,6},{3,7},{4,0},{5,1},{6,2},{7,3},{8,12},{9,13},{10,... | collective-permute-start | bytes 638984 | tf_op jit(solution)/shard_map/ppermute | solution.py:352
  113.4 7.5 %collective-permute-start.15 = (bf16[416,256]{1,0:T(8,128)(2,1)S(1)}, bf16[416,256]{1,0:T(8,128)(2,1)S(1)}, u32[]{:S(2)}, u32[]{:S(2)}) collective-permute-start(bf16[416,256]{1,0:T(8,128)(2,1)S(1)} %bitcast.85), channel_id=1, source_target_pairs={{0,5},{1,4},{2,7},{3,6},{4,1},{5,0},{6,3},{7,2},{8,13},{9,12},{10,... | collective-permute-start | bytes 638984 | tf_op jit(solution)/shard_map/ppermute | solution.py:352
  120.9 2.4 %collective-permute-start.16 = (bf16[1664,256]{1,0:T(8,128)(2,1)S(1)}, bf16[1664,256]{1,0:T(8,128)(2,1)S(1)}, u32[]{:S(2)}, u32[]{:S(2)}) collective-permute-start(bf16[1664,256]{1,0:T(8,128)(2,1)S(1)} %bitcast.75), channel_id=1, source_target_pairs={{0,2},{1,3},{2,0},{3,1},{4,6},{5,7},{6,4},{7,5},{8,10},{9,11},{10,... | collective-permute-start | bytes 2555912 | tf_op jit(solution)/shard_map/ppermute | solution.py:352
where the time goes:
time: 130 us; the launch traced here: 129 us
  Pallas kernels  50.8 us (39%)
  waiting for transfers between devices  29 us (22%)
  starting transfers between devices  24.9 us (19%)
  other arithmetic  13.8 us (11%)
  local copies, waits for them, and re-layouts  10.1 us (8%)
    pallas_call x1, Pallas kernels, layer(): pl.pallas_call(functools.partial(layer_kernel, rows), out_shape=(jax.Shap...  50.8 us
    ppermute x14, waiting for transfers between devices, swapped(): return lax.ppermute(value, BOTH, [(i, i ^ mask) for i in range(count)])  29 us
    ppermute x14, starting transfers between devices, swapped(): return lax.ppermute(value, BOTH, [(i, i ^ mask) for i in range(count)])  16.1 us
    ppermute x1, starting transfers between devices, shards(): lax.ppermute(tokens[own - WINDOW:], BOTH, [(i, i + 1) for i in range(devi...  4.55 us
    unnamed x10, local copies, waits for them, and re-layouts  3.93 us
    ppermute x1, starting transfers between devices, shards(): other = lax.ppermute(mine, 'head', [(0, 1), (1, 0)])  2.97 us
    concatenate x1, other arithmetic, shards(): cot_ext = jnp.concatenate([cotangent, after[WINDOW:]])  2.81 us
  transfers between devices with their start and end apart: 17, of which 12 were waited for; matrix products, arithmetic and copies ran while one was open for 8% of the time, Pallas kernels for 0%

commit v1 on v0

v1 whole, which is shorter than its diff:
```python
import functools

import jax
import jax.numpy as jnp
from jax import lax
from jax.experimental import pallas as pl
from jax.experimental.pallas import tpu as pltpu
from jax.sharding import PartitionSpec as P

HEAD_DIM = 128
HEADS = 2
WINDOW = 96
BOTH = ("seq", "head")

EPSILON = 1e-05
MASKED = -1000000000.0
LOG2E = 1.4426950408889634
SCALE = HEAD_DIM ** (-0.5)

F32 = jnp.float32
BF16 = jnp.bfloat16
LANES = (((1,), (1,)), ((), ()))
ROWS = (((0,), (0,)), ((), ()))

CHUNK = 8
LAG = 4


def dot(a, b):
    return jnp.dot(a, b, preferred_element_type=F32)


def dot_lanes(a, b):
    return lax.dot_general(a, b, LANES, preferred_element_type=F32)


def dot_rows(a, b):
    return lax.dot_general(a, b, ROWS, preferred_element_type=F32)


def standardize(inputs):
    center = inputs - jnp.mean(inputs, axis=1, keepdims=True)
    spread = jnp.mean(center * center, axis=1, keepdims=True)
    inverse = lax.rsqrt(spread + EPSILON)
    return center * inverse, inverse


def normalize_back(weighted, scaled, inverse):
    return inverse * (
        weighted
        - jnp.mean(weighted, axis=1, keepdims=True)
        - scaled * jnp.mean(weighted * scaled, axis=1, keepdims=True)
    )


def twice_gelu(x):
    z = x * 0.7071067811865476
    below = 1.0 + lax.erf(z)
    bell = jnp.exp2(z * z * -LOG2E)
    return x * below, below + x * bell * 0.7978845608028654


def column_sums(value):
    return jnp.sum(value, axis=0, keepdims=True)


def merge(*lists):
    marked = [
        ((n + 0.5) / len(work), k, n, job) for k, work in enumerate(lists) for n, job in enumerate(work)
    ]
    return [job for *_, job in sorted(marked, key=lambda item: item[:3])]


VECTOR_ROWS = 128


def half_rows(FF, D):
    return (2 * FF * D + 4 * D * D) // (2 * HEAD_DIM) + VECTOR_ROWS


def vector_slots(FF, D):
    found = [
        (n, slice(c, c + HEAD_DIM)) for n in range(5) for c in range(0, D, HEAD_DIM)
    ]
    return found + [(8, slice(c, c + HEAD_DIM)) for c in range(0, FF, HEAD_DIM)]


def layer_kernel(
    rows,
    tok_ref,
    cot_in_ref,
    rim_ref,
    image_rows_ref,
    image_fill_ref,
    gain1_ref,
    shift1_ref,
    query_ref,
    key_ref,
    value_ref,
    out_ref,
    heads_ref,
    gain2_ref,
    shift2_ref,
    up_in_ref,
    up_bias_ref,
    down_in_ref,
    down_bias_ref,
    mixed_ref,
    in_grad_ref,
    keep_ref,
    send_ref,
    x_ref,
    cot_ref,
    up_ref,
    down_ref,
    wqkv,
    wout,
    low_mark,
    fill_mark,
    normed,
    xhat,
    inv,
    qbuf,
    kbuf,
    vbuf,
    gbuf,
    att,
    probs,
    mid_grad,
    dqkv,
    act,
    hid_grad,
    mixed_buf,
    in_grad_buf,
    acc_down,
    acc_up,
    acc_qkv,
    acc_out,
    acc_vec,
    vec_rows,
    in_sem,
    out_sem,
):
    D = x_ref.shape[1]
    FF = up_ref.shape[1]
    own = rows * WINDOW
    head = lax.axis_index("head")
    place = lax.axis_index("seq") * lax.axis_size("head") + head
    step = CHUNK * WINDOW
    steps = rows // CHUNK

    arriving = {}
    for i in range(steps):
        piece = pl.ds(i * step, step)
        arriving["x", i] = pltpu.make_async_copy(
            tok_ref.at[piece], x_ref.at[pl.ds(WINDOW + i * step, step)], in_sem.at[i]
        )
    arriving["up"] = pltpu.make_async_copy(up_in_ref, up_ref, in_sem.at[steps])
    arriving["down"] = pltpu.make_async_copy(down_in_ref, down_ref, in_sem.at[steps + 1])
    arriving["cot"] = pltpu.make_async_copy(cot_in_ref, cot_ref.at[pl.ds(0, own)], in_sem.at[steps + 2])
    for copy in arriving.values():
        copy.start()
    leaving = []

    mine = [query_ref[...], key_ref[...], value_ref[...]]
    for part in range(3):
        theirs = heads_ref[part * D : (part + 1) * D, :]
        at = pl.multiple_of(part * D + head * HEAD_DIM, HEAD_DIM)
        wqkv[:, pl.ds(at, HEAD_DIM)] = mine[part]
        at = pl.multiple_of(part * D + (1 - head) * HEAD_DIM, HEAD_DIM)
        wqkv[:, pl.ds(at, HEAD_DIM)] = theirs
    wout[pl.ds(pl.multiple_of(head * HEAD_DIM, HEAD_DIM), HEAD_DIM), :] = out_ref[...]
    for half in range(D // HEAD_DIM):
        wout[
            pl.ds(pl.multiple_of((1 - head) * HEAD_DIM, HEAD_DIM), HEAD_DIM),
            half * HEAD_DIM : (half + 1) * HEAD_DIM,
        ] = heads_ref[3 * D + half * HEAD_DIM : 3 * D + (half + 1) * HEAD_DIM, :]
    acc_vec[...] = jnp.zeros_like(acc_vec)
    for half in range(D // HEAD_DIM):
        cols = slice(half * HEAD_DIM, (half + 1) * HEAD_DIM)
        near = heads_ref[4 * D + half * 2 * WINDOW : 4 * D + (half + 1) * 2 * WINDOW, :]
        far = rim_ref[half * 2 * WINDOW : (half + 1) * 2 * WINDOW, :]
        x_ref[:WINDOW, cols] = jnp.where(head == 0, far[:WINDOW], near[:WINDOW])
        x_ref[WINDOW + own :, cols] = jnp.where(head == 0, near[:WINDOW], far[:WINDOW])
        cot_ref[own:, cols] = jnp.where(head == 0, near[WINDOW:], far[WINDOW:])

    images = image_rows_ref.shape[1]
    earlier = lax.broadcasted_iota(jnp.int32, (images, images), 0) <= lax.broadcasted_iota(
        jnp.int32, (images, images), 1
    )
    counts = jnp.broadcast_to(image_rows_ref[...], (8, images)).astype(F32)
    ends = dot(counts.astype(BF16), jnp.where(earlier, 1.0, 0.0).astype(BF16))[:1]
    starts = ends - counts[:1]
    mark_rows = low_mark.shape[0]
    row = (place * rows + lax.broadcasted_iota(jnp.int32, (mark_rows, 1), 0)).astype(F32)
    opens = jnp.sum(jnp.where(starts == row, 1.0, 0.0), axis=1, keepdims=True)
    opens = jnp.where(row >= ends[:, images - 1 :], 1.0, opens)
    missing = WINDOW - image_fill_ref[...].astype(F32)
    short = jnp.sum(jnp.where(ends == row + 1.0, missing, 0.0), axis=1, keepdims=True)
    low_mark[...] = jnp.broadcast_to(
        jnp.where(opens > 0.0, 0.0, -1.0 * WINDOW), low_mark.shape
    ).astype(jnp.int32)
    fill_mark[...] = jnp.broadcast_to(WINDOW - short, fill_mark.shape).astype(jnp.int32)

    def project(first, count):
        here = slice(first * WINDOW, (first + count) * WINDOW)
        scaled, inverse = standardize(x_ref[here, :].astype(F32))
        xhat[here, :] = scaled
        inv[here, :] = inverse
        value = (scaled * gain1_ref[...] + shift1_ref[...]).astype(BF16)
        normed[here, :] = value
        for part, buf in enumerate((qbuf, kbuf, vbuf)):
            made = dot(value, wqkv[:, part * D : (part + 1) * D]).astype(BF16)
            for g in range(count):
                buf[(first + g) * WINDOW : (first + g + 1) * WINDOW, :] = made[
                    g * WINDOW : (g + 1) * WINDOW
                ]

    key_id = lax.broadcasted_iota(jnp.int32, (WINDOW, WINDOW), 0)
    query_id = lax.broadcasted_iota(jnp.int32, (WINDOW, WINDOW), 1)
    current = key_id <= query_id
    current_t = key_id >= query_id
    offset = jnp.where(current, key_id, key_id - WINDOW)
    columns = [slice(h * HEAD_DIM, (h + 1) * HEAD_DIM) for h in range(HEADS)]
    held = {}

    def pair(buf, j, h):
        return buf[(j - 1) * WINDOW : (j + 1) * WINDOW, columns[h]]

    def row_of(buf, j, h):
        return buf[j * WINDOW : (j + 1) * WINDOW, columns[h]]

    def window_sum(weights, buf, j, h):
        turned = weights.T
        zero = jnp.zeros_like(turned)
        both = pair(buf, j, h)
        return dot(jnp.where(current_t, zero, turned), both[:WINDOW]) + dot(
            jnp.where(current_t, turned, zero), both[WINDOW:]
        )

    def key_sum(weights, queries):
        zero = jnp.zeros_like(weights)
        both = jnp.concatenate([jnp.where(current, zero, weights), jnp.where(current, weights, zero)])
        made = dot(both, queries)
        return made[:WINDOW], made[WINDOW:]

    def score(j, h):
        raw = dot_lanes(pair(kbuf, j, h), row_of(qbuf, j, h))
        held[j, h] = jnp.where(current, raw[WINDOW:], raw[:WINDOW])

    def soften(j, h):
        r = j - 1
        keep = (offset >= low_mark[r : r + 1, :WINDOW]) & (offset < fill_mark[r : r + 1, :WINDOW])
        scores = jnp.where(keep, held.pop((j, h)) * (SCALE * LOG2E), MASKED * LOG2E)
        lifted = jnp.exp2(scores - jnp.max(scores, axis=0, keepdims=True))
        weights = lifted * (1.0 / jnp.sum(lifted, axis=0, keepdims=True))
        probs[r * HEADS + h] = weights
        held[j, h] = weights.astype(BF16)

    def gather(j, h):
        r = j - 1
        att[r * WINDOW : (r + 1) * WINDOW, columns[h]] = window_sum(
            held.pop((j, h)), vbuf, j, h
        ).astype(BF16)

    def feed_forward(first, count, own_rows):
        at = first * WINDOW
        size = count * WINDOW
        here = slice(at, at + size)
        held = {}
        block = 256

        def enter():
            attended = att[here, :]
            middle = x_ref[at + WINDOW : at + WINDOW + size, :].astype(F32) + dot(attended, wout[...])
            scaled, inverse = standardize(middle)
            held.update(middle=middle, scaled=scaled, inverse=inverse)
            held["normed"] = (scaled * gain2_ref[...] + shift2_ref[...]).astype(BF16)

        def hide(f):
            cols = slice(f * block, (f + 1) * block)
            cot = cot_ref[here, :]
            hidden = dot(held["normed"], up_ref[:, cols]) + up_bias_ref[:, cols]
            active, slope = twice_gelu(hidden)
            grad = dot_lanes(cot, down_ref[cols, :]) * slope
            hid_grad[:size, cols] = grad.astype(BF16)
            if own_rows:
                act[:size, cols] = active.astype(BF16)
                acc_vec[8:9, cols] += column_sums(grad)

        def weigh(f):
            cols = slice(f * block, (f + 1) * block)
            down_part = dot_rows(cot_ref[here, :], act[:size, cols])
            up_part = dot_rows(held["normed"], hid_grad[:size, cols])
            if at:
                acc_down[:, cols] += down_part
                acc_up[:, cols] += up_part
            else:
                acc_down[:, cols] = down_part
                acc_up[:, cols] = up_part

        def mix():
            mixed_buf[here, :] = (
                held["middle"] + dot(act[:size], down_ref[...]) + down_bias_ref[...]
            ).astype(BF16)
            copy = pltpu.make_async_copy(
                mixed_buf.at[pl.ds(at, size)], mixed_ref.at[pl.ds(at, size)], out_sem.at[0, at // size]
            )
            copy.start()
            leaving.append(copy)

        def back():
            scaled = held["scaled"]
            g2 = dot_lanes(hid_grad[:size], up_ref[...])
            cot32 = cot_ref[here, :].astype(F32)
            middle_grad = cot32 + normalize_back(g2 * gain2_ref[...], scaled, held["inverse"])
            mixing_grad = middle_grad.astype(BF16)
            if own_rows:
                mid_grad[here, :] = middle_grad
                acc_vec[2:3, :D] += column_sums(g2 * scaled)
                acc_vec[3:4, :D] += column_sums(g2)
                acc_vec[4:5, :D] += column_sums(cot32)
                out_part = dot_rows(att[here, :], mixing_grad)
                if at:
                    acc_out[...] += out_part
                else:
                    acc_out[...] = out_part
            made = dot_lanes(mixing_grad, wout[...]).astype(BF16)
            for g in range(count):
                j = first + 1 + g
                gbuf[j * WINDOW : (j + 1) * WINDOW, :] = made[g * WINDOW : (g + 1) * WINDOW]

        jobs = [enter]
        for f in range(FF // block):
            jobs.append(functools.partial(hide, f))
            if own_rows and f:
                jobs.append(functools.partial(weigh, f - 1))
        if own_rows:
            jobs.append(functools.partial(weigh, FF // block - 1))
            jobs.append(mix)
        jobs.append(back)
        return jobs

    held_back = {}
    unfinished = {}

    def weigh_grads(j, h):
        raw = dot_lanes(pair(vbuf, j, h), row_of(gbuf, j, h))
        held_back[j, h] = jnp.where(current, raw[WINDOW:], raw[:WINDOW])

    def soften_back(j, h):
        dweights = held_back.pop((j, h))
        weights = probs[(j - 1) * HEADS + h]
        inner = jnp.sum(weights * dweights, axis=0, keepdims=True)
        dscores = (weights * (dweights - inner)).astype(BF16)
        held_back[j, h] = (dscores, weights.astype(BF16))

    def gather_back(j, h):
        r = j - 1
        dscores, weights = held_back.pop((j, h))
        found = [key_sum(dscores, row_of(qbuf, j, h)), key_sum(weights, row_of(gbuf, j, h))]
        if j > 1:
            there = slice((r - 1) * WINDOW, r * WINDOW)
            for part, (before, _) in enumerate(found):
                total = unfinished[part, h] + before
                at = (part + 1) * D + h * HEAD_DIM
                dqkv[there, at : at + HEAD_DIM] = (total if part else total * SCALE).astype(BF16)
        for part, (_, current_part) in enumerate(found):
            unfinished[part, h] = current_part
        if j <= rows:
            dqkv[r * WINDOW : (r + 1) * WINDOW, columns[h]] = (
                window_sum(dscores, kbuf, j, h) * SCALE
            ).astype(BF16)

    def project_back(i):
        at = i * step
        here = slice(at, at + step)
        there = slice(at + WINDOW, at + WINDOW + step)
        grads = dqkv[here, :]
        part = dot_rows(normed[there, :], grads)
        if at:
            acc_qkv[...] += part
        else:
            acc_qkv[...] = part
        g1 = dot_lanes(grads, wqkv[...])
        scaled = xhat[there, :]
        acc_vec[0:1, :D] += column_sums(g1 * scaled)
        acc_vec[1:2, :D] += column_sums(g1)
        in_grad_buf[here, :] = (
            mid_grad[here, :] + normalize_back(g1 * gain1_ref[...], scaled, inv[there, :])
        ).astype(BF16)
        copy = pltpu.make_async_copy(
            in_grad_buf.at[pl.ds(at, step)], in_grad_ref.at[pl.ds(at, step)], out_sem.at[1, i]
        )
        copy.start()
        leaving.append(copy)

    def do(jobs):
        for job in jobs:
            job()

    def staggered(first, last, *kinds):
        units = [(j, h) for j in range(first, last + 1) for h in range(HEADS)]
        jobs = []
        for t in range(len(units) + LAG * (len(kinds) - 1)):
            for k, kind in enumerate(kinds):
                if 0 <= t - LAG * k < len(units):
                    jobs.append(functools.partial(kind, *units[t - LAG * k]))
        return jobs

    def forward(first, last):
        return staggered(first, last, score, soften, gather)

    def backward(first, last):
        return staggered(first, last, weigh_grads, soften_back, gather_back)

    for i in range(steps):
        arriving["x", i].wait()
        project(i * CHUNK + (1 if i else 0), CHUNK + (0 if i else 1))
    project(rows + 1, 1)
    do(forward(1, rows + 1))
    for name in ("up", "down", "cot"):
        arriving[name].wait()
    down_ref[...] = (down_ref[...].astype(F32) * 0.5).astype(BF16)
    for i in range(steps):
        do(feed_forward(i * CHUNK, CHUNK, True))
    do(feed_forward(rows, 1, False))
    do(backward(1, rows + 1))
    for i in range(steps):
        project_back(i)

    for s, (n, cols) in enumerate(vector_slots(FF, D)):
        vec_rows[s : s + 1, :] = acc_vec[n : n + 1, cols]
    core = (place & 2) // 2
    wide = FF // 2
    for c, ref in ((core, keep_ref), (1 - core, send_ref)):
        base = 0
        for f in range(0, wide, D):
            at = pl.ds(pl.multiple_of(c * wide + f, D), D)
            block = (acc_down[:, at] * 0.5).astype(BF16).T
            for half in range(D // HEAD_DIM):
                ref[half * wide + f : half * wide + f + D, :] = block[
                    :, half * HEAD_DIM : (half + 1) * HEAD_DIM
                ]
        base = D // HEAD_DIM * wide
        for f in range(0, wide, HEAD_DIM):
            at = pl.ds(pl.multiple_of(c * wide + f, HEAD_DIM), HEAD_DIM)
            ref[base : base + D, :] = acc_up[:, at].astype(BF16)
            base += D
        mine = pl.ds(pl.multiple_of(c * HEAD_DIM, HEAD_DIM), HEAD_DIM)
        for h in range(HEADS):
            for part in range(3):
                at = part * D + h * HEAD_DIM
                ref[base : base + HEAD_DIM, :] = acc_qkv[mine, at : at + HEAD_DIM].astype(BF16)
                base += HEAD_DIM
            ref[base : base + HEAD_DIM, :] = acc_out[
                h * HEAD_DIM : (h + 1) * HEAD_DIM, mine
            ].astype(BF16)
            base += HEAD_DIM
        flat = vec_rows[pl.ds(pl.multiple_of(c * 16, 16), 16), :].astype(BF16)
        ref[base:, :] = jnp.concatenate([flat] * (VECTOR_ROWS // 16))
    for copy in leaving:
        copy.wait()


def layer(
    tokens, cotangent, rim, image_rows, image_fill, gain1, shift1, weights, other, gain2, shift2, up,
    up_bias, down, down_bias
):
    own, D = tokens.shape
    FF = up.shape[1]
    rows = own // WINDOW
    count = own + 2 * WINDOW
    half = half_rows(FF, D)
    in_vmem = functools.partial(pltpu.with_memory_space_constraint, memory_space=pltpu.VMEM)
    rim, other = in_vmem(rim), in_vmem(other)
    vmem = pl.BlockSpec(memory_space=pltpu.VMEM)
    anywhere = pl.BlockSpec(memory_space=pl.ANY)
    steps = rows // CHUNK
    mark_rows = -(-(rows + 1) // 8) * 8
    return pl.pallas_call(
        functools.partial(layer_kernel, rows),
        out_shape=(
            jax.ShapeDtypeStruct((own, D), BF16),
            jax.ShapeDtypeStruct((own, D), BF16),
            pltpu.VMEM((half, HEAD_DIM), BF16),
            pltpu.VMEM((half, HEAD_DIM), BF16),
        ),
        in_specs=[anywhere, anywhere] + [vmem] * 12 + [anywhere, vmem, anywhere, vmem],
        out_specs=(anywhere, anywhere, vmem, vmem),
        scratch_shapes=[
            pltpu.VMEM((count, D), BF16),
            pltpu.VMEM((count - WINDOW, D), BF16),
            pltpu.VMEM((D, FF), BF16),
            pltpu.VMEM((FF, D), BF16),
            pltpu.VMEM((D, 3 * D), BF16),
            pltpu.VMEM((D, D), BF16),
            pltpu.VMEM((mark_rows, 128), jnp.int32),
            pltpu.VMEM((mark_rows, 128), jnp.int32),
            pltpu.VMEM((count, D), BF16),
            pltpu.VMEM((count, D), F32),
            pltpu.VMEM((count, 1), F32),
            pltpu.VMEM((count, D), BF16),
            pltpu.VMEM((count, D), BF16),
            pltpu.VMEM((count, D), BF16),
            pltpu.VMEM((count, D), BF16),
            pltpu.VMEM((count - WINDOW, D), BF16),
            pltpu.VMEM(((rows + 1) * HEADS, WINDOW, WINDOW), F32),
            pltpu.VMEM((own, D), F32),
            pltpu.VMEM((own, 3 * D), BF16),
            pltpu.VMEM((CHUNK * WINDOW, FF), BF16),
            pltpu.VMEM((CHUNK * WINDOW, FF), BF16),
            pltpu.VMEM((own, D), BF16),
            pltpu.VMEM((own, D), BF16),
            pltpu.VMEM((D, FF), F32),
            pltpu.VMEM((D, FF), F32),
            pltpu.VMEM((D, 3 * D), F32),
            pltpu.VMEM((D, D), F32),
            pltpu.VMEM((16, FF), F32),
            pltpu.VMEM((32, HEAD_DIM), F32),
            pltpu.SemaphoreType.DMA((steps + 3,)),
            pltpu.SemaphoreType.DMA((2, steps)),
        ],
        compiler_params=pltpu.CompilerParams(vmem_limit_bytes=56 * 1024 * 1024),
        name="layer",
    )(
        tokens, cotangent, rim, image_rows, image_fill, gain1, shift1, *weights, other, gain2, shift2, up,
        up_bias, down, down_bias
    )


def pack_kernel(query_ref, key_ref, value_ref, out_ref, tok_ref, cot_ref, near_ref, far_ref, sem):
    D = query_ref.shape[0]
    own = tok_ref.shape[0]
    head = lax.axis_index("head")
    moves = [
        (ref, near_ref.at[pl.ds(part * D, D)]) for part, ref in enumerate((query_ref, key_ref, value_ref))
    ]
    last = own - WINDOW
    near_from = pl.multiple_of((1 - head) * last, WINDOW)
    far_from = pl.multiple_of(head * last, WINDOW)
    for half in range(D // HEAD_DIM):
        cols = pl.ds(half * HEAD_DIM, HEAD_DIM)
        moves.append((out_ref.at[:, cols], near_ref.at[pl.ds(3 * D + half * HEAD_DIM, HEAD_DIM)]))
        for k, ref in enumerate((tok_ref, cot_ref)):
            at = (half * 2 + k) * WINDOW
            moves.append((ref.at[pl.ds(near_from, WINDOW), cols], near_ref.at[pl.ds(4 * D + at, WINDOW)]))
            moves.append((ref.at[pl.ds(far_from, WINDOW), cols], far_ref.at[pl.ds(at, WINDOW)]))
    copies = [pltpu.make_async_copy(a, b, sem.at[n]) for n, (a, b) in enumerate(moves)]
    for copy in copies:
        copy.start()
    for copy in copies:
        copy.wait()


def pack(query_weight, key_weight, value_weight, out_weight, tokens, cotangent):
    D = query_weight.shape[0]
    rim = 2 * WINDOW * D // HEAD_DIM
    anywhere = pl.BlockSpec(memory_space=pl.ANY)
    vmem = pl.BlockSpec(memory_space=pltpu.VMEM)
    return pl.pallas_call(
        pack_kernel,
        out_shape=(pltpu.VMEM((4 * D + rim, HEAD_DIM), BF16), pltpu.VMEM((rim, HEAD_DIM), BF16)),
        in_specs=[anywhere] * 6,
        out_specs=(vmem, vmem),
        scratch_shapes=[pltpu.SemaphoreType.DMA((3 + 5 * (D // HEAD_DIM),))],
        name="pack",
    )(query_weight, key_weight, value_weight, out_weight, tokens, cotangent)


def finish_kernel(FF, D, mine_ref, other_ref, *refs):
    outs, (down_buf, up_buf, vec_rows, sem) = refs[:12], refs[12:]
    gain1, shift1, query, key, value, out, gain2, shift2, up, up_bias, down, down_bias = outs
    core = lax.axis_index("seq") % 2
    head = lax.axis_index("head")
    halves = ((core, mine_ref), (1 - core, other_ref))
    wide = FF // 2
    for c, ref in halves:
        rows = pl.ds(pl.multiple_of(c * wide, wide), wide)
        for half in range(D // HEAD_DIM):
            down_buf[rows, half * HEAD_DIM : (half + 1) * HEAD_DIM] = ref[
                half * wide : (half + 1) * wide, :
            ].astype(F32)
    copies = [pltpu.make_async_copy(down_buf, down, sem.at[0])]
    copies[0].start()
    start = D // HEAD_DIM * wide
    for c, ref in halves:
        for n, f in enumerate(range(0, wide, HEAD_DIM)):
            at = pl.ds(pl.multiple_of(c * wide + f, HEAD_DIM), HEAD_DIM)
            up_buf[:, at] = ref[start + n * D : start + (n + 1) * D, :].astype(F32)
    copies.append(pltpu.make_async_copy(up_buf, up, sem.at[1]))
    copies[1].start()
    start += wide // HEAD_DIM * D
    for c, ref in halves:
        mine = pl.ds(pl.multiple_of(c * HEAD_DIM, HEAD_DIM), HEAD_DIM)
        base = start + head * (4 * HEAD_DIM)
        for part, made in enumerate((query, key, value)):
            at = pl.multiple_of(base + part * HEAD_DIM, HEAD_DIM)
            made[mine, :] = ref[pl.ds(at, HEAD_DIM), :].astype(F32)
        at = pl.multiple_of(base + 3 * HEAD_DIM, HEAD_DIM)
        out[:, mine] = ref[pl.ds(at, HEAD_DIM), :].astype(F32)
        base = start + 8 * HEAD_DIM
        vec_rows[pl.ds(pl.multiple_of(c * 16, 16), 16), :] = ref[base : base + 16, :].astype(F32)
    vectors = (gain1, shift1, gain2, shift2, down_bias)
    for s, (n, cols) in enumerate(vector_slots(FF, D)):
        made = up_bias if n == 8 else vectors[n]
        made[cols] = vec_rows[s, :]
    for copy in copies:
        copy.wait()


def finish(mine, other, FF, D):
    vmem = pl.BlockSpec(memory_space=pltpu.VMEM)
    anywhere = pl.BlockSpec(memory_space=pl.ANY)
    shapes = [(D,), (D,)] + [(D, HEAD_DIM)] * 3 + [(HEAD_DIM, D), (D,), (D,), (D, FF), (FF,), (FF, D), (D,)]
    in_vmem = functools.partial(pltpu.with_memory_space_constraint, memory_space=pltpu.VMEM)
    return pl.pallas_call(
        functools.partial(finish_kernel, FF, D),
        out_shape=tuple(jax.ShapeDtypeStruct(shape, F32) for shape in shapes),
        in_specs=[vmem, vmem],
        out_specs=tuple(anywhere if n in (8, 10) else vmem for n in range(len(shapes))),
        scratch_shapes=[
            pltpu.VMEM((FF, D), F32),
            pltpu.VMEM((D, FF), F32),
            pltpu.VMEM((32, HEAD_DIM), F32),
            pltpu.SemaphoreType.DMA((2,)),
        ],
        name="finish",
    )(in_vmem(mine), in_vmem(other))


def spans(masks):
    found = [0]
    for mask in masks:
        found = found + [f ^ mask for f in found]
    return found


def stages(count):
    bits = [1 << b for b in range(count.bit_length() - 1)]
    plane, rest = [bits[0], bits[2]], bits[3:]
    found = [plane] + [rest[i : i + 2] for i in range(0, len(rest), 2)]
    if len(found) > 1 and len(found[1]) == 2:
        return [(found[0], found[1]), (found[1], found[0])] + [(masks, masks) for masks in found[2:]]
    return [(masks, masks) for masks in found]


def partners(value, masks, k):
    count = lax.axis_size("seq") * lax.axis_size("head")
    hops = [spans(side)[k] for side in masks]
    return lax.ppermute(value, BOTH, [(i, i ^ hops[i // 2 % 2]) for i in range(count)])


def all_sum(value):
    count = lax.axis_size("seq") * lax.axis_size("head")
    place = lax.axis_index("seq") * lax.axis_size("head") + lax.axis_index("head")
    width = value.shape[1]
    steps = []
    for masks in stages(count):
        code, other_code = (
            sum(((place & mask) // mask) << j for j, mask in enumerate(side)) for side in masks
        )
        steps.append((masks, jnp.where(place & 2 == 0, code, other_code)))
    for masks, code in steps:
        parts = value.reshape(1 << len(masks[0]), -1, width)
        total = lax.dynamic_index_in_dim(parts, code, 0, False).astype(F32)
        arrived = [
            partners(lax.dynamic_index_in_dim(parts, code ^ k, 0, False), masks, k)
            for k in range(1, parts.shape[0])
        ]
        for part in arrived:
            total = total + part.astype(F32)
        value = total.astype(BF16)
    for masks, code in steps[::-1]:
        parts = 1 << len(masks[0])
        found = [value] + [partners(value, masks, k) for k in range(1, parts)]
        whole = jnp.zeros((parts,) + value.shape, value.dtype)
        for k, part in enumerate(found):
            whole = lax.dynamic_update_index_in_dim(whole, part, code ^ k, 0)
        value = whole.reshape(-1, width)
    return value


def across_cores(value):
    return partners(value, ([2], [2]), 1)


def shards(
    tokens,
    cotangent,
    image_rows,
    image_fill,
    first_gain,
    first_shift,
    query_weight,
    key_weight,
    value_weight,
    out_weight,
    second_gain,
    second_shift,
    up_weight,
    up_bias,
    down_weight,
    down_bias,
):
    own, D = tokens.shape
    FF = up_weight.shape[1]
    devices = lax.axis_size("seq") * lax.axis_size("head")
    near, far = pack(query_weight, key_weight, value_weight, out_weight, tokens, cotangent)
    other = lax.ppermute(near, "head", [(0, 1), (1, 0)])
    pairs = [(i, i + 1) for i in range(1, devices - 1, 2)]
    rim = lax.ppermute(far, BOTH, pairs + [(b, a) for a, b in pairs])
    mixed, input_grad, keep, send = layer(
        tokens,
        cotangent,
        rim,
        image_rows[None],
        image_fill[None],
        first_gain[None],
        first_shift[None],
        (query_weight, key_weight, value_weight, out_weight),
        other,
        second_gain[None],
        second_shift[None],
        up_weight,
        up_bias[None],
        down_weight,
        down_bias[None],
    )
    summed = (keep.astype(F32) + across_cores(send).astype(F32)).astype(BF16)
    mine = all_sum(summed)
    return (mixed, input_grad, *finish(mine, across_cores(mine), FF, D))


def solution(mesh):
    stream = P(("seq", "head"), None)
    columns = P(None, "head")
    in_specs = (stream, stream) + (P(),) * 4 + (columns,) * 3 + (P("head", None),) + (P(),) * 6
    out_specs = (
        (stream, stream) + (P(),) * 2 + (columns,) * 3 + (P("head", None),) + (P(),) * 6
    )
    return jax.shard_map(shards, mesh=mesh, in_specs=in_specs, out_specs=out_specs, check_vma=False)
```

time: 130 us -> 93.3 us (0.72)
  Pallas kernels: 50.8 us -> 36.1 us
  other arithmetic: 13.8 us -> 0.38 us
  local copies, waits for them, and re-layouts: 10.1 us -> 0.37 us
  waiting for transfers between devices: 29 us -> 34 us
  starting transfers between devices: 24.9 us -> 21.2 us
    pallas_call x1, Pallas kernels: 50.8 us -> 32.8 us  [layer(): pl.pallas_call(functools.partial(layer_kernel, rows), out_shape=(jax.Shap...]
    convert_element_type x8 -> x1, other arithmetic: 5.97 us -> 0.21 us  [shards(): summed = (keep.astype(F32) + across_cores(send).astype(F32)).astype(BF16)]
    ppermute x17 -> x16, waiting for transfers between devices: 29 us -> 34 us  [the longest x14 24.9 us: partners(): lax.ppermute(value, BOTH, [(i, i ^ hops[i // 2 % 2]) for i in range(count)])]
    concatenate x3 -> x0, other arithmetic: 4.11 us -> none  [the longest x1 2.81 us: shards(): cot_ext = jnp.concatenate([cotangent, after[WINDOW:]])]
    unnamed x10 -> x0, local copies, waits for them, and re-layouts: 3.93 us -> none
    ppermute x17 -> x16, starting transfers between devices: 24.9 us -> 21.2 us  [the longest x14 17.5 us: partners(): lax.ppermute(value, BOTH, [(i, i ^ hops[i // 2 % 2]) for i in range(count)])]
    pallas_call x0 -> x2, Pallas kernels: none -> 3.29 us  [the longest x1 2.22 us: finish(): pl.pallas_call(functools.partial(finish_kernel, FF, D), out_shape=tuple((...]
    slice x6 -> x0, local copies, waits for them, and re-layouts: 2.82 us -> none  [the longest x1 0.83 us: shards(): tokens[own - WINDOW:]]
  transfers between devices with their start and end apart: 17 -> 16, of which waited for: 12 -> 13; matrix products, arithmetic and copies ran while one was open for 8% -> 0% of each run, Pallas kernels for 0% -> 0%
where the time goes in v1:
time: 93.3 us; the launch traced here: 93.1 us
  Pallas kernels  36.1 us (39%)
  waiting for transfers between devices  34 us (36%)
  starting transfers between devices  21.2 us (23%)
  between operations  0.99 us (1%)
    pallas_call x1, Pallas kernels, layer(): pl.pallas_call(functools.partial(layer_kernel, rows), out_shape=(jax.Shap...  32.8 us
    ppermute x14, waiting for transfers between devices, partners(): lax.ppermute(value, BOTH, [(i, i ^ hops[i // 2 % 2]) for i in range(count)])  24.9 us
    ppermute x14, starting transfers between devices, partners(): lax.ppermute(value, BOTH, [(i, i ^ hops[i // 2 % 2]) for i in range(count)])  17.5 us
    ppermute x1, waiting for transfers between devices, shards(): other = lax.ppermute(near, 'head', [(0, 1), (1, 0)])  9.1 us
    ppermute x1, starting transfers between devices, shards(): other = lax.ppermute(near, 'head', [(0, 1), (1, 0)])  3.03 us
    pallas_call x1, Pallas kernels, finish(): pl.pallas_call(functools.partial(finish_kernel, FF, D), out_shape=tuple((...  2.22 us
  transfers between devices with their start and end apart: 16, of which 13 were waited for; matrix products, arithmetic and copies ran while one was open for 0% of the time, Pallas kernels for 0%

profile of v1, /device:TPU:0, one launch (start us, length us, event | category | flops | bytes accessed | tf_op | source)
XLA Modules:
  0.0 93.1 jit_solution(8650627420701042771)
XLA Ops:
  0.6 1.1 %pack.1 = (bf16[1408,128]{1,0:T(8,128)(2,1)S(1)}, bf16[384,128]{1,0:T(8,128)(2,1)S(1)}) custom-call(bf16[256,128]{1,0:T(8,128)(2,1)} %query_ref.3, bf16[256,128]{1,0:T(8,128)(2,1)} %key_ref.3, bf16[256,128]{1,0:T(8,128)(2,1)} %value_ref.3, bf16[128,256]{1,0:T(8,128)(2,1)} %out_ref.3, bf16[3072,256]{1,0:T(8,128)(2,1)} %tok_ref.3, bf16[3072,256]{1,0:T(8,128)(2,1)} %cot_in_ref.1), custom_call_target="tpu_custom_call" | custom-call | tf_op jit(solution)/shard_map/pack/pallas_call | solution.py:561
  1.7 3.0 %collective-permute-start.1 = (bf16[1408,128]{1,0:T(8,128)(2,1)S(1)}, bf16[1408,128]{1,0:T(8,128)(2,1)S(1)}, u32[]{:S(2)}, u32[]{:S(2)}) collective-permute-start(bf16[1408,128]{1,0:T(8,128)(2,1)S(1)} %get-tuple-element.33), channel_id=1, source_target_pairs={{0,1},{1,0},{2,3},{3,2},{4,5},{5,4},{6,7},{7,6},{8,9},{9,8},{10,11... | collective-permute-start | bytes 1081352 | tf_op jit(solution)/shard_map/ppermute | solution.py:710
  4.8 0.7 collective-permute-start
  5.4 9.1 %collective-permute-done.1.heads_ref = bf16[1408,128]{1,0:T(8,128)(2,1)S(1)} collective-permute-done((bf16[1408,128]{1,0:T(8,128)(2,1)S(1)}, bf16[1408,128]{1,0:T(8,128)(2,1)S(1)}, u32[]{:S(2)}, u32[]{:S(2)}) %collective-permute-start.1) | collective-permute-done | bytes 360480 | tf_op jit(solution)/shard_map/ppermute | solution.py:710
  14.5 32.8 %layer.1 = (bf16[3072,256]{1,0:T(8,128)(2,1)}, bf16[3072,256]{1,0:T(8,128)(2,1)}, bf16[3200,128]{1,0:T(8,128)(2,1)S(1)}, bf16[3200,128]{1,0:T(8,128)(2,1)S(1)}) custom-call(bf16[3072,256]{1,0:T(8,128)(2,1)} %tok_ref.3, bf16[3072,256]{1,0:T(8,128)(2,1)} %cot_in_ref.1, bf16[384,128]{1,0:T(8,128)(2,1)S(1)} %collective-permute-done.rim_ref, s32[1,128]{1,0:T(1,128)} %bitcast.64, ...), custom_call_target="tpu_custom_call" | custom-call | tf_op jit(solution)/shard_map/layer/pallas_call | solution.py:481
  47.5 2.3 %collective-permute-done.2 = bf16[3200,128]{1,0:T(8,128)(2,1)S(1)} collective-permute-done((bf16[3200,128]{1,0:T(8,128)(2,1)S(1)}, bf16[3200,128]{1,0:T(8,128)(2,1)S(1)}, u32[]{:S(2)}, u32[]{:S(2)}) %collective-permute-start.2) | collective-permute-done | bytes 819232 | tf_op jit(solution)/shard_map/ppermute | solution.py:651
  49.8 0.2 add_convert_fusion
  50.0 2.5 %collective-permute-start.3 = (bf16[800,128]{1,0:T(8,128)(2,1)S(1)}, bf16[800,128]{1,0:T(8,128)(2,1)S(1)}, u32[]{:S(2)}, u32[]{:S(2)}) collective-permute-start(bf16[800,128]{1,0:T(8,128)(2,1)S(1)} %get-tuple-element.52), channel_id=1, source_target_pairs={{0,1},{1,0},{2,10},{3,11},{4,5},{5,4},{6,14},{7,15},{8,9},{9,8},{1... | collective-permute-start | bytes 614408 | tf_op jit(solution)/shard_map/ppermute | solution.py:651
  52.6 1.0 %collective-permute-start.5 = (bf16[800,128]{1,0:T(8,128)(2,1)S(1)}, bf16[800,128]{1,0:T(8,128)(2,1)S(1)}, u32[]{:S(2)}, u32[]{:S(2)}) collective-permute-start(bf16[800,128]{1,0:T(8,128)(2,1)S(1)} %get-tuple-element.53), channel_id=1, source_target_pairs={{0,5},{1,4},{2,26},{3,27},{4,1},{5,0},{6,30},{7,31},{8,13},{9,12},... | collective-permute-start | bytes 614408 | tf_op jit(solution)/shard_map/ppermute | solution.py:651
  53.6 0.5 collective-permute-start.4
  54.1 3.9 %collective-permute-done.3 = bf16[800,128]{1,0:T(8,128)(2,1)S(1)} collective-permute-done((bf16[800,128]{1,0:T(8,128)(2,1)S(1)}, bf16[800,128]{1,0:T(8,128)(2,1)S(1)}, u32[]{:S(2)}, u32[]{:S(2)}) %collective-permute-start.3) | collective-permute-done | bytes 204832 | tf_op jit(solution)/shard_map/ppermute | solution.py:651
  58.0 1.2 %collective-permute-done.5 = bf16[800,128]{1,0:T(8,128)(2,1)S(1)} collective-permute-done((bf16[800,128]{1,0:T(8,128)(2,1)S(1)}, bf16[800,128]{1,0:T(8,128)(2,1)S(1)}, u32[]{:S(2)}, u32[]{:S(2)}) %collective-permute-start.5) | collective-permute-done | bytes 204832 | tf_op jit(solution)/shard_map/ppermute | solution.py:651
  59.2 0.9 collective-permute-done.4
  60.2 1.6 %collective-permute-start.6 = (bf16[200,128]{1,0:T(8,128)(2,1)S(1)}, bf16[200,128]{1,0:T(8,128)(2,1)S(1)}, u32[]{:S(2)}, u32[]{:S(2)}) collective-permute-start(bf16[200,128]{1,0:T(8,128)(2,1)S(1)} %get-tuple-element.55), channel_id=1, source_target_pairs={{0,8},{1,9},{2,3},{3,2},{4,12},{5,13},{6,7},{7,6},{8,0},{9,1},{10,... | collective-permute-start | bytes 153608 | tf_op jit(solution)/shard_map/ppermute | solution.py:651
  61.9 2.5 %collective-permute-start.8 = (bf16[200,128]{1,0:T(8,128)(2,1)S(1)}, bf16[200,128]{1,0:T(8,128)(2,1)S(1)}, u32[]{:S(2)}, u32[]{:S(2)}) collective-permute-start(bf16[200,128]{1,0:T(8,128)(2,1)S(1)} %get-tuple-element.56), channel_id=1, source_target_pairs={{0,24},{1,25},{2,7},{3,6},{4,28},{5,29},{6,3},{7,2},{8,16},{9,17},... | collective-permute-start | bytes 153608 | tf_op jit(solution)/shard_map/ppermute | solution.py:651
  64.4 0.1 collective-permute-start.7
  64.5 0.5 collective-permute-done.6
  64.9 2.8 %collective-permute-done.8 = bf16[200,128]{1,0:T(8,128)(2,1)S(1)} collective-permute-done((bf16[200,128]{1,0:T(8,128)(2,1)S(1)}, bf16[200,128]{1,0:T(8,128)(2,1)S(1)}, u32[]{:S(2)}, u32[]{:S(2)}) %collective-permute-start.8) | collective-permute-done | bytes 51232 | tf_op jit(solution)/shard_map/ppermute | solution.py:651
  67.8 2.1 %collective-permute-done.7 = bf16[200,128]{1,0:T(8,128)(2,1)S(1)} collective-permute-done((bf16[200,128]{1,0:T(8,128)(2,1)S(1)}, bf16[200,128]{1,0:T(8,128)(2,1)S(1)}, u32[]{:S(2)}, u32[]{:S(2)}) %collective-permute-start.7) | collective-permute-done | bytes 51232 | tf_op jit(solution)/shard_map/ppermute | solution.py:651
  70.0 0.3 collective-permute-start.9
  70.3 1.8 %collective-permute-start.10 = (bf16[200,128]{1,0:T(8,128)(2,1)S(1)}, bf16[200,128]{1,0:T(8,128)(2,1)S(1)}, u32[]{:S(2)}, u32[]{:S(2)}) collective-permute-start(bf16[200,128]{1,0:T(8,128)(2,1)S(1)} %get-tuple-element.51), channel_id=1, source_target_pairs={{0,16},{1,17},{2,6},{3,7},{4,20},{5,21},{6,2},{7,3},{8,24},{9,25},... | collective-permute-start | bytes 153608 | tf_op jit(solution)/shard_map/ppermute | solution.py:651
  72.1 2.4 %collective-permute-start.11 = (bf16[200,128]{1,0:T(8,128)(2,1)S(1)}, bf16[200,128]{1,0:T(8,128)(2,1)S(1)}, u32[]{:S(2)}, u32[]{:S(2)}) collective-permute-start(bf16[200,128]{1,0:T(8,128)(2,1)S(1)} %get-tuple-element.51), channel_id=1, source_target_pairs={{0,24},{1,25},{2,7},{3,6},{4,28},{5,29},{6,3},{7,2},{8,16},{9,17},... | collective-permute-start | bytes 153608 | tf_op jit(solution)/shard_map/ppermute | solution.py:651
  74.5 0.8 collective-permute-done.10
  75.3 2.7 %collective-permute-done.11 = bf16[200,128]{1,0:T(8,128)(2,1)S(1)} collective-permute-done((bf16[200,128]{1,0:T(8,128)(2,1)S(1)}, bf16[200,128]{1,0:T(8,128)(2,1)S(1)}, u32[]{:S(2)}, u32[]{:S(2)}) %collective-permute-start.11) | collective-permute-done | bytes 51232 | tf_op jit(solution)/shard_map/ppermute | solution.py:651
  78.0 2.2 %collective-permute-start.12 = (bf16[800,128]{1,0:T(8,128)(2,1)S(1)}, bf16[800,128]{1,0:T(8,128)(2,1)S(1)}, u32[]{:S(2)}, u32[]{:S(2)}) collective-permute-start(bf16[800,128]{1,0:T(8,128)(2,1)S(1)} %bitcast.54), channel_id=1, source_target_pairs={{0,1},{1,0},{2,10},{3,11},{4,5},{5,4},{6,14},{7,15},{8,9},{9,8},{1... | collective-permute-start | bytes 614408 | tf_op jit(solution)/shard_map/ppermute | solution.py:651
  80.2 1.1 %collective-permute-start.14 = (bf16[800,128]{1,0:T(8,128)(2,1)S(1)}, bf16[800,128]{1,0:T(8,128)(2,1)S(1)}, u32[]{:S(2)}, u32[]{:S(2)}) collective-permute-start(bf16[800,128]{1,0:T(8,128)(2,1)S(1)} %bitcast.55), channel_id=1, source_target_pairs={{0,5},{1,4},{2,26},{3,27},{4,1},{5,0},{6,30},{7,31},{8,13},{9,12},... | collective-permute-start | bytes 614408 | tf_op jit(solution)/shard_map/ppermute | solution.py:651
  81.3 0.5 collective-permute-start.13
  81.9 3.7 %collective-permute-done.12 = bf16[800,128]{1,0:T(8,128)(2,1)S(1)} collective-permute-done((bf16[800,128]{1,0:T(8,128)(2,1)S(1)}, bf16[800,128]{1,0:T(8,128)(2,1)S(1)}, u32[]{:S(2)}, u32[]{:S(2)}) %collective-permute-start.12) | collective-permute-done | bytes 204832 | tf_op jit(solution)/shard_map/ppermute | solution.py:651
  85.7 2.1 %collective-permute-done.13 = bf16[800,128]{1,0:T(8,128)(2,1)S(1)} collective-permute-done((bf16[800,128]{1,0:T(8,128)(2,1)S(1)}, bf16[800,128]{1,0:T(8,128)(2,1)S(1)}, u32[]{:S(2)}, u32[]{:S(2)}) %collective-permute-start.13) | collective-permute-done | bytes 204832 | tf_op jit(solution)/shard_map/ppermute | solution.py:651
  87.8 0.9 collective-permute-start.15
  88.7 2.0 %collective-permute-done.15.other_ref = bf16[3200,128]{1,0:T(8,128)(2,1)S(1)} collective-permute-done((bf16[3200,128]{1,0:T(8,128)(2,1)S(1)}, bf16[3200,128]{1,0:T(8,128)(2,1)S(1)}, u32[]{:S(2)}, u32[]{:S(2)}) %collective-permute-start.15) | collective-permute-done | bytes 819232 | tf_op jit(solution)/shard_map/ppermute | solution.py:651
  90.7 2.2 %finish.1 = (f32[256]{0:T(256)}, f32[256]{0:T(256)}, f32[256,128]{1,0:T(8,128)}, f32[256,128]{1,0:T(8,128)}, f32[256,128]{1,0:T(8,128)}, /*index=5*/f32[128,256]...) custom-call(bf16[3200,128]{1,0:T(8,128)(2,1)S(1)} %bitcast.49, ...), custom_call_target="tpu_custom_call" | custom-call | tf_op jit(solution)/shard_map/finish/pallas_call | solution.py:617
  (17 shorter events, 0.6 us)
Async XLA Ops:
  1.7 12.8 %collective-permute-start.1 = (bf16[1408,128]{1,0:T(8,128)(2,1)S(1)}, bf16[1408,128]{1,0:T(8,128)(2,1)S(1)}, u32[]{:S(2)}, u32[]{:S(2)}) collective-permute-start(bf16[1408,128]{1,0:T(8,128)(2,1)S(1)} %get-tuple-element.33), channel_id=1, source_target_pairs={{0,1},{1,0},{2,3},{3,2},{4,5},{5,4},{6,7},{7,6},{8,9},{9,8},{10,11... | collective-permute-start | bytes 1081352 | tf_op jit(solution)/shard_map/ppermute | solution.py:710
  4.8 0.7 collective-permute-start
  47.4 2.4 %collective-permute-start.2 = (bf16[3200,128]{1,0:T(8,128)(2,1)S(1)}, bf16[3200,128]{1,0:T(8,128)(2,1)S(1)}, u32[]{:S(2)}, u32[]{:S(2)}) collective-permute-start(bf16[3200,128]{1,0:T(8,128)(2,1)S(1)} %get-tuple-element.37), channel_id=1, source_target_pairs={{0,2},{1,3},{2,0},{3,1},{4,6},{5,7},{6,4},{7,5},{8,10},{9,11},{10,... | collective-permute-start | bytes 2457608 | tf_op jit(solution)/shard_map/ppermute | solution.py:651
  50.0 8.0 %collective-permute-start.3 = (bf16[800,128]{1,0:T(8,128)(2,1)S(1)}, bf16[800,128]{1,0:T(8,128)(2,1)S(1)}, u32[]{:S(2)}, u32[]{:S(2)}) collective-permute-start(bf16[800,128]{1,0:T(8,128)(2,1)S(1)} %get-tuple-element.52), channel_id=1, source_target_pairs={{0,1},{1,0},{2,10},{3,11},{4,5},{5,4},{6,14},{7,15},{8,9},{9,8},{1... | collective-permute-start | bytes 614408 | tf_op jit(solution)/shard_map/ppermute | solution.py:651
  52.6 6.7 %collective-permute-start.5 = (bf16[800,128]{1,0:T(8,128)(2,1)S(1)}, bf16[800,128]{1,0:T(8,128)(2,1)S(1)}, u32[]{:S(2)}, u32[]{:S(2)}) collective-permute-start(bf16[800,128]{1,0:T(8,128)(2,1)S(1)} %get-tuple-element.53), channel_id=1, source_target_pairs={{0,5},{1,4},{2,26},{3,27},{4,1},{5,0},{6,30},{7,31},{8,13},{9,12},... | collective-permute-start | bytes 614408 | tf_op jit(solution)/shard_map/ppermute | solution.py:651
  53.6 6.5 %collective-permute-start.4 = (bf16[800,128]{1,0:T(8,128)(2,1)S(1)}, bf16[800,128]{1,0:T(8,128)(2,1)S(1)}, u32[]{:S(2)}, u32[]{:S(2)}) collective-permute-start(bf16[800,128]{1,0:T(8,128)(2,1)S(1)} %get-tuple-element.54), channel_id=1, source_target_pairs={{0,4},{1,5},{2,18},{3,19},{4,0},{5,1},{6,22},{7,23},{8,12},{9,13},... | collective-permute-start | bytes 614408 | tf_op jit(solution)/shard_map/ppermute | solution.py:651
  60.2 4.7 %collective-permute-start.6 = (bf16[200,128]{1,0:T(8,128)(2,1)S(1)}, bf16[200,128]{1,0:T(8,128)(2,1)S(1)}, u32[]{:S(2)}, u32[]{:S(2)}) collective-permute-start(bf16[200,128]{1,0:T(8,128)(2,1)S(1)} %get-tuple-element.55), channel_id=1, source_target_pairs={{0,8},{1,9},{2,3},{3,2},{4,12},{5,13},{6,7},{7,6},{8,0},{9,1},{10,... | collective-permute-start | bytes 153608 | tf_op jit(solution)/shard_map/ppermute | solution.py:651
  61.9 5.9 %collective-permute-start.8 = (bf16[200,128]{1,0:T(8,128)(2,1)S(1)}, bf16[200,128]{1,0:T(8,128)(2,1)S(1)}, u32[]{:S(2)}, u32[]{:S(2)}) collective-permute-start(bf16[200,128]{1,0:T(8,128)(2,1)S(1)} %get-tuple-element.56), channel_id=1, source_target_pairs={{0,24},{1,25},{2,7},{3,6},{4,28},{5,29},{6,3},{7,2},{8,16},{9,17},... | collective-permute-start | bytes 153608 | tf_op jit(solution)/shard_map/ppermute | solution.py:651
  64.4 5.6 %collective-permute-start.7 = (bf16[200,128]{1,0:T(8,128)(2,1)S(1)}, bf16[200,128]{1,0:T(8,128)(2,1)S(1)}, u32[]{:S(2)}, u32[]{:S(2)}) collective-permute-start(bf16[200,128]{1,0:T(8,128)(2,1)S(1)} %get-tuple-element.57), channel_id=1, source_target_pairs={{0,16},{1,17},{2,6},{3,7},{4,20},{5,21},{6,2},{7,3},{8,24},{9,25},... | collective-permute-start | bytes 153608 | tf_op jit(solution)/shard_map/ppermute | solution.py:651
  70.0 4.5 %collective-permute-start.9 = (bf16[200,128]{1,0:T(8,128)(2,1)S(1)}, bf16[200,128]{1,0:T(8,128)(2,1)S(1)}, u32[]{:S(2)}, u32[]{:S(2)}) collective-permute-start(bf16[200,128]{1,0:T(8,128)(2,1)S(1)} %get-tuple-element.51), channel_id=1, source_target_pairs={{0,8},{1,9},{2,3},{3,2},{4,12},{5,13},{6,7},{7,6},{8,0},{9,1},{10,... | collective-permute-start | bytes 153608 | tf_op jit(solution)/shard_map/ppermute | solution.py:651
  70.3 5.0 %collective-permute-start.10 = (bf16[200,128]{1,0:T(8,128)(2,1)S(1)}, bf16[200,128]{1,0:T(8,128)(2,1)S(1)}, u32[]{:S(2)}, u32[]{:S(2)}) collective-permute-start(bf16[200,128]{1,0:T(8,128)(2,1)S(1)} %get-tuple-element.51), channel_id=1, source_target_pairs={{0,16},{1,17},{2,6},{3,7},{4,20},{5,21},{6,2},{7,3},{8,24},{9,25},... | collective-permute-start | bytes 153608 | tf_op jit(solution)/shard_map/ppermute | solution.py:651
  72.1 5.9 %collective-permute-start.11 = (bf16[200,128]{1,0:T(8,128)(2,1)S(1)}, bf16[200,128]{1,0:T(8,128)(2,1)S(1)}, u32[]{:S(2)}, u32[]{:S(2)}) collective-permute-start(bf16[200,128]{1,0:T(8,128)(2,1)S(1)} %get-tuple-element.51), channel_id=1, source_target_pairs={{0,24},{1,25},{2,7},{3,6},{4,28},{5,29},{6,3},{7,2},{8,16},{9,17},... | collective-permute-start | bytes 153608 | tf_op jit(solution)/shard_map/ppermute | solution.py:651
  78.0 7.7 %collective-permute-start.12 = (bf16[800,128]{1,0:T(8,128)(2,1)S(1)}, bf16[800,128]{1,0:T(8,128)(2,1)S(1)}, u32[]{:S(2)}, u32[]{:S(2)}) collective-permute-start(bf16[800,128]{1,0:T(8,128)(2,1)S(1)} %bitcast.54), channel_id=1, source_target_pairs={{0,1},{1,0},{2,10},{3,11},{4,5},{5,4},{6,14},{7,15},{8,9},{9,8},{1... | collective-permute-start | bytes 614408 | tf_op jit(solution)/shard_map/ppermute | solution.py:651
  80.2 7.6 %collective-permute-start.14 = (bf16[800,128]{1,0:T(8,128)(2,1)S(1)}, bf16[800,128]{1,0:T(8,128)(2,1)S(1)}, u32[]{:S(2)}, u32[]{:S(2)}) collective-permute-start(bf16[800,128]{1,0:T(8,128)(2,1)S(1)} %bitcast.55), channel_id=1, source_target_pairs={{0,5},{1,4},{2,26},{3,27},{4,1},{5,0},{6,30},{7,31},{8,13},{9,12},... | collective-permute-start | bytes 614408 | tf_op jit(solution)/shard_map/ppermute | solution.py:651
  81.3 6.5 %collective-permute-start.13 = (bf16[800,128]{1,0:T(8,128)(2,1)S(1)}, bf16[800,128]{1,0:T(8,128)(2,1)S(1)}, u32[]{:S(2)}, u32[]{:S(2)}) collective-permute-start(bf16[800,128]{1,0:T(8,128)(2,1)S(1)} %bitcast.56), channel_id=1, source_target_pairs={{0,4},{1,5},{2,18},{3,19},{4,0},{5,1},{6,22},{7,23},{8,12},{9,13},... | collective-permute-start | bytes 614408 | tf_op jit(solution)/shard_map/ppermute | solution.py:651
  87.8 2.8 %collective-permute-start.15 = (bf16[3200,128]{1,0:T(8,128)(2,1)S(1)}, bf16[3200,128]{1,0:T(8,128)(2,1)S(1)}, u32[]{:S(2)}, u32[]{:S(2)}) collective-permute-start(bf16[3200,128]{1,0:T(8,128)(2,1)S(1)} %bitcast.48), channel_id=1, source_target_pairs={{0,2},{1,3},{2,0},{3,1},{4,6},{5,7},{6,4},{7,5},{8,10},{9,11},{10,... | collective-permute-start | bytes 2457608 | tf_op jit(solution)/shard_map/ppermute | solution.py:651

commit v2 on v1

v2 whole, which is shorter than its diff:
```python
import functools

import jax
import jax.numpy as jnp
from jax import lax
from jax.experimental import pallas as pl
from jax.experimental.pallas import tpu as pltpu
from jax.sharding import PartitionSpec as P

HEAD_DIM = 128
HEADS = 2
WINDOW = 96
BOTH = ("seq", "head")

EPSILON = 1e-05
MASKED = -1000000000.0
LOG2E = 1.4426950408889634
SCALE = HEAD_DIM ** (-0.5)

F32 = jnp.float32
BF16 = jnp.bfloat16
LANES = (((1,), (1,)), ((), ()))
ROWS = (((0,), (0,)), ((), ()))

CHUNK = 8
LAG = 4


def dot(a, b):
    return jnp.dot(a, b, preferred_element_type=F32)


def split_dot(a, b, how=None):
    how = how or dot
    half = a.shape[0] // 2
    if half % 16:
        return how(a, b)
    return jnp.concatenate([how(a[:half], b), how(a[half:], b)])


def dot_lanes(a, b):
    return lax.dot_general(a, b, LANES, preferred_element_type=F32)


def dot_rows(a, b):
    return lax.dot_general(a, b, ROWS, preferred_element_type=F32)


def standardize(inputs):
    center = inputs - jnp.mean(inputs, axis=1, keepdims=True)
    spread = jnp.mean(center * center, axis=1, keepdims=True)
    inverse = lax.rsqrt(spread + EPSILON)
    return center * inverse, inverse


def normalize_back(weighted, scaled, inverse):
    return inverse * (
        weighted
        - jnp.mean(weighted, axis=1, keepdims=True)
        - scaled * jnp.mean(weighted * scaled, axis=1, keepdims=True)
    )


def twice_gelu(x):
    z = x * 0.7071067811865476
    below = 1.0 + lax.erf(z)
    bell = jnp.exp2(z * z * -LOG2E)
    return x * below, below + x * bell * 0.7978845608028654


def column_sums(value):
    return jnp.sum(value, axis=0, keepdims=True)


def merge(*lists):
    marked = [
        ((n + 0.5) / len(work), k, n, job) for k, work in enumerate(lists) for n, job in enumerate(work)
    ]
    return [job for *_, job in sorted(marked, key=lambda item: item[:3])]


VECTOR_ROWS = 128


def half_rows(FF, D):
    return (2 * FF * D + 4 * D * D) // (2 * HEAD_DIM) + VECTOR_ROWS


def vector_slots(FF, D):
    found = [
        (n, slice(c, c + HEAD_DIM)) for n in range(5) for c in range(0, D, HEAD_DIM)
    ]
    return found + [(8, slice(c, c + HEAD_DIM)) for c in range(0, FF, HEAD_DIM)]


def masks():
    key_id = lax.broadcasted_iota(jnp.int32, (WINDOW, WINDOW), 0)
    query_id = lax.broadcasted_iota(jnp.int32, (WINDOW, WINDOW), 1)
    current = key_id <= query_id
    return current, key_id >= query_id, jnp.where(current, key_id, key_id - WINDOW)


def merged_scores(keys, query, current):
    raw = dot_lanes(keys, query)
    return jnp.where(current, raw[WINDOW:], raw[:WINDOW])


def soft_weights(scores, offset, low, fill):
    keep = (offset >= low) & (offset < fill)
    scores = jnp.where(keep, scores * (SCALE * LOG2E), MASKED * LOG2E)
    lifted = jnp.exp2(scores - jnp.max(scores, axis=0, keepdims=True))
    return lifted * (1.0 / jnp.sum(lifted, axis=0, keepdims=True))


def window_sum(weights, values, current_t):
    turned = weights.T
    zero = jnp.zeros_like(turned)
    return dot(jnp.where(current_t, zero, turned), values[:WINDOW]) + dot(
        jnp.where(current_t, turned, zero), values[WINDOW:]
    )


def staggered(units, *kinds):
    jobs = []
    for t in range(len(units) + LAG * (len(kinds) - 1)):
        for k, kind in enumerate(kinds):
            if 0 <= t - LAG * k < len(units):
                jobs.append(functools.partial(kind, *units[t - LAG * k]))
    return jobs


def do(jobs):
    for job in jobs:
        job()


def local_kernel(
    rows,
    x_ref,
    cot_in_ref,
    down_in_ref,
    image_rows_ref,
    image_fill_ref,
    gain1_ref,
    shift1_ref,
    query_ref,
    key_ref,
    value_ref,
    xhat,
    inv,
    qbuf,
    kbuf,
    vbuf,
    probs,
    att,
    low_mark,
    fill_mark,
    normed_t,
    cot_t,
    cot_ref,
    down_ref,
    weight,
    in_sem,
):
    own = rows * WINDOW
    step = CHUNK * WINDOW
    place = lax.axis_index("seq") * lax.axis_size("head") + lax.axis_index("head")
    for part, ref in enumerate((query_ref, key_ref, value_ref)):
        weight[:, part * HEAD_DIM : (part + 1) * HEAD_DIM] = ref[...]
    later = [
        pltpu.make_async_copy(a, b, in_sem.at[n])
        for n, (a, b) in enumerate(((cot_in_ref, cot_ref), (down_in_ref, down_ref)))
    ]
    for copy in later:
        copy.start()

    images = image_rows_ref.shape[1]
    earlier = lax.broadcasted_iota(jnp.int32, (images, images), 0) <= lax.broadcasted_iota(
        jnp.int32, (images, images), 1
    )
    counts = jnp.broadcast_to(image_rows_ref[...], (8, images)).astype(F32)
    ends = dot(counts.astype(BF16), jnp.where(earlier, 1.0, 0.0).astype(BF16))[:1]
    starts = ends - counts[:1]
    mark_rows = low_mark.shape[0]
    row = (place * rows + lax.broadcasted_iota(jnp.int32, (mark_rows, 1), 0)).astype(F32)
    opens = jnp.sum(jnp.where(starts == row, 1.0, 0.0), axis=1, keepdims=True)
    opens = jnp.where(row >= ends[:, images - 1 :], 1.0, opens)
    missing = WINDOW - image_fill_ref[...].astype(F32)
    short = jnp.sum(jnp.where(ends == row + 1.0, missing, 0.0), axis=1, keepdims=True)
    low_mark[...] = jnp.broadcast_to(
        jnp.where(opens > 0.0, 0.0, -1.0 * WINDOW), low_mark.shape
    ).astype(jnp.int32)
    fill_mark[...] = jnp.broadcast_to(WINDOW - short, fill_mark.shape).astype(jnp.int32)

    for i in range(rows // CHUNK):
        here = slice(i * step, (i + 1) * step)
        scaled, inverse = standardize(x_ref[here, :].astype(F32))
        xhat[here, :] = scaled
        inv[here, :] = inverse
        value = (scaled * gain1_ref[...] + shift1_ref[...]).astype(BF16)
        normed_t[:, here] = value.T
        made = dot(value, weight[...]).astype(BF16)
        for part, buf in enumerate((qbuf, kbuf, vbuf)):
            buf[here, :] = made[:, part * HEAD_DIM : (part + 1) * HEAD_DIM]

    current, current_t, offset = masks()
    held = {}

    def score(r):
        held[r] = merged_scores(
            kbuf[(r - 1) * WINDOW : (r + 1) * WINDOW, :], qbuf[r * WINDOW : (r + 1) * WINDOW, :], current
        )

    def soften(r):
        weights = soft_weights(
            held[r], offset, low_mark[r : r + 1, :WINDOW], fill_mark[r : r + 1, :WINDOW]
        )
        probs[r] = weights
        held[r] = weights.astype(BF16)

    def gather(r):
        values = vbuf[(r - 1) * WINDOW : (r + 1) * WINDOW, :]
        att[r * WINDOW : (r + 1) * WINDOW, :] = window_sum(held.pop(r), values, current_t).astype(BF16)

    do(staggered([(r,) for r in range(1, rows)], score, soften, gather))
    for copy in later:
        copy.wait()
    cot_t[...] = cot_ref[...].T
    down_ref[...] = (down_ref[...].astype(F32) * 0.5).astype(BF16)


def in_vmem(array):
    return pltpu.with_memory_space_constraint(array, pltpu.VMEM)


def in_hbm(array):
    return pltpu.with_memory_space_constraint(array, pltpu.HBM)


def local(tokens, cotangent, down, image_rows, image_fill, gain1, shift1, weights):
    own, D = tokens.shape
    rows = own // WINDOW
    mark_rows = -(-(rows + 1) // 8) * 8
    vmem = pl.BlockSpec(memory_space=pltpu.VMEM)
    return pl.pallas_call(
        functools.partial(local_kernel, rows),
        out_shape=(
            pltpu.VMEM((own, D), F32),
            pltpu.VMEM((own, 1), F32),
            pltpu.VMEM((own, HEAD_DIM), BF16),
            pltpu.VMEM((own, HEAD_DIM), BF16),
            pltpu.VMEM((own, HEAD_DIM), BF16),
            pltpu.VMEM((rows, WINDOW, WINDOW), F32),
            pltpu.VMEM((own, HEAD_DIM), BF16),
            pltpu.VMEM((mark_rows, 128), jnp.int32),
            pltpu.VMEM((mark_rows, 128), jnp.int32),
            pltpu.VMEM((D, own), BF16),
            pltpu.VMEM((D, own), BF16),
            pltpu.VMEM((own, D), BF16),
            pltpu.VMEM(down.shape, BF16),
        ),
        in_specs=[vmem] + [pl.BlockSpec(memory_space=pltpu.HBM)] * 2 + [vmem] * 7,
        out_specs=(vmem,) * 13,
        scratch_shapes=[
            pltpu.VMEM((D, 3 * HEAD_DIM), BF16),
            pltpu.SemaphoreType.DMA((2,)),
        ],
        compiler_params=pltpu.CompilerParams(vmem_limit_bytes=24 * 1024 * 1024),
        name="local",
    )(
        in_vmem(tokens), in_hbm(cotangent), in_hbm(down), image_rows, image_fill, gain1, shift1, *weights[:3]
    )


def layer_kernel(
    rows,
    rim_ref,
    xhat,
    inv,
    own_q,
    own_k,
    own_v,
    own_probs,
    own_att,
    low_mark,
    fill_mark,
    normed_t,
    cot_t,
    cot_ref,
    down_ref,
    x_ref,
    up_ref,
    gain1_ref,
    shift1_ref,
    query_ref,
    key_ref,
    value_ref,
    out_ref,
    heads_ref,
    gain2_ref,
    shift2_ref,
    up_bias_ref,
    down_bias_ref,
    mixed_ref,
    in_grad_ref,
    keep_ref,
    send_ref,
    rim_x,
    rim_cot,
    halo_grad,
    wqkv,
    wother,
    wout,
    rim_q,
    rim_k,
    rim_v,
    qbuf,
    kbuf,
    vbuf,
    gbuf,
    att,
    probs,
    mid_grad,
    dqkv,
    act,
    hid_grad,
    mixed_buf,
    in_grad_buf,
    acc_down,
    acc_up,
    acc_qkv,
    acc_out,
    acc_vec,
    vec_rows,
    out_sem,
):
    D = x_ref.shape[1]
    FF = up_ref.shape[1]
    own = rows * WINDOW
    head = lax.axis_index("head")
    place = lax.axis_index("seq") * lax.axis_size("head") + head
    step = CHUNK * WINDOW
    steps = rows // CHUNK
    sent = {}

    for part, ref in enumerate((query_ref, key_ref, value_ref)):
        wqkv[:, part * D : part * D + HEAD_DIM] = ref[...]
        wqkv[:, part * D + HEAD_DIM : (part + 1) * D] = heads_ref[part * D : (part + 1) * D, :]
        wother[:, part * HEAD_DIM : (part + 1) * HEAD_DIM] = heads_ref[part * D : (part + 1) * D, :]
    wout[:HEAD_DIM, :] = out_ref[...]
    for half in range(D // HEAD_DIM):
        wout[HEAD_DIM:, half * HEAD_DIM : (half + 1) * HEAD_DIM] = heads_ref[
            3 * D + half * HEAD_DIM : 3 * D + (half + 1) * HEAD_DIM, :
        ]
    acc_vec[...] = jnp.zeros_like(acc_vec)

    for half in range(D // HEAD_DIM):
        cols = slice(half * HEAD_DIM, (half + 1) * HEAD_DIM)
        near = heads_ref[4 * D + half * 2 * WINDOW : 4 * D + (half + 1) * 2 * WINDOW, :]
        far = rim_ref[half * 2 * WINDOW : (half + 1) * 2 * WINDOW, :]
        rim_x[:WINDOW, cols] = jnp.where(head == 0, far[:WINDOW], near[:WINDOW])
        rim_x[WINDOW:, cols] = jnp.where(head == 0, near[:WINDOW], far[:WINDOW])
        rim_cot[:, cols] = jnp.where(head == 0, near[WINDOW:], far[WINDOW:])

    att[WINDOW:own, :HEAD_DIM] = own_att[WINDOW:, :]
    queries = (own_q, rim_q, qbuf)
    keys = (own_k, rim_k, kbuf)
    values = (own_v, rim_v, vbuf)

    def project_rim(j):
        here = slice(j * WINDOW, (j + 1) * WINDOW)
        there = slice(WINDOW, 2 * WINDOW) if j else slice(0, WINDOW)
        scaled, _ = standardize(rim_x[there, :].astype(F32))
        value = (scaled * gain1_ref[...] + shift1_ref[...]).astype(BF16)
        made = dot(value, wqkv[...]).astype(BF16)
        for part, (_, rim, other) in enumerate((queries, keys, values)):
            rim[there, :] = made[:, part * D : part * D + HEAD_DIM]
            other[here, :] = made[:, part * D + HEAD_DIM : (part + 1) * D]

    def project(i):
        here = slice(WINDOW + i * step, WINDOW + (i + 1) * step)
        value = xhat[i * step : (i + 1) * step, :] * gain1_ref[...] + shift1_ref[...]
        made = dot(value.astype(BF16), wother[...]).astype(BF16)
        for part, (_, _, other) in enumerate((queries, keys, values)):
            other[here, :] = made[:, part * HEAD_DIM : (part + 1) * HEAD_DIM]

    current, current_t, offset = masks()
    columns = [slice(h * HEAD_DIM, (h + 1) * HEAD_DIM) for h in range(HEADS)]
    held = {}

    def row_of(bufs, j, h):
        mine, rim, other = bufs
        if h:
            return other[j * WINDOW : (j + 1) * WINDOW, :]
        if 1 <= j <= rows:
            return mine[(j - 1) * WINDOW : j * WINDOW, :]
        return rim[WINDOW:, :] if j else rim[:WINDOW, :]

    def pair(bufs, j, h):
        if h:
            return bufs[2][(j - 1) * WINDOW : (j + 1) * WINDOW, :]
        if 1 < j <= rows:
            return bufs[0][(j - 2) * WINDOW : j * WINDOW, :]
        return jnp.concatenate([row_of(bufs, j - 1, 0), row_of(bufs, j, 0)])

    def grad_of(j, h):
        return gbuf[j * WINDOW : (j + 1) * WINDOW, columns[h]]

    def probs_of(j, h):
        if h:
            return probs.at[j - 1]
        return own_probs.at[j - 1] if 1 < j <= rows else probs.at[rows + 1 + (j > 1)]

    def key_sum(weights, queries):
        zero = jnp.zeros_like(weights)
        both = jnp.concatenate([jnp.where(current, zero, weights), jnp.where(current, weights, zero)])
        made = dot(both, queries)
        return made[:WINDOW], made[WINDOW:]

    def score(j, h):
        held[j, h] = merged_scores(pair(keys, j, h), row_of(queries, j, h), current)

    def soften(j, h):
        r = j - 1
        weights = soft_weights(
            held[j, h], offset, low_mark[r : r + 1, :WINDOW], fill_mark[r : r + 1, :WINDOW]
        )
        probs_of(j, h)[...] = weights
        held[j, h] = weights.astype(BF16)

    def gather(j, h):
        r = j - 1
        att[r * WINDOW : (r + 1) * WINDOW, columns[h]] = window_sum(
            held.pop((j, h)), pair(values, j, h), current_t
        ).astype(BF16)

    def feed_forward(first, count, own_rows):
        at = first * WINDOW
        size = count * WINDOW
        here = slice(at, at + size)
        held = {}
        block = 256
        slot = at // step % 2
        grads = hid_grad.at[slot] if own_rows else halo_grad
        xs, cots = (x_ref, cot_ref) if own_rows else (rim_x.at[pl.ds(WINDOW, WINDOW)], rim_cot)
        there = here if own_rows else slice(0, size)

        def enter():
            attended = att[here, :]
            middle = xs[there, :].astype(F32) + split_dot(attended, wout[...])
            scaled, inverse = standardize(middle)
            held.update(middle=middle, scaled=scaled, inverse=inverse)
            held["normed"] = (scaled * gain2_ref[...] + shift2_ref[...]).astype(BF16)

        def hide(f):
            cols = slice(f * block, (f + 1) * block)
            cot = cots[there, :]
            hidden = dot(held["normed"], up_ref[:, cols]) + up_bias_ref[:, cols]
            active, slope = twice_gelu(hidden)
            grad = dot_lanes(cot, down_ref[cols, :]) * slope
            grads[:size, cols] = grad.astype(BF16)
            if own_rows:
                act[slot, :size, cols] = active.astype(BF16)
                acc_vec[8:9, cols] += column_sums(grad)

        def weigh(f):
            cols = slice(f * block, (f + 1) * block)
            down_part = dot(cot_t[:, here], act[slot, :size, cols])
            up_part = dot_rows(held["normed"], grads[:size, cols])
            if at:
                acc_down[:, cols] += down_part
                acc_up[:, cols] += up_part
            else:
                acc_down[:, cols] = down_part
                acc_up[:, cols] = up_part

        def mix():
            if at >= 2 * step:
                sent["mixed", at // step - 2].wait()
            mixed_buf[slot, :, :] = (
                held["middle"] + split_dot(act[slot, :size], down_ref[...]) + down_bias_ref[...]
            ).astype(BF16)
            copy = pltpu.make_async_copy(
                mixed_buf.at[slot], mixed_ref.at[pl.ds(at, size)], out_sem.at[0, at // size]
            )
            copy.start()
            sent["mixed", at // step] = copy

        def back():
            scaled = held["scaled"]
            g2 = split_dot(grads[:size, :], up_ref[...], dot_lanes)
            cot32 = cots[there, :].astype(F32)
            middle_grad = cot32 + normalize_back(g2 * gain2_ref[...], scaled, held["inverse"])
            mixing_grad = middle_grad.astype(BF16)
            if own_rows:
                mid_grad[here, :] = middle_grad
                acc_vec[2:3, :D] += column_sums(g2 * scaled)
                acc_vec[3:4, :D] += column_sums(g2)
                acc_vec[4:5, :D] += column_sums(cot32)
                out_part = dot_rows(att[here, :], mixing_grad)
                if at:
                    acc_out[...] += out_part
                else:
                    acc_out[...] = out_part
            made = split_dot(mixing_grad, wout[...], dot_lanes).astype(BF16)
            for g in range(count):
                j = first + 1 + g
                gbuf[j * WINDOW : (j + 1) * WINDOW, :] = made[g * WINDOW : (g + 1) * WINDOW]

        call = functools.partial
        parts = FF // block
        hides = [call(hide, f) for f in range(parts)]
        weighs = [call(weigh, f) for f in range(parts)] if own_rows else []
        return enter, hides, weighs, mix, back

    held_back = {}
    unfinished = {}

    def weigh_grads(j, h):
        held_back[j, h] = merged_scores(pair(values, j, h), grad_of(j, h), current)

    def soften_back(j, h):
        dweights = held_back.pop((j, h))
        weights = probs_of(j, h)[...]
        inner = jnp.sum(weights * dweights, axis=0, keepdims=True)
        dscores = (weights * (dweights - inner)).astype(BF16)
        held_back[j, h] = (dscores, weights.astype(BF16))

    def gather_back(j, h):
        r = j - 1
        dscores, weights = held_back.pop((j, h))
        found = [key_sum(dscores, row_of(queries, j, h)), key_sum(weights, grad_of(j, h))]
        if j > 1:
            there = slice((r - 1) * WINDOW, r * WINDOW)
            for part, (before, _) in enumerate(found):
                total = unfinished[part, h] + before
                at = (part + 1) * D + h * HEAD_DIM
                dqkv[there, at : at + HEAD_DIM] = (total if part else total * SCALE).astype(BF16)
        for part, (_, current_part) in enumerate(found):
            unfinished[part, h] = current_part
        if j <= rows:
            dqkv[r * WINDOW : (r + 1) * WINDOW, columns[h]] = (
                window_sum(dscores, pair(keys, j, h), current_t) * SCALE
            ).astype(BF16)

    def project_back(i):
        at = i * step
        here = slice(at, at + step)
        found = {}

        def multiply():
            grads = dqkv[here, :]
            part = dot(normed_t[:, here], grads)
            acc_qkv[...] = (acc_qkv[...] + part) if at else part
            found["g1"] = split_dot(grads, wqkv[...], dot_lanes)

        def back():
            g1 = found["g1"]
            scaled = xhat[here, :]
            acc_vec[0:1, :D] += column_sums(g1 * scaled)
            acc_vec[1:2, :D] += column_sums(g1)
            if i > 1:
                sent["grad", i - 2].wait()
            in_grad_buf[i % 2, :, :] = (
                mid_grad[here, :] + normalize_back(g1 * gain1_ref[...], scaled, inv[here, :])
            ).astype(BF16)
            copy = pltpu.make_async_copy(
                in_grad_buf.at[i % 2], in_grad_ref.at[pl.ds(at, step)], out_sem.at[1, i]
            )
            copy.start()
            sent["grad", i] = copy

        return multiply, back

    def units(first, last):
        return [(j, h) for j in range(first, last + 1) for h in range(HEADS)]

    project_rim(0)
    project_rim(rows + 1)
    for i in range(steps):
        project(i)
    forward = [(j, h) for j, h in units(1, rows + 1) if h or not 1 < j <= rows]
    do(staggered(forward, score, soften, gather))
    feeds = [feed_forward(i * CHUNK, CHUNK, True) for i in range(steps)]
    halo_enter, halo_hides, _, _, halo_back = feed_forward(rows, 1, False)
    halo = [halo_enter] + halo_hides + [halo_back]
    enter, hides, weighs, mix, back = feeds[0]
    do([enter, halo.pop(0), hides[0], hides[1], weighs[0]])
    for i in range(steps):
        enter, hides, weighs, mix, back = feeds[i]
        for f in range(2, len(hides)):
            do([hides[f], weighs[f - 1]] + halo[:1])
            halo = halo[1:]
        if i + 1 < steps:
            later = feeds[i + 1]
            do([later[0], weighs[-1], later[1][0], mix, later[1][1], back, later[2][0]] + halo[:1])
            halo = halo[1:]
        else:
            do([weighs[-1]] + halo + [mix, back])

    core = (place & 2) // 2
    wide = FF // 2
    halves = ((core, keep_ref), (1 - core, send_ref))
    after_down = D // HEAD_DIM * wide
    after_up = after_down + wide // HEAD_DIM * D

    def export_down(c, ref, f):
        at = pl.ds(pl.multiple_of(c * wide + f, D), D)
        block = (acc_down[:, at] * 0.5).astype(BF16).T
        for half in range(D // HEAD_DIM):
            ref[half * wide + f : half * wide + f + D, :] = block[
                :, half * HEAD_DIM : (half + 1) * HEAD_DIM
            ]

    def export_up(c, ref, n):
        at = pl.ds(pl.multiple_of(c * wide + n * HEAD_DIM, HEAD_DIM), HEAD_DIM)
        ref[after_down + n * D : after_down + (n + 1) * D, :] = acc_up[:, at].astype(BF16)

    def export_heads(c, ref, h, part):
        mine = pl.ds(pl.multiple_of(c * HEAD_DIM, HEAD_DIM), HEAD_DIM)
        true_head = head if h == 0 else 1 - head
        if part < 3:
            at = part * D + h * HEAD_DIM
            block = acc_qkv[mine, at : at + HEAD_DIM]
        else:
            block = acc_out[h * HEAD_DIM : (h + 1) * HEAD_DIM, mine]
        at = after_up + (true_head * 4 + part) * HEAD_DIM
        ref[pl.ds(pl.multiple_of(at, HEAD_DIM), HEAD_DIM), :] = block.astype(BF16)

    def export_vectors(c, ref):
        flat = vec_rows[pl.ds(pl.multiple_of(c * 16, 16), 16), :].astype(BF16)
        ref[after_up + 8 * HEAD_DIM :, :] = jnp.concatenate([flat] * (VECTOR_ROWS // 16))

    call = functools.partial
    exports = [call(export_down, c, ref, f) for c, ref in halves for f in range(0, wide, D)]
    exports += [call(export_up, c, ref, n) for c, ref in halves for n in range(wide // HEAD_DIM)]
    exports += [call(export_heads, c, ref, h, 3) for c, ref in halves for h in range(HEADS)]
    ends = [project_back(i) for i in range(steps)]
    backs = staggered(units(1, rows + 1), weigh_grads, soften_back, gather_back)
    marks = []
    for i in range(steps):
        done = [n for n, job in enumerate(backs) if job.func is gather_back and job.args == ((i + 1) * CHUNK + 1, 1)]
        marks.append(done[0] + 1)
    exports = merge(exports, list(range(0)))
    share = -(-len(exports) // marks[0])
    do(merge(backs[: marks[0]], exports))
    for i in range(1, steps):
        ends[i - 1][0]()
        do(merge(backs[marks[i - 1] : marks[i]], [ends[i - 1][1]]))
    do(backs[marks[-1] :])
    ends[-1][0]()
    ends[-1][1]()

    for c, ref in halves:
        do([call(export_heads, c, ref, h, part) for h in range(HEADS) for part in range(3)])
    for n, (row, cols) in enumerate(vector_slots(FF, D)):
        vec_rows[n : n + 1, :] = acc_vec[row : row + 1, cols]
    for c, ref in halves:
        export_vectors(c, ref)
    for kind in ("mixed", "grad"):
        for i in range(max(steps - 2, 0), steps):
            sent[kind, i].wait()


def layer(
    rim, made, tokens, up, gain1, shift1, weights, other, gain2, shift2, up_bias, down_bias
):
    own, D = tokens.shape
    FF = up.shape[1]
    rows = own // WINDOW
    count = own + 2 * WINDOW
    half = half_rows(FF, D)
    tokens, up, rim, other = in_vmem(tokens), in_vmem(up), in_vmem(rim), in_vmem(other)
    made = [in_vmem(array) for array in made]
    vmem = pl.BlockSpec(memory_space=pltpu.VMEM)
    anywhere = pl.BlockSpec(memory_space=pl.ANY)
    steps = rows // CHUNK
    return pl.pallas_call(
        functools.partial(layer_kernel, rows),
        out_shape=(
            jax.ShapeDtypeStruct((own, D), BF16),
            jax.ShapeDtypeStruct((own, D), BF16),
            pltpu.VMEM((half, HEAD_DIM), BF16),
            pltpu.VMEM((half, HEAD_DIM), BF16),
        ),
        in_specs=[vmem] * 27,
        out_specs=(anywhere, anywhere, vmem, vmem),
        scratch_shapes=[
            pltpu.VMEM((2 * WINDOW, D), BF16),
            pltpu.VMEM((WINDOW, D), BF16),
            pltpu.VMEM((WINDOW, FF), BF16),
            pltpu.VMEM((D, 3 * D), BF16),
            pltpu.VMEM((D, 3 * HEAD_DIM), BF16),
            pltpu.VMEM((D, D), BF16),
            pltpu.VMEM((2 * WINDOW, HEAD_DIM), BF16),
            pltpu.VMEM((2 * WINDOW, HEAD_DIM), BF16),
            pltpu.VMEM((2 * WINDOW, HEAD_DIM), BF16),
            pltpu.VMEM((count, HEAD_DIM), BF16),
            pltpu.VMEM((count, HEAD_DIM), BF16),
            pltpu.VMEM((count, HEAD_DIM), BF16),
            pltpu.VMEM((count, D), BF16),
            pltpu.VMEM((count - WINDOW, D), BF16),
            pltpu.VMEM((rows + 3, WINDOW, WINDOW), F32),
            pltpu.VMEM((own, D), F32),
            pltpu.VMEM((own, 3 * D), BF16),
            pltpu.VMEM((2, CHUNK * WINDOW, FF), BF16),
            pltpu.VMEM((2, CHUNK * WINDOW, FF), BF16),
            pltpu.VMEM((2, CHUNK * WINDOW, D), BF16),
            pltpu.VMEM((2, CHUNK * WINDOW, D), BF16),
            pltpu.VMEM((D, FF), F32),
            pltpu.VMEM((D, FF), F32),
            pltpu.VMEM((D, 3 * D), F32),
            pltpu.VMEM((D, D), F32),
            pltpu.VMEM((16, FF), F32),
            pltpu.VMEM((32, HEAD_DIM), F32),
            pltpu.SemaphoreType.DMA((2, steps)),
        ],
        compiler_params=pltpu.CompilerParams(vmem_limit_bytes=34 * 1024 * 1024),
        name="layer",
    )(
        rim, *made, tokens, up, gain1, shift1, *weights, other, gain2, shift2, up_bias, down_bias
    )


def pack_kernel(query_ref, key_ref, value_ref, out_ref, tok_ref, cot_ref, near_ref, far_ref, sem):
    D = query_ref.shape[0]
    own = tok_ref.shape[0]
    head = lax.axis_index("head")
    moves = [
        (ref, near_ref.at[pl.ds(part * D, D)]) for part, ref in enumerate((query_ref, key_ref, value_ref))
    ]
    last = own - WINDOW
    near_from = pl.multiple_of((1 - head) * last, WINDOW)
    far_from = pl.multiple_of(head * last, WINDOW)
    for half in range(D // HEAD_DIM):
        cols = pl.ds(half * HEAD_DIM, HEAD_DIM)
        moves.append((out_ref.at[:, cols], near_ref.at[pl.ds(3 * D + half * HEAD_DIM, HEAD_DIM)]))
        for k, ref in enumerate((tok_ref, cot_ref)):
            at = (half * 2 + k) * WINDOW
            moves.append((ref.at[pl.ds(near_from, WINDOW), cols], near_ref.at[pl.ds(4 * D + at, WINDOW)]))
            moves.append((ref.at[pl.ds(far_from, WINDOW), cols], far_ref.at[pl.ds(at, WINDOW)]))
    copies = [pltpu.make_async_copy(a, b, sem.at[n]) for n, (a, b) in enumerate(moves)]
    for copy in copies:
        copy.start()
    for copy in copies:
        copy.wait()


def pack(query_weight, key_weight, value_weight, out_weight, tokens, cotangent):
    D = query_weight.shape[0]
    rim = 2 * WINDOW * D // HEAD_DIM
    anywhere = pl.BlockSpec(memory_space=pl.ANY)
    vmem = pl.BlockSpec(memory_space=pltpu.VMEM)
    return pl.pallas_call(
        pack_kernel,
        out_shape=(pltpu.VMEM((4 * D + rim, HEAD_DIM), BF16), pltpu.VMEM((rim, HEAD_DIM), BF16)),
        in_specs=[anywhere] * 6,
        out_specs=(vmem, vmem),
        scratch_shapes=[pltpu.SemaphoreType.DMA((3 + 5 * (D // HEAD_DIM),))],
        name="pack",
    )(query_weight, key_weight, value_weight, out_weight, tokens, cotangent)


def finish_kernel(FF, D, mine_ref, other_ref, *refs):
    outs, (down_buf, up_buf, vec_rows, sem) = refs[:12], refs[12:]
    gain1, shift1, query, key, value, out, gain2, shift2, up, up_bias, down, down_bias = outs
    core = lax.axis_index("seq") % 2
    head = lax.axis_index("head")
    halves = ((core, mine_ref), (1 - core, other_ref))
    wide = FF // 2
    for c, ref in halves:
        rows = pl.ds(pl.multiple_of(c * wide, wide), wide)
        for half in range(D // HEAD_DIM):
            down_buf[rows, half * HEAD_DIM : (half + 1) * HEAD_DIM] = ref[
                half * wide : (half + 1) * wide, :
            ].astype(F32)
    copies = [pltpu.make_async_copy(down_buf, down, sem.at[0])]
    copies[0].start()
    start = D // HEAD_DIM * wide
    for c, ref in halves:
        for n, f in enumerate(range(0, wide, HEAD_DIM)):
            at = pl.ds(pl.multiple_of(c * wide + f, HEAD_DIM), HEAD_DIM)
            up_buf[:, at] = ref[start + n * D : start + (n + 1) * D, :].astype(F32)
    copies.append(pltpu.make_async_copy(up_buf, up, sem.at[1]))
    copies[1].start()
    start += wide // HEAD_DIM * D
    for c, ref in halves:
        mine = pl.ds(pl.multiple_of(c * HEAD_DIM, HEAD_DIM), HEAD_DIM)
        base = start + head * (4 * HEAD_DIM)
        for part, made in enumerate((query, key, value)):
            at = pl.multiple_of(base + part * HEAD_DIM, HEAD_DIM)
            made[mine, :] = ref[pl.ds(at, HEAD_DIM), :].astype(F32)
        at = pl.multiple_of(base + 3 * HEAD_DIM, HEAD_DIM)
        out[:, mine] = ref[pl.ds(at, HEAD_DIM), :].astype(F32)
        base = start + 8 * HEAD_DIM
        vec_rows[pl.ds(pl.multiple_of(c * 16, 16), 16), :] = ref[base : base + 16, :].astype(F32)
    vectors = (gain1, shift1, gain2, shift2, down_bias)
    for s, (n, cols) in enumerate(vector_slots(FF, D)):
        made = up_bias if n == 8 else vectors[n]
        made[cols] = vec_rows[s, :]
    for copy in copies:
        copy.wait()


def finish(mine, other, FF, D):
    vmem = pl.BlockSpec(memory_space=pltpu.VMEM)
    anywhere = pl.BlockSpec(memory_space=pl.ANY)
    shapes = [(D,), (D,)] + [(D, HEAD_DIM)] * 3 + [(HEAD_DIM, D), (D,), (D,), (D, FF), (FF,), (FF, D), (D,)]
    return pl.pallas_call(
        functools.partial(finish_kernel, FF, D),
        out_shape=tuple(jax.ShapeDtypeStruct(shape, F32) for shape in shapes),
        in_specs=[vmem, vmem],
        out_specs=tuple(anywhere if n in (8, 10) else vmem for n in range(len(shapes))),
        scratch_shapes=[
            pltpu.VMEM((FF, D), F32),
            pltpu.VMEM((D, FF), F32),
            pltpu.VMEM((32, HEAD_DIM), F32),
            pltpu.SemaphoreType.DMA((2,)),
        ],
        name="finish",
    )(in_vmem(mine), in_vmem(other))


def spans(masks):
    found = [0]
    for mask in masks:
        found = found + [f ^ mask for f in found]
    return found


def stages(count):
    bits = [1 << b for b in range(count.bit_length() - 1)]
    plane, rest = [bits[0], bits[2]], bits[3:]
    found = [plane] + [rest[i : i + 2] for i in range(0, len(rest), 2)]
    if len(found) > 1 and len(found[1]) == 2:
        return [(found[0], found[1]), (found[1], found[0])] + [(masks, masks) for masks in found[2:]]
    return [(masks, masks) for masks in found]


def partners(value, masks, k):
    count = lax.axis_size("seq") * lax.axis_size("head")
    hops = [spans(side)[k] for side in masks]
    return lax.ppermute(value, BOTH, [(i, i ^ hops[i // 2 % 2]) for i in range(count)])


def all_sum(value):
    count = lax.axis_size("seq") * lax.axis_size("head")
    place = lax.axis_index("seq") * lax.axis_size("head") + lax.axis_index("head")
    width = value.shape[1]
    steps = []
    for masks in stages(count):
        code, other_code = (
            sum(((place & mask) // mask) << j for j, mask in enumerate(side)) for side in masks
        )
        steps.append((masks, jnp.where(place & 2 == 0, code, other_code)))
    def spread(value, masks, code):
        parts = 1 << len(masks[0])
        found = [value] + [partners(value, masks, k) for k in range(1, parts)]
        whole = jnp.zeros((parts,) + value.shape, value.dtype)
        for k, part in enumerate(found):
            whole = lax.dynamic_update_index_in_dim(whole, part, code ^ k, 0)
        return whole

    for masks, code in steps[:-1]:
        parts = value.reshape(1 << len(masks[0]), -1, width)
        total = lax.dynamic_index_in_dim(parts, code, 0, False).astype(F32)
        arrived = [
            partners(lax.dynamic_index_in_dim(parts, code ^ k, 0, False), masks, k)
            for k in range(1, parts.shape[0])
        ]
        for part in arrived:
            total = total + part.astype(F32)
        value = total.astype(BF16)
    whole = spread(value, *steps[-1])
    total = whole[0].astype(F32)
    for part in whole[1:]:
        total = total + part.astype(F32)
    value = total.astype(BF16)
    for masks, code in steps[-2::-1]:
        value = spread(value, masks, code).reshape(-1, width)
    return value


def across_cores(value):
    return partners(value, ([2], [2]), 1)


def shards(
    tokens,
    cotangent,
    image_rows,
    image_fill,
    first_gain,
    first_shift,
    query_weight,
    key_weight,
    value_weight,
    out_weight,
    second_gain,
    second_shift,
    up_weight,
    up_bias,
    down_weight,
    down_bias,
):
    own, D = tokens.shape
    FF = up_weight.shape[1]
    devices = lax.axis_size("seq") * lax.axis_size("head")
    near, far = pack(query_weight, key_weight, value_weight, out_weight, tokens, cotangent)
    other = lax.ppermute(near, "head", [(0, 1), (1, 0)])
    pairs = [(i, i + 1) for i in range(1, devices - 1, 2)]
    rim = lax.ppermute(far, BOTH, pairs + [(b, a) for a, b in pairs])
    weights = (query_weight, key_weight, value_weight, out_weight)
    gain1, shift1 = first_gain[None], first_shift[None]
    made = local(tokens, cotangent, down_weight, image_rows[None], image_fill[None], gain1, shift1, weights)
    mixed, input_grad, keep, send = layer(
        rim,
        made,
        tokens,
        up_weight,
        gain1,
        shift1,
        weights,
        other,
        second_gain[None],
        second_shift[None],
        up_bias[None],
        down_bias[None],
    )
    summed = (keep.astype(F32) + across_cores(send).astype(F32)).astype(BF16)
    mine = all_sum(summed)
    return (mixed, input_grad, *finish(mine, across_cores(mine), FF, D))


def solution(mesh):
    stream = P(("seq", "head"), None)
    columns = P(None, "head")
    in_specs = (stream, stream) + (P(),) * 4 + (columns,) * 3 + (P("head", None),) + (P(),) * 6
    out_specs = (
        (stream, stream) + (P(),) * 2 + (columns,) * 3 + (P("head", None),) + (P(),) * 6
    )
    return jax.shard_map(shards, mesh=mesh, in_specs=in_specs, out_specs=out_specs, check_vma=False)
```

time: 93.3 us -> 85.2 us (0.913)
  starting transfers between devices: 21.2 us -> 16.1 us
  waiting for transfers between devices: 34 us -> 30 us
    ppermute x14 -> x11, starting transfers between devices: 17.5 us -> 12.4 us  [partners(): lax.ppermute(value, BOTH, [(i, i ^ hops[i // 2 % 2]) for i in range(count)])]
    ppermute x1, waiting for transfers between devices: 9.1 us -> 4.67 us  [shards(): other = lax.ppermute(near, 'head', [(0, 1), (1, 0)])]
    pallas_call x0 -> x1, Pallas kernels: none -> 4.27 us  [local(): pl.pallas_call(functools.partial(local_kernel, rows), out_shape=(pltpu.VM...]
    pallas_call x1, Pallas kernels: 32.8 us -> 29.1 us  [layer(): pl.pallas_call(functools.partial(layer_kernel, rows), out_shape=(jax.Shap...]
    ppermute x14 -> x11, waiting for transfers between devices: 24.9 us -> 25.3 us  [partners(): lax.ppermute(value, BOTH, [(i, i ^ hops[i // 2 % 2]) for i in range(count)])]
  transfers between devices with their start and end apart: 16 -> 13, of which waited for: 13 -> 11; matrix products, arithmetic and copies ran while one was open for 0% -> 0% of each run, Pallas kernels for 0% -> 5%
where the time goes in v2:
time: 85.2 us; the launch traced here: 85 us
  Pallas kernels  36.7 us (43%)
  waiting for transfers between devices  30 us (35%)
  starting transfers between devices  16.1 us (19%)
  between operations  1.17 us (1%)
    pallas_call x1, Pallas kernels, layer(): pl.pallas_call(functools.partial(layer_kernel, rows), out_shape=(jax.Shap...  29.1 us
    ppermute x11, waiting for transfers between devices, partners(): lax.ppermute(value, BOTH, [(i, i ^ hops[i // 2 % 2]) for i in range(count)])  25.3 us
    ppermute x11, starting transfers between devices, partners(): lax.ppermute(value, BOTH, [(i, i ^ hops[i // 2 % 2]) for i in range(count)])  12.4 us
    ppermute x1, waiting for transfers between devices, shards(): other = lax.ppermute(near, 'head', [(0, 1), (1, 0)])  4.67 us
    pallas_call x1, Pallas kernels, local(): pl.pallas_call(functools.partial(local_kernel, rows), out_shape=(pltpu.VM...  4.27 us
    ppermute x1, starting transfers between devices, shards(): other = lax.ppermute(near, 'head', [(0, 1), (1, 0)])  3.03 us
    pallas_call x1, Pallas kernels, finish(): pl.pallas_call(functools.partial(finish_kernel, FF, D), out_shape=tuple((...  2.22 us
  transfers between devices with their start and end apart: 13, of which 11 were waited for; matrix products, arithmetic and copies ran while one was open for 0% of the time, Pallas kernels for 5%

profile of v2, /device:TPU:0, one launch (start us, length us, event | category | flops | bytes accessed | tf_op | source)
XLA Modules:
  0.0 85.0 jit_solution(6439201666652184772)
XLA Ops:
  0.7 1.2 %pack.1 = (bf16[1408,128]{1,0:T(8,128)(2,1)S(1)}, bf16[384,128]{1,0:T(8,128)(2,1)S(1)}) custom-call(bf16[256,128]{1,0:T(8,128)(2,1)} %query_ref.5, bf16[256,128]{1,0:T(8,128)(2,1)} %key_ref.5, bf16[256,128]{1,0:T(8,128)(2,1)} %value_ref.5, bf16[128,256]{1,0:T(8,128)(2,1)} %out_ref.3, bf16[3072,256]{1,0:T(8,128)(2,1)} %x_ref.3, bf16[3072,256]{1,0:T(8,128)(2,1)} %cot_in_ref.1), custom_call_target="tpu_custom_call" | custom-call | tf_op jit(solution)/shard_map/pack/pallas_call | solution.py:754
  1.9 3.0 %collective-permute-start.1 = (bf16[1408,128]{1,0:T(8,128)(2,1)S(1)}, bf16[1408,128]{1,0:T(8,128)(2,1)S(1)}, u32[]{:S(2)}, u32[]{:S(2)}) collective-permute-start(bf16[1408,128]{1,0:T(8,128)(2,1)S(1)} %get-tuple-element.59), channel_id=1, source_target_pairs={{0,1},{1,0},{2,3},{3,2},{4,5},{5,4},{6,7},{7,6},{8,9},{9,8},{10,11... | collective-permute-start | bytes 1081352 | tf_op jit(solution)/shard_map/ppermute | solution.py:910
  4.9 0.7 collective-permute-start
  5.7 4.3 %local.1 = (f32[3072,256]{1,0:T(8,128)S(1)}, f32[3072,1]{1,0:T(8,128)S(1)}, bf16[3072,128]{1,0:T(8,128)(2,1)S(1)}, bf16[3072,128]{1,0:T(8,128)(2,1)S(1)}, bf16[3...) custom-call(bf16[3072,256]{1,0:T(8,128)(2,1)S(1)} %copy-done, ...), custom_call_target="tpu_custom_call" | custom-call | tf_op jit(solution)/shard_map/local/pallas_call | solution.py:245
  10.0 4.7 %collective-permute-done.1.heads_ref = bf16[1408,128]{1,0:T(8,128)(2,1)S(1)} collective-permute-done((bf16[1408,128]{1,0:T(8,128)(2,1)S(1)}, bf16[1408,128]{1,0:T(8,128)(2,1)S(1)}, u32[]{:S(2)}, u32[]{:S(2)}) %collective-permute-start.1) | collective-permute-done | bytes 360480 | tf_op jit(solution)/shard_map/ppermute | solution.py:910
  14.7 29.1 %layer.1 = (bf16[3072,256]{1,0:T(8,128)(2,1)}, bf16[3072,256]{1,0:T(8,128)(2,1)}, bf16[3200,128]{1,0:T(8,128)(2,1)S(1)}, bf16[3200,128]{1,0:T(8,128)(2,1)}) custom-call(bf16[384,128]{1,0:T(8,128)(2,1)S(1)} %collective-permute-done.rim_ref, f32[3072,256]{1,0:T(8,128)S(1)} %get-tuple-element.46.xhat, f32[3072,1]{1,0:T(8,128)S(1)} %get-tuple-element.47.inv, ...), custom_call_target="tpu_custom_call" | custom-call | tf_op jit(solution)/shard_map/layer/pallas_call | solution.py:678
  43.8 0.1 collective-permute-start.2
  44.0 2.5 %collective-permute-done.2 = bf16[3200,128]{1,0:T(8,128)(2,1)S(1)} collective-permute-done((bf16[3200,128]{1,0:T(8,128)(2,1)}, bf16[3200,128]{1,0:T(8,128)(2,1)S(1)}, u32[]{:S(2)}, u32[]{:S(2)}) %collective-permute-start.2) | collective-permute-done | bytes 819232 | tf_op jit(solution)/shard_map/ppermute | solution.py:843
  46.4 0.2 add_convert_fusion
  46.7 2.6 %collective-permute-start.3 = (bf16[800,128]{1,0:T(8,128)(2,1)S(1)}, bf16[800,128]{1,0:T(8,128)(2,1)S(1)}, u32[]{:S(2)}, u32[]{:S(2)}) collective-permute-start(bf16[800,128]{1,0:T(8,128)(2,1)S(1)} %get-tuple-element.80), channel_id=1, source_target_pairs={{0,1},{1,0},{2,10},{3,11},{4,5},{5,4},{6,14},{7,15},{8,9},{9,8},{1... | collective-permute-start | bytes 614408 | tf_op jit(solution)/shard_map/ppermute | solution.py:843
  49.3 1.5 %collective-permute-start.4 = (bf16[800,128]{1,0:T(8,128)(2,1)S(1)}, bf16[800,128]{1,0:T(8,128)(2,1)S(1)}, u32[]{:S(2)}, u32[]{:S(2)}) collective-permute-start(bf16[800,128]{1,0:T(8,128)(2,1)S(1)} %get-tuple-element.82), channel_id=1, source_target_pairs={{0,4},{1,5},{2,18},{3,19},{4,0},{5,1},{6,22},{7,23},{8,12},{9,13},... | collective-permute-start | bytes 614408 | tf_op jit(solution)/shard_map/ppermute | solution.py:843
  50.8 2.2 %collective-permute-done.3 = bf16[800,128]{1,0:T(8,128)(2,1)S(1)} collective-permute-done((bf16[800,128]{1,0:T(8,128)(2,1)S(1)}, bf16[800,128]{1,0:T(8,128)(2,1)S(1)}, u32[]{:S(2)}, u32[]{:S(2)}) %collective-permute-start.3) | collective-permute-done | bytes 204832 | tf_op jit(solution)/shard_map/ppermute | solution.py:843
  53.0 2.0 %collective-permute-done.4 = bf16[800,128]{1,0:T(8,128)(2,1)S(1)} collective-permute-done((bf16[800,128]{1,0:T(8,128)(2,1)S(1)}, bf16[800,128]{1,0:T(8,128)(2,1)S(1)}, u32[]{:S(2)}, u32[]{:S(2)}) %collective-permute-start.4) | collective-permute-done | bytes 204832 | tf_op jit(solution)/shard_map/ppermute | solution.py:843
  55.0 2.4 %collective-permute-done.5 = bf16[800,128]{1,0:T(8,128)(2,1)S(1)} collective-permute-done((bf16[800,128]{1,0:T(8,128)(2,1)S(1)}, bf16[800,128]{1,0:T(8,128)(2,1)S(1)}, u32[]{:S(2)}, u32[]{:S(2)}) %collective-permute-start.5) | collective-permute-done | bytes 204832 | tf_op jit(solution)/shard_map/ppermute | solution.py:843
  57.4 0.1 broadcast.7.clone
  57.5 0.1 bitcast_dynamic-update-slice_fusion.6
  57.7 1.6 %collective-permute-start.6 = (bf16[800,128]{1,0:T(8,128)(2,1)S(1)}, bf16[800,128]{1,0:T(8,128)(2,1)S(1)}, u32[]{:S(2)}, u32[]{:S(2)}) collective-permute-start(bf16[800,128]{1,0:T(8,128)(2,1)S(1)} %get-tuple-element.79), channel_id=1, source_target_pairs={{0,8},{1,9},{2,3},{3,2},{4,12},{5,13},{6,7},{7,6},{8,0},{9,1},{10,... | collective-permute-start | bytes 614408 | tf_op jit(solution)/shard_map/ppermute | solution.py:843
  59.3 1.9 %collective-permute-start.7 = (bf16[800,128]{1,0:T(8,128)(2,1)S(1)}, bf16[800,128]{1,0:T(8,128)(2,1)S(1)}, u32[]{:S(2)}, u32[]{:S(2)}) collective-permute-start(bf16[800,128]{1,0:T(8,128)(2,1)S(1)} %get-tuple-element.79), channel_id=1, source_target_pairs={{0,16},{1,17},{2,6},{3,7},{4,20},{5,21},{6,2},{7,3},{8,24},{9,25},... | collective-permute-start | bytes 614408 | tf_op jit(solution)/shard_map/ppermute | solution.py:843
  61.2 0.9 %collective-permute-start.8 = (bf16[800,128]{1,0:T(8,128)(2,1)S(1)}, bf16[800,128]{1,0:T(8,128)(2,1)S(1)}, u32[]{:S(2)}, u32[]{:S(2)}) collective-permute-start(bf16[800,128]{1,0:T(8,128)(2,1)S(1)} %get-tuple-element.79), channel_id=1, source_target_pairs={{0,24},{1,25},{2,7},{3,6},{4,28},{5,29},{6,3},{7,2},{8,16},{9,17},... | collective-permute-start | bytes 614408 | tf_op jit(solution)/shard_map/ppermute | solution.py:843
  62.1 1.4 %collective-permute-done.6 = bf16[800,128]{1,0:T(8,128)(2,1)S(1)} collective-permute-done((bf16[800,128]{1,0:T(8,128)(2,1)S(1)}, bf16[800,128]{1,0:T(8,128)(2,1)S(1)}, u32[]{:S(2)}, u32[]{:S(2)}) %collective-permute-start.6) | collective-permute-done | bytes 204832 | tf_op jit(solution)/shard_map/ppermute | solution.py:843
  63.5 6.8 %collective-permute-done.7 = bf16[800,128]{1,0:T(8,128)(2,1)S(1)} collective-permute-done((bf16[800,128]{1,0:T(8,128)(2,1)S(1)}, bf16[800,128]{1,0:T(8,128)(2,1)S(1)}, u32[]{:S(2)}, u32[]{:S(2)}) %collective-permute-start.7) | collective-permute-done | bytes 204832 | tf_op jit(solution)/shard_map/ppermute | solution.py:843
  70.5 0.1 broadcast.7
  70.6 0.1 constant_dynamic-update-slice_fusion
  70.7 1.3 %collective-permute-start.9 = (bf16[800,128]{1,0:T(8,128)(2,1)S(1)}, bf16[800,128]{1,0:T(8,128)(2,1)S(1)}, u32[]{:S(2)}, u32[]{:S(2)}) collective-permute-start(bf16[800,128]{1,0:T(8,128)(2,1)S(1)} %bitcast.49), channel_id=1, source_target_pairs={{0,1},{1,0},{2,10},{3,11},{4,5},{5,4},{6,14},{7,15},{8,9},{9,8},{1... | collective-permute-start | bytes 614408 | tf_op jit(solution)/shard_map/ppermute | solution.py:843
  72.1 1.5 %collective-permute-start.10 = (bf16[800,128]{1,0:T(8,128)(2,1)S(1)}, bf16[800,128]{1,0:T(8,128)(2,1)S(1)}, u32[]{:S(2)}, u32[]{:S(2)}) collective-permute-start(bf16[800,128]{1,0:T(8,128)(2,1)S(1)} %bitcast.50), channel_id=1, source_target_pairs={{0,4},{1,5},{2,18},{3,19},{4,0},{5,1},{6,22},{7,23},{8,12},{9,13},... | collective-permute-start | bytes 614408 | tf_op jit(solution)/shard_map/ppermute | solution.py:843
  73.5 0.7 collective-permute-start.11
  74.3 2.3 %collective-permute-done.9 = bf16[800,128]{1,0:T(8,128)(2,1)S(1)} collective-permute-done((bf16[800,128]{1,0:T(8,128)(2,1)S(1)}, bf16[800,128]{1,0:T(8,128)(2,1)S(1)}, u32[]{:S(2)}, u32[]{:S(2)}) %collective-permute-start.9) | collective-permute-done | bytes 204832 | tf_op jit(solution)/shard_map/ppermute | solution.py:843
  76.6 1.2 %collective-permute-done.10 = bf16[800,128]{1,0:T(8,128)(2,1)S(1)} collective-permute-done((bf16[800,128]{1,0:T(8,128)(2,1)S(1)}, bf16[800,128]{1,0:T(8,128)(2,1)S(1)}, u32[]{:S(2)}, u32[]{:S(2)}) %collective-permute-start.10) | collective-permute-done | bytes 204832 | tf_op jit(solution)/shard_map/ppermute | solution.py:843
  77.8 2.3 %collective-permute-done.11 = bf16[800,128]{1,0:T(8,128)(2,1)S(1)} collective-permute-done((bf16[800,128]{1,0:T(8,128)(2,1)S(1)}, bf16[800,128]{1,0:T(8,128)(2,1)S(1)}, u32[]{:S(2)}, u32[]{:S(2)}) %collective-permute-start.11) | collective-permute-done | bytes 204832 | tf_op jit(solution)/shard_map/ppermute | solution.py:843
  80.2 0.2 collective-permute-start.12
  80.5 2.2 %collective-permute-done.12.other_ref = bf16[3200,128]{1,0:T(8,128)(2,1)S(1)} collective-permute-done((bf16[3200,128]{1,0:T(8,128)(2,1)S(1)}, bf16[3200,128]{1,0:T(8,128)(2,1)S(1)}, u32[]{:S(2)}, u32[]{:S(2)}) %collective-permute-start.12) | collective-permute-done | bytes 819232 | tf_op jit(solution)/shard_map/ppermute | solution.py:843
  82.6 2.2 %finish.1 = (f32[256]{0:T(256)}, f32[256]{0:T(256)}, f32[256,128]{1,0:T(8,128)}, f32[256,128]{1,0:T(8,128)}, f32[256,128]{1,0:T(8,128)}, /*index=5*/f32[128,256]...) custom-call(bf16[3200,128]{1,0:T(8,128)(2,1)S(1)} %bitcast.36, ...), custom_call_target="tpu_custom_call" | custom-call | tf_op jit(solution)/shard_map/finish/pallas_call | solution.py:809
  (38 shorter events, 0.4 us)
Async XLA Ops:
  0.6 4.9 %copy-start = (bf16[3072,256]{1,0:T(8,128)(2,1)S(1)}, bf16[3072,256]{1,0:T(8,128)(2,1)}, u32[]{:S(2)}) copy-start(bf16[3072,256]{1,0:T(8,128)(2,1)} %x_ref.3) | copy-start | bytes 4718596
  0.7 4.9 %copy-start.1 = (bf16[256,128]{1,0:T(8,128)(2,1)S(1)}, bf16[256,128]{1,0:T(8,128)(2,1)}, u32[]{:S(2)}) copy-start(bf16[256,128]{1,0:T(8,128)(2,1)} %query_ref.5) | copy-start | bytes 196612
  0.7 4.9 %copy-start.2 = (bf16[256,128]{1,0:T(8,128)(2,1)S(1)}, bf16[256,128]{1,0:T(8,128)(2,1)}, u32[]{:S(2)}) copy-start(bf16[256,128]{1,0:T(8,128)(2,1)} %key_ref.5) | copy-start | bytes 196612
  0.7 4.9 %copy-start.3 = (bf16[256,128]{1,0:T(8,128)(2,1)S(1)}, bf16[256,128]{1,0:T(8,128)(2,1)}, u32[]{:S(2)}) copy-start(bf16[256,128]{1,0:T(8,128)(2,1)} %value_ref.5) | copy-start | bytes 196612
  0.7 4.9 %copy-start.7 = (f32[256]{0:T(256)S(1)}, f32[256]{0:T(256)}, u32[]{:S(2)}) copy-start(f32[256]{0:T(256)} %param.20) | copy-start | bytes 3076
  0.7 4.9 %copy-start.8 = (f32[256]{0:T(256)S(1)}, f32[256]{0:T(256)}, u32[]{:S(2)}) copy-start(f32[256]{0:T(256)} %param.21) | copy-start | bytes 3076
  0.7 4.9 %copy-start.12 = (s32[128]{0:T(128)S(1)}, s32[128]{0:T(128)}, u32[]{:S(2)}) copy-start(s32[128]{0:T(128)} %param.18) | copy-start | bytes 1540
  0.7 4.9 %copy-start.13 = (s32[128]{0:T(128)S(1)}, s32[128]{0:T(128)}, u32[]{:S(2)}) copy-start(s32[128]{0:T(128)} %param.19) | copy-start | bytes 1540
  1.9 12.8 %collective-permute-start.1 = (bf16[1408,128]{1,0:T(8,128)(2,1)S(1)}, bf16[1408,128]{1,0:T(8,128)(2,1)S(1)}, u32[]{:S(2)}, u32[]{:S(2)}) collective-permute-start(bf16[1408,128]{1,0:T(8,128)(2,1)S(1)} %get-tuple-element.59), channel_id=1, source_target_pairs={{0,1},{1,0},{2,3},{3,2},{4,5},{5,4},{6,7},{7,6},{8,9},{9,8},{10,11... | collective-permute-start | bytes 1081352 | tf_op jit(solution)/shard_map/ppermute | solution.py:910
  4.9 5.1 %collective-permute-start = (bf16[384,128]{1,0:T(8,128)(2,1)S(1)}, bf16[384,128]{1,0:T(8,128)(2,1)S(1)}, u32[]{:S(2)}, u32[]{:S(2)}) collective-permute-start(bf16[384,128]{1,0:T(8,128)(2,1)S(1)} %get-tuple-element.45), channel_id=1, source_target_pairs={{1,2},{3,4},{5,6},{7,8},{9,10},{11,12},{13,14},{15,16},{17,18},{19... | collective-permute-start | bytes 294920 | tf_op jit(solution)/shard_map/ppermute | solution.py:912
  5.7 9.0 %copy-start.4 = (bf16[256,1024]{1,0:T(8,128)(2,1)S(1)}, bf16[256,1024]{1,0:T(8,128)(2,1)}, u32[]{:S(2)}) copy-start(bf16[256,1024]{1,0:T(8,128)(2,1)} %up_ref.1) | copy-start | bytes 1572868
  5.7 9.0 %copy-start.5 = (bf16[128,256]{1,0:T(8,128)(2,1)S(1)}, bf16[128,256]{1,0:T(8,128)(2,1)}, u32[]{:S(2)}) copy-start(bf16[128,256]{1,0:T(8,128)(2,1)} %out_ref.3) | copy-start | bytes 196612
  5.7 9.0 %copy-start.6 = (f32[1024]{0:T(1024)S(1)}, f32[1024]{0:T(1024)}, u32[]{:S(2)}) copy-start(f32[1024]{0:T(1024)} %param.29) | copy-start | bytes 12292
  5.7 9.0 %copy-start.9 = (f32[256]{0:T(256)S(1)}, f32[256]{0:T(256)}, u32[]{:S(2)}) copy-start(f32[256]{0:T(256)} %param.26) | copy-start | bytes 3076
  5.7 9.0 %copy-start.10 = (f32[256]{0:T(256)S(1)}, f32[256]{0:T(256)}, u32[]{:S(2)}) copy-start(f32[256]{0:T(256)} %param.27) | copy-start | bytes 3076
  5.7 9.0 %copy-start.11 = (f32[256]{0:T(256)S(1)}, f32[256]{0:T(256)}, u32[]{:S(2)}) copy-start(f32[256]{0:T(256)} %param.31) | copy-start | bytes 3076
  43.8 2.6 %collective-permute-start.2 = (bf16[3200,128]{1,0:T(8,128)(2,1)}, bf16[3200,128]{1,0:T(8,128)(2,1)S(1)}, u32[]{:S(2)}, u32[]{:S(2)}) collective-permute-start(bf16[3200,128]{1,0:T(8,128)(2,1)} %get-tuple-element.63), channel_id=1, source_target_pairs={{0,2},{1,3},{2,0},{3,1},{4,6},{5,7},{6,4},{7,5},{8,10},{9,11},{10,... | collective-permute-start | bytes 2457608 | tf_op jit(solution)/shard_map/ppermute | solution.py:843
  46.7 6.3 %collective-permute-start.3 = (bf16[800,128]{1,0:T(8,128)(2,1)S(1)}, bf16[800,128]{1,0:T(8,128)(2,1)S(1)}, u32[]{:S(2)}, u32[]{:S(2)}) collective-permute-start(bf16[800,128]{1,0:T(8,128)(2,1)S(1)} %get-tuple-element.80), channel_id=1, source_target_pairs={{0,1},{1,0},{2,10},{3,11},{4,5},{5,4},{6,14},{7,15},{8,9},{9,8},{1... | collective-permute-start | bytes 614408 | tf_op jit(solution)/shard_map/ppermute | solution.py:843
  49.3 5.8 %collective-permute-start.4 = (bf16[800,128]{1,0:T(8,128)(2,1)S(1)}, bf16[800,128]{1,0:T(8,128)(2,1)S(1)}, u32[]{:S(2)}, u32[]{:S(2)}) collective-permute-start(bf16[800,128]{1,0:T(8,128)(2,1)S(1)} %get-tuple-element.82), channel_id=1, source_target_pairs={{0,4},{1,5},{2,18},{3,19},{4,0},{5,1},{6,22},{7,23},{8,12},{9,13},... | collective-permute-start | bytes 614408 | tf_op jit(solution)/shard_map/ppermute | solution.py:843
  50.8 6.7 %collective-permute-start.5 = (bf16[800,128]{1,0:T(8,128)(2,1)S(1)}, bf16[800,128]{1,0:T(8,128)(2,1)S(1)}, u32[]{:S(2)}, u32[]{:S(2)}) collective-permute-start(bf16[800,128]{1,0:T(8,128)(2,1)S(1)} %get-tuple-element.81), channel_id=1, source_target_pairs={{0,5},{1,4},{2,26},{3,27},{4,1},{5,0},{6,30},{7,31},{8,13},{9,12},... | collective-permute-start | bytes 614408 | tf_op jit(solution)/shard_map/ppermute | solution.py:843
  57.7 5.8 %collective-permute-start.6 = (bf16[800,128]{1,0:T(8,128)(2,1)S(1)}, bf16[800,128]{1,0:T(8,128)(2,1)S(1)}, u32[]{:S(2)}, u32[]{:S(2)}) collective-permute-start(bf16[800,128]{1,0:T(8,128)(2,1)S(1)} %get-tuple-element.79), channel_id=1, source_target_pairs={{0,8},{1,9},{2,3},{3,2},{4,12},{5,13},{6,7},{7,6},{8,0},{9,1},{10,... | collective-permute-start | bytes 614408 | tf_op jit(solution)/shard_map/ppermute | solution.py:843
  59.3 11.0 %collective-permute-start.7 = (bf16[800,128]{1,0:T(8,128)(2,1)S(1)}, bf16[800,128]{1,0:T(8,128)(2,1)S(1)}, u32[]{:S(2)}, u32[]{:S(2)}) collective-permute-start(bf16[800,128]{1,0:T(8,128)(2,1)S(1)} %get-tuple-element.79), channel_id=1, source_target_pairs={{0,16},{1,17},{2,6},{3,7},{4,20},{5,21},{6,2},{7,3},{8,24},{9,25},... | collective-permute-start | bytes 614408 | tf_op jit(solution)/shard_map/ppermute | solution.py:843
  61.2 9.2 %collective-permute-start.8 = (bf16[800,128]{1,0:T(8,128)(2,1)S(1)}, bf16[800,128]{1,0:T(8,128)(2,1)S(1)}, u32[]{:S(2)}, u32[]{:S(2)}) collective-permute-start(bf16[800,128]{1,0:T(8,128)(2,1)S(1)} %get-tuple-element.79), channel_id=1, source_target_pairs={{0,24},{1,25},{2,7},{3,6},{4,28},{5,29},{6,3},{7,2},{8,16},{9,17},... | collective-permute-start | bytes 614408 | tf_op jit(solution)/shard_map/ppermute | solution.py:843
  70.7 5.8 %collective-permute-start.9 = (bf16[800,128]{1,0:T(8,128)(2,1)S(1)}, bf16[800,128]{1,0:T(8,128)(2,1)S(1)}, u32[]{:S(2)}, u32[]{:S(2)}) collective-permute-start(bf16[800,128]{1,0:T(8,128)(2,1)S(1)} %bitcast.49), channel_id=1, source_target_pairs={{0,1},{1,0},{2,10},{3,11},{4,5},{5,4},{6,14},{7,15},{8,9},{9,8},{1... | collective-permute-start | bytes 614408 | tf_op jit(solution)/shard_map/ppermute | solution.py:843
  72.1 5.8 %collective-permute-start.10 = (bf16[800,128]{1,0:T(8,128)(2,1)S(1)}, bf16[800,128]{1,0:T(8,128)(2,1)S(1)}, u32[]{:S(2)}, u32[]{:S(2)}) collective-permute-start(bf16[800,128]{1,0:T(8,128)(2,1)S(1)} %bitcast.50), channel_id=1, source_target_pairs={{0,4},{1,5},{2,18},{3,19},{4,0},{5,1},{6,22},{7,23},{8,12},{9,13},... | collective-permute-start | bytes 614408 | tf_op jit(solution)/shard_map/ppermute | solution.py:843
  73.5 6.7 %collective-permute-start.11 = (bf16[800,128]{1,0:T(8,128)(2,1)S(1)}, bf16[800,128]{1,0:T(8,128)(2,1)S(1)}, u32[]{:S(2)}, u32[]{:S(2)}) collective-permute-start(bf16[800,128]{1,0:T(8,128)(2,1)S(1)} %bitcast.51), channel_id=1, source_target_pairs={{0,5},{1,4},{2,26},{3,27},{4,1},{5,0},{6,30},{7,31},{8,13},{9,12},... | collective-permute-start | bytes 614408 | tf_op jit(solution)/shard_map/ppermute | solution.py:843
  80.2 2.4 %collective-permute-start.12 = (bf16[3200,128]{1,0:T(8,128)(2,1)S(1)}, bf16[3200,128]{1,0:T(8,128)(2,1)S(1)}, u32[]{:S(2)}, u32[]{:S(2)}) collective-permute-start(bf16[3200,128]{1,0:T(8,128)(2,1)S(1)} %bitcast.35), channel_id=1, source_target_pairs={{0,2},{1,3},{2,0},{3,1},{4,6},{5,7},{6,4},{7,5},{8,10},{9,11},{10,... | collective-permute-start | bytes 2457608 | tf_op jit(solution)/shard_map/ppermute | solution.py:843

commit v3 on v2

--- a/solution.py
+++ b/solution.py
@@ -146,8 +146,7 @@
     query_ref,
     key_ref,
     value_ref,
-    xhat,
-    inv,
+    normed,
     qbuf,
     kbuf,
     vbuf,
@@ -155,15 +154,17 @@
     att,
     low_mark,
     fill_mark,
-    normed_t,
+    xhat_t,
     cot_t,
     cot_ref,
     down_ref,
+    cot_sum,
     weight,
     in_sem,
 ):
-    own = rows * WINDOW
+    D = x_ref.shape[1]
     step = CHUNK * WINDOW
+    xhat_t[D:, :] = jnp.ones((16, rows * WINDOW), BF16)
     place = lax.axis_index("seq") * lax.axis_size("head") + lax.axis_index("head")
     for part, ref in enumerate((query_ref, key_ref, value_ref)):
         weight[:, part * HEAD_DIM : (part + 1) * HEAD_DIM] = ref[...]
@@ -194,11 +195,10 @@
 
     for i in range(rows // CHUNK):
         here = slice(i * step, (i + 1) * step)
-        scaled, inverse = standardize(x_ref[here, :].astype(F32))
-        xhat[here, :] = scaled
-        inv[here, :] = inverse
+        scaled, _ = standardize(x_ref[here, :].astype(F32))
+        xhat_t[:D, here] = scaled.astype(BF16).T
         value = (scaled * gain1_ref[...] + shift1_ref[...]).astype(BF16)
-        normed_t[:, here] = value.T
+        normed[here, :] = value
         made = dot(value, weight[...]).astype(BF16)
         for part, buf in enumerate((qbuf, kbuf, vbuf)):
             buf[here, :] = made[:, part * HEAD_DIM : (part + 1) * HEAD_DIM]
@@ -227,6 +227,10 @@
         copy.wait()
     cot_t[...] = cot_ref[...].T
     down_ref[...] = (down_ref[...].astype(F32) * 0.5).astype(BF16)
+    total = jnp.zeros((8, D), F32)
+    for i in range(rows // CHUNK):
+        total += jnp.sum(cot_ref[i * step : (i + 1) * step, :].astype(F32).reshape(step // 8, 8, D), axis=0)
+    cot_sum[...] = total
 
 
 def in_vmem(array):
@@ -245,8 +249,7 @@
     return pl.pallas_call(
         functools.partial(local_kernel, rows),
         out_shape=(
-            pltpu.VMEM((own, D), F32),
-            pltpu.VMEM((own, 1), F32),
+            pltpu.VMEM((own, D), BF16),
             pltpu.VMEM((own, HEAD_DIM), BF16),
             pltpu.VMEM((own, HEAD_DIM), BF16),
             pltpu.VMEM((own, HEAD_DIM), BF16),
@@ -254,10 +257,11 @@
             pltpu.VMEM((own, HEAD_DIM), BF16),
             pltpu.VMEM((mark_rows, 128), jnp.int32),
             pltpu.VMEM((mark_rows, 128), jnp.int32),
-            pltpu.VMEM((D, own), BF16),
+            pltpu.VMEM((D + 16, own), BF16),
             pltpu.VMEM((D, own), BF16),
             pltpu.VMEM((own, D), BF16),
             pltpu.VMEM(down.shape, BF16),
+            pltpu.VMEM((8, D), F32),
         ),
         in_specs=[vmem] + [pl.BlockSpec(memory_space=pltpu.HBM)] * 2 + [vmem] * 7,
         out_specs=(vmem,) * 13,
@@ -275,8 +279,7 @@
 def layer_kernel(
     rows,
     rim_ref,
-    xhat,
-    inv,
+    normed,
     own_q,
     own_k,
     own_v,
@@ -284,10 +287,11 @@
     own_att,
     low_mark,
     fill_mark,
-    normed_t,
+    xhat_t,
     cot_t,
     cot_ref,
     down_ref,
+    cot_sum,
     x_ref,
     up_ref,
     gain1_ref,
@@ -300,17 +304,25 @@
     gain2_ref,
     shift2_ref,
     up_bias_ref,
-    down_bias_ref,
-    mixed_ref,
-    in_grad_ref,
     keep_ref,
     send_ref,
+    act_out,
+    att_out,
+    mid_grad_out,
+    dqkv_out,
+    wqkv_out,
+    wout_out,
+    act,
+    att,
+    mid_grad,
+    dqkv,
+    wqkv,
+    wout,
     rim_x,
     rim_cot,
     halo_grad,
-    wqkv,
+    halo_att,
     wother,
-    wout,
     rim_q,
     rim_k,
     rim_v,
@@ -318,14 +330,8 @@
     kbuf,
     vbuf,
     gbuf,
-    att,
     probs,
-    mid_grad,
-    dqkv,
-    act,
     hid_grad,
-    mixed_buf,
-    in_grad_buf,
     acc_down,
     acc_up,
     acc_qkv,
@@ -341,7 +347,11 @@
     place = lax.axis_index("seq") * lax.axis_size("head") + head
     step = CHUNK * WINDOW
     steps = rows // CHUNK
-    sent = {}
+    leaving = {}
+
+    def leave(kind, n, source, target):
+        leaving[kind, n] = pltpu.make_async_copy(source, target, out_sem.at[kind, n])
+        leaving[kind, n].start()
 
     for part, ref in enumerate((query_ref, key_ref, value_ref)):
         wqkv[:, part * D : part * D + HEAD_DIM] = ref[...]
@@ -352,6 +362,8 @@
         wout[HEAD_DIM:, half * HEAD_DIM : (half + 1) * HEAD_DIM] = heads_ref[
             3 * D + half * HEAD_DIM : 3 * D + (half + 1) * HEAD_DIM, :
         ]
+    leave(4, 0, wqkv, wqkv_out)
+    leave(4, 1, wout, wout_out)
     acc_vec[...] = jnp.zeros_like(acc_vec)
 
     for half in range(D // HEAD_DIM):
@@ -362,7 +374,7 @@
         rim_x[WINDOW:, cols] = jnp.where(head == 0, near[:WINDOW], far[:WINDOW])
         rim_cot[:, cols] = jnp.where(head == 0, near[WINDOW:], far[WINDOW:])
 
-    att[WINDOW:own, :HEAD_DIM] = own_att[WINDOW:, :]
+    att[WINDOW:, :HEAD_DIM] = own_att[WINDOW:, :]
     queries = (own_q, rim_q, qbuf)
     keys = (own_k, rim_k, kbuf)
     values = (own_v, rim_v, vbuf)
@@ -379,8 +391,7 @@
 
     def project(i):
         here = slice(WINDOW + i * step, WINDOW + (i + 1) * step)
-        value = xhat[i * step : (i + 1) * step, :] * gain1_ref[...] + shift1_ref[...]
-        made = dot(value.astype(BF16), wother[...]).astype(BF16)
+        made = dot(normed[i * step : (i + 1) * step, :], wother[...]).astype(BF16)
         for part, (_, _, other) in enumerate((queries, keys, values)):
             other[here, :] = made[:, part * HEAD_DIM : (part + 1) * HEAD_DIM]
 
@@ -430,9 +441,11 @@
 
     def gather(j, h):
         r = j - 1
-        att[r * WINDOW : (r + 1) * WINDOW, columns[h]] = window_sum(
-            held.pop((j, h)), pair(values, j, h), current_t
-        ).astype(BF16)
+        made = window_sum(held.pop((j, h)), pair(values, j, h), current_t).astype(BF16)
+        if r < rows:
+            att[r * WINDOW : (r + 1) * WINDOW, columns[h]] = made
+        else:
+            halo_att[:, columns[h]] = made
 
     def feed_forward(first, count, own_rows):
         at = first * WINDOW
@@ -442,22 +455,26 @@
         block = 256
         slot = at // step % 2
         grads = hid_grad.at[slot] if own_rows else halo_grad
-        xs, cots = (x_ref, cot_ref) if own_rows else (rim_x.at[pl.ds(WINDOW, WINDOW)], rim_cot)
+        xs, cots, atts = (x_ref, cot_ref, att) if own_rows else (rim_x.at[pl.ds(WINDOW, WINDOW)], rim_cot, halo_att)
         there = here if own_rows else slice(0, size)
 
         def enter():
-            attended = att[here, :]
+            if own_rows:
+                if at >= 2 * step:
+                    leaving[0, at // step - 2].wait()
+                    leaving[2, at // step - 2].wait()
+                leave(1, at // step, att.at[pl.ds(at, size)], att_out.at[pl.ds(at, size)])
+            attended = atts[there, :]
             middle = xs[there, :].astype(F32) + split_dot(attended, wout[...])
             scaled, inverse = standardize(middle)
-            held.update(middle=middle, scaled=scaled, inverse=inverse)
+            held.update(scaled=scaled, inverse=inverse)
             held["normed"] = (scaled * gain2_ref[...] + shift2_ref[...]).astype(BF16)
 
         def hide(f):
             cols = slice(f * block, (f + 1) * block)
-            cot = cots[there, :]
             hidden = dot(held["normed"], up_ref[:, cols]) + up_bias_ref[:, cols]
             active, slope = twice_gelu(hidden)
-            grad = dot_lanes(cot, down_ref[cols, :]) * slope
+            grad = dot_lanes(cots[there, :], down_ref[cols, :]) * slope
             grads[:size, cols] = grad.astype(BF16)
             if own_rows:
                 act[slot, :size, cols] = active.astype(BF16)
@@ -474,30 +491,20 @@
                 acc_down[:, cols] = down_part
                 acc_up[:, cols] = up_part
 
-        def mix():
-            if at >= 2 * step:
-                sent["mixed", at // step - 2].wait()
-            mixed_buf[slot, :, :] = (
-                held["middle"] + split_dot(act[slot, :size], down_ref[...]) + down_bias_ref[...]
-            ).astype(BF16)
-            copy = pltpu.make_async_copy(
-                mixed_buf.at[slot], mixed_ref.at[pl.ds(at, size)], out_sem.at[0, at // size]
-            )
-            copy.start()
-            sent["mixed", at // step] = copy
-
         def back():
+            if own_rows:
+                leave(0, at // step, act.at[slot], act_out.at[pl.ds(at, size)])
             scaled = held["scaled"]
             g2 = split_dot(grads[:size, :], up_ref[...], dot_lanes)
             cot32 = cots[there, :].astype(F32)
             middle_grad = cot32 + normalize_back(g2 * gain2_ref[...], scaled, held["inverse"])
             mixing_grad = middle_grad.astype(BF16)
             if own_rows:
-                mid_grad[here, :] = middle_grad
+                mid_grad[slot, :, :] = middle_grad
+                leave(2, at // step, mid_grad.at[slot], mid_grad_out.at[pl.ds(at, size)])
                 acc_vec[2:3, :D] += column_sums(g2 * scaled)
                 acc_vec[3:4, :D] += column_sums(g2)
-                acc_vec[4:5, :D] += column_sums(cot32)
-                out_part = dot_rows(att[here, :], mixing_grad)
+                out_part = dot_rows(atts[there, :], mixing_grad)
                 if at:
                     acc_out[...] += out_part
                 else:
@@ -511,7 +518,7 @@
         parts = FF // block
         hides = [call(hide, f) for f in range(parts)]
         weighs = [call(weigh, f) for f in range(parts)] if own_rows else []
-        return enter, hides, weighs, mix, back
+        return enter, hides, weighs, back
 
     held_back = {}
     unfinished = {}
@@ -545,32 +552,9 @@
 
     def project_back(i):
         at = i * step
-        here = slice(at, at + step)
-        found = {}
-
-        def multiply():
-            grads = dqkv[here, :]
-            part = dot(normed_t[:, here], grads)
-            acc_qkv[...] = (acc_qkv[...] + part) if at else part
-            found["g1"] = split_dot(grads, wqkv[...], dot_lanes)
-
-        def back():
-            g1 = found["g1"]
-            scaled = xhat[here, :]
-            acc_vec[0:1, :D] += column_sums(g1 * scaled)
-            acc_vec[1:2, :D] += column_sums(g1)
-            if i > 1:
-                sent["grad", i - 2].wait()
-            in_grad_buf[i % 2, :, :] = (
-                mid_grad[here, :] + normalize_back(g1 * gain1_ref[...], scaled, inv[here, :])
-            ).astype(BF16)
-            copy = pltpu.make_async_copy(
-                in_grad_buf.at[i % 2], in_grad_ref.at[pl.ds(at, step)], out_sem.at[1, i]
-            )
-            copy.start()
-            sent["grad", i] = copy
-
-        return multiply, back
+        leave(3, i, dqkv.at[pl.ds(at, step)], dqkv_out.at[pl.ds(at, step)])
+        made = dot(xhat_t[:, at : at + step], dqkv[at : at + step, :])
+        acc_qkv[...] = (acc_qkv[...] + made) if at else made
 
     def units(first, last):
         return [(j, h) for j in range(first, last + 1) for h in range(HEADS)]
@@ -582,21 +566,21 @@
     forward = [(j, h) for j, h in units(1, rows + 1) if h or not 1 < j <= rows]
     do(staggered(forward, score, soften, gather))
     feeds = [feed_forward(i * CHUNK, CHUNK, True) for i in range(steps)]
-    halo_enter, halo_hides, _, _, halo_back = feed_forward(rows, 1, False)
+    halo_enter, halo_hides, _, halo_back = feed_forward(rows, 1, False)
     halo = [halo_enter] + halo_hides + [halo_back]
-    enter, hides, weighs, mix, back = feeds[0]
+    enter, hides, weighs, back = feeds[0]
     do([enter, halo.pop(0), hides[0], hides[1], weighs[0]])
     for i in range(steps):
-        enter, hides, weighs, mix, back = feeds[i]
+        enter, hides, weighs, back = feeds[i]
         for f in range(2, len(hides)):
             do([hides[f], weighs[f - 1]] + halo[:1])
             halo = halo[1:]
         if i + 1 < steps:
             later = feeds[i + 1]
-            do([later[0], weighs[-1], later[1][0], mix, later[1][1], back, later[2][0]] + halo[:1])
+            do([later[0], weighs[-1], later[1][0], back, later[1][1], later[2][0]] + halo[:1])
             halo = halo[1:]
         else:
-            do([weighs[-1]] + halo + [mix, back])
+            do([weighs[-1]] + halo + [back])
 
     core = (place & 2) // 2
     wide = FF // 2
@@ -635,21 +619,33 @@
     exports = [call(export_down, c, ref, f) for c, ref in halves for f in range(0, wide, D)]
     exports += [call(export_up, c, ref, n) for c, ref in halves for n in range(wide // HEAD_DIM)]
     exports += [call(export_heads, c, ref, h, 3) for c, ref in halves for h in range(HEADS)]
-    ends = [project_back(i) for i in range(steps)]
     backs = staggered(units(1, rows + 1), weigh_grads, soften_back, gather_back)
     marks = []
     for i in range(steps):
         done = [n for n, job in enumerate(backs) if job.func is gather_back and job.args == ((i + 1) * CHUNK + 1, 1)]
         marks.append(done[0] + 1)
-    exports = merge(exports, list(range(0)))
-    share = -(-len(exports) // marks[0])
     do(merge(backs[: marks[0]], exports))
     for i in range(1, steps):
-        ends[i - 1][0]()
-        do(merge(backs[marks[i - 1] : marks[i]], [ends[i - 1][1]]))
+        project_back(i - 1)
+        do(backs[marks[i - 1] : marks[i]])
     do(backs[marks[-1] :])
-    ends[-1][0]()
-    ends[-1][1]()
+    project_back(steps - 1)
+
+    gain_t = jnp.broadcast_to(gain1_ref[...], (HEAD_DIM, D)).T
+    shift_t = jnp.broadcast_to(shift1_ref[...], (HEAD_DIM, D)).T
+    gain_sum = jnp.zeros((D, HEAD_DIM), F32)
+    shift_sum = jnp.zeros((D, HEAD_DIM), F32)
+    for n in range(3 * D // HEAD_DIM):
+        cols = slice(n * HEAD_DIM, (n + 1) * HEAD_DIM)
+        product = acc_qkv[:D, cols]
+        total = acc_qkv[D : D + 1, cols]
+        weight = wqkv[:, cols].astype(F32)
+        gain_sum += weight * product
+        shift_sum += weight * total
+        acc_qkv[:D, cols] = gain_t * product + shift_t * total
+    acc_vec[0:1, :D] = column_sums(gain_sum.T)
+    acc_vec[1:2, :D] = column_sums(shift_sum.T)
+    acc_vec[4:5, :D] = column_sums(cot_sum[...])
 
     for c, ref in halves:
         do([call(export_heads, c, ref, h, part) for h in range(HEADS) for part in range(3)])
@@ -657,14 +653,12 @@
         vec_rows[n : n + 1, :] = acc_vec[row : row + 1, cols]
     for c, ref in halves:
         export_vectors(c, ref)
-    for kind in ("mixed", "grad"):
-        for i in range(max(steps - 2, 0), steps):
-            sent[kind, i].wait()
-
-
-def layer(
-    rim, made, tokens, up, gain1, shift1, weights, other, gain2, shift2, up_bias, down_bias
-):
+    for (kind, n), copy in leaving.items():
+        if kind not in (0, 2) or n >= steps - 2:
+            copy.wait()
+
+
+def layer(rim, made, tokens, up, gain1, shift1, weights, other, gain2, shift2, up_bias):
     own, D = tokens.shape
     FF = up.shape[1]
     rows = own // WINDOW
@@ -673,25 +667,32 @@
     tokens, up, rim, other = in_vmem(tokens), in_vmem(up), in_vmem(rim), in_vmem(other)
     made = [in_vmem(array) for array in made]
     vmem = pl.BlockSpec(memory_space=pltpu.VMEM)
-    anywhere = pl.BlockSpec(memory_space=pl.ANY)
-    steps = rows // CHUNK
     return pl.pallas_call(
         functools.partial(layer_kernel, rows),
         out_shape=(
-            jax.ShapeDtypeStruct((own, D), BF16),
-            jax.ShapeDtypeStruct((own, D), BF16),
             pltpu.VMEM((half, HEAD_DIM), BF16),
             pltpu.VMEM((half, HEAD_DIM), BF16),
+            pltpu.HBM((own, FF), BF16),
+            pltpu.HBM((own, D), BF16),
+            pltpu.HBM((own, D), F32),
+            pltpu.HBM((own, 3 * D), BF16),
+            pltpu.HBM((D, 3 * D), BF16),
+            pltpu.HBM((D, D), BF16),
         ),
-        in_specs=[vmem] * 27,
-        out_specs=(anywhere, anywhere, vmem, vmem),
+        in_specs=[vmem] * (1 + len(made) + 2 + 2 + 4 + 1 + 3),
+        out_specs=(vmem, vmem) + (pl.BlockSpec(memory_space=pltpu.HBM),) * 6,
         scratch_shapes=[
+            pltpu.VMEM((2, CHUNK * WINDOW, FF), BF16),
+            pltpu.VMEM((own, D), BF16),
+            pltpu.VMEM((2, CHUNK * WINDOW, D), F32),
+            pltpu.VMEM((own, 3 * D), BF16),
+            pltpu.VMEM((D, 3 * D), BF16),
+            pltpu.VMEM((D, D), BF16),
             pltpu.VMEM((2 * WINDOW, D), BF16),
             pltpu.VMEM((WINDOW, D), BF16),
             pltpu.VMEM((WINDOW, FF), BF16),
-            pltpu.VMEM((D, 3 * D), BF16),
+            pltpu.VMEM((WINDOW, D), BF16),
             pltpu.VMEM((D, 3 * HEAD_DIM), BF16),
-            pltpu.VMEM((D, D), BF16),
             pltpu.VMEM((2 * WINDOW, HEAD_DIM), BF16),
             pltpu.VMEM((2 * WINDOW, HEAD_DIM), BF16),
             pltpu.VMEM((2 * WINDOW, HEAD_DIM), BF16),
@@ -699,27 +700,91 @@
             pltpu.VMEM((count, HEAD_DIM), BF16),
             pltpu.VMEM((count, HEAD_DIM), BF16),
             pltpu.VMEM((count, D), BF16),
-            pltpu.VMEM((count - WINDOW, D), BF16),
             pltpu.VMEM((rows + 3, WINDOW, WINDOW), F32),
-            pltpu.VMEM((own, D), F32),
-            pltpu.VMEM((own, 3 * D), BF16),
             pltpu.VMEM((2, CHUNK * WINDOW, FF), BF16),
-            pltpu.VMEM((2, CHUNK * WINDOW, FF), BF16),
-            pltpu.VMEM((2, CHUNK * WINDOW, D), BF16),
-            pltpu.VMEM((2, CHUNK * WINDOW, D), BF16),
             pltpu.VMEM((D, FF), F32),
             pltpu.VMEM((D, FF), F32),
-            pltpu.VMEM((D, 3 * D), F32),
+            pltpu.VMEM((D + 16, 3 * D), F32),
             pltpu.VMEM((D, D), F32),
             pltpu.VMEM((16, FF), F32),
             pltpu.VMEM((32, HEAD_DIM), F32),
-            pltpu.SemaphoreType.DMA((2, steps)),
+            pltpu.SemaphoreType.DMA((5, max(rows // CHUNK, 2))),
         ],
         compiler_params=pltpu.CompilerParams(vmem_limit_bytes=34 * 1024 * 1024),
         name="layer",
-    )(
-        rim, *made, tokens, up, gain1, shift1, *weights, other, gain2, shift2, up_bias, down_bias
-    )
+    )(rim, *made, tokens, up, gain1, shift1, *weights, other, gain2, shift2, up_bias)
+
+
+def token_chunks(streams, out_ref, buf, in_sem, out_sem, fixed, work):
+    step = CHUNK * WINDOW
+    arriving = [pltpu.make_async_copy(a, b, in_sem.at[0, n]) for n, (a, b) in enumerate(fixed)]
+    steps = buf.shape[0] // step
+    chunks = []
+    for i in range(steps):
+        here = pl.ds(i * step, step)
+        chunks.append(
+            [pltpu.make_async_copy(a.at[here], b.at[here], in_sem.at[i + 1, n]) for n, (a, b) in enumerate(streams)]
+        )
+    for copy in arriving + [copy for chunk in chunks for copy in chunk]:
+        copy.start()
+    for copy in arriving:
+        copy.wait()
+    leaving = []
+    for i in range(steps):
+        for copy in chunks[i]:
+            copy.wait()
+        work(slice(i * step, (i + 1) * step))
+        here = pl.ds(i * step, step)
+        leaving.append(pltpu.make_async_copy(buf.at[here], out_ref.at[here], out_sem.at[i]))
+        leaving[-1].start()
+    for copy in leaving:
+        copy.wait()
+
+
+def input_grad_kernel(
+    x_in, mid_in, dqkv_in, wqkv_in, gain1_ref, out_ref, buf, in_sem, out_sem, x_ref, mid_grad, dqkv, wqkv
+):
+    def work(here):
+        scaled, inverse = standardize(x_ref[here, :].astype(F32))
+        g1 = split_dot(dqkv[here, :], wqkv[...], dot_lanes)
+        buf[here, :] = (
+            mid_grad[here, :] + normalize_back(g1 * gain1_ref[...], scaled, inverse)
+        ).astype(BF16)
+
+    streams = ((x_in, x_ref), (mid_in, mid_grad), (dqkv_in, dqkv))
+    token_chunks(streams, out_ref, buf, in_sem, out_sem, ((wqkv_in, wqkv),), work)
+
+
+def mixed_kernel(
+    x_in, att_in, act_in, wout_in, down_in, down_bias_ref, out_ref, buf, in_sem, out_sem, x_ref, att, act, wout, down
+):
+    def work(here):
+        middle = x_ref[here, :].astype(F32) + split_dot(att[here, :], wout[...])
+        mixed = middle + split_dot(act[here, :], down[...]) * 0.5 + down_bias_ref[...]
+        buf[here, :] = mixed.astype(BF16)
+
+    streams = ((x_in, x_ref), (att_in, att), (act_in, act))
+    token_chunks(streams, out_ref, buf, in_sem, out_sem, ((wout_in, wout), (down_in, down)), work)
+
+
+def late(kernel, name, arrays, small):
+    own, D = arrays[0].shape
+    steps = own // (CHUNK * WINDOW)
+    hbm = pl.BlockSpec(memory_space=pltpu.HBM)
+    return pl.pallas_call(
+        kernel,
+        out_shape=pltpu.HBM((own, D), BF16),
+        in_specs=[hbm] * len(arrays) + [pl.BlockSpec(memory_space=pltpu.VMEM)],
+        out_specs=hbm,
+        scratch_shapes=[
+            pltpu.VMEM((own, D), BF16),
+            pltpu.SemaphoreType.DMA((steps + 1, 3)),
+            pltpu.SemaphoreType.DMA((steps,)),
+        ]
+        + [pltpu.VMEM(array.shape, array.dtype) for array in arrays],
+        compiler_params=pltpu.CompilerParams(vmem_limit_bytes=32 * 1024 * 1024),
+        name=name,
+    )(*[in_hbm(array) for array in arrays], small)
 
 
 def pack_kernel(query_ref, key_ref, value_ref, out_ref, tok_ref, cot_ref, near_ref, far_ref, sem):
@@ -843,42 +908,50 @@
     return lax.ppermute(value, BOTH, [(i, i ^ hops[i // 2 % 2]) for i in range(count)])
 
 
-def all_sum(value):
+def all_sum(value, side):
     count = lax.axis_size("seq") * lax.axis_size("head")
     place = lax.axis_index("seq") * lax.axis_size("head") + lax.axis_index("head")
     width = value.shape[1]
+    made = []
     steps = []
     for masks in stages(count):
         code, other_code = (
-            sum(((place & mask) // mask) << j for j, mask in enumerate(side)) for side in masks
+            sum(((place & mask) // mask) << j for j, mask in enumerate(bits)) for bits in masks
         )
         steps.append((masks, jnp.where(place & 2 == 0, code, other_code)))
-    def spread(value, masks, code):
-        parts = 1 << len(masks[0])
-        found = [value] + [partners(value, masks, k) for k in range(1, parts)]
-        whole = jnp.zeros((parts,) + value.shape, value.dtype)
+
+    def exchange(value, send, masks, number):
+        if number >= len(side):
+            return [partners(send(value, k), masks, k) for k in range(1, 1 << len(masks[0]))]
+        work, small = side[number]
+        value, small = lax.optimization_barrier((value, small))
+        arrived = [partners(send(value, k), masks, k) for k in range(1, 1 << len(masks[0]))]
+        arrived, done = lax.optimization_barrier((arrived, work(small)))
+        made.append(done)
+        return arrived
+
+    def spread(value, masks, code, number):
+        found = [value] + exchange(value, lambda v, k: v, masks, number)
+        whole = jnp.zeros((len(found),) + value.shape, value.dtype)
         for k, part in enumerate(found):
             whole = lax.dynamic_update_index_in_dim(whole, part, code ^ k, 0)
         return whole
 
-    for masks, code in steps[:-1]:
+    for number, (masks, code) in enumerate(steps[:-1]):
         parts = value.reshape(1 << len(masks[0]), -1, width)
         total = lax.dynamic_index_in_dim(parts, code, 0, False).astype(F32)
-        arrived = [
-            partners(lax.dynamic_index_in_dim(parts, code ^ k, 0, False), masks, k)
-            for k in range(1, parts.shape[0])
-        ]
-        for part in arrived:
+        pick = lambda parts, k, code=code: lax.dynamic_index_in_dim(parts, code ^ k, 0, False)
+        for part in exchange(parts, pick, masks, number):
             total = total + part.astype(F32)
         value = total.astype(BF16)
-    whole = spread(value, *steps[-1])
+    whole = spread(value, *steps[-1], len(steps) - 1)
     total = whole[0].astype(F32)
     for part in whole[1:]:
         total = total + part.astype(F32)
     value = total.astype(BF16)
     for masks, code in steps[-2::-1]:
-        value = spread(value, masks, code).reshape(-1, width)
-    return value
+        value = spread(value, masks, code, len(side)).reshape(-1, width)
+    return value, made
 
 
 def across_cores(value):
@@ -913,7 +986,7 @@
     weights = (query_weight, key_weight, value_weight, out_weight)
     gain1, shift1 = first_gain[None], first_shift[None]
     made = local(tokens, cotangent, down_weight, image_rows[None], image_fill[None], gain1, shift1, weights)
-    mixed, input_grad, keep, send = layer(
+    keep, send, act, att, mid_grad, dqkv, wqkv, wout = layer(
         rim,
         made,
         tokens,
@@ -925,10 +998,13 @@
         second_gain[None],
         second_shift[None],
         up_bias[None],
-        down_bias[None],
     )
+    side = [
+        (lambda small: late(input_grad_kernel, "input_grad", (tokens, mid_grad, dqkv, wqkv), small), gain1),
+        (lambda small: late(mixed_kernel, "mixed", (tokens, att, act, wout, down_weight), small), down_bias[None]),
+    ]
     summed = (keep.astype(F32) + across_cores(send).astype(F32)).astype(BF16)
-    mine = all_sum(summed)
+    mine, (input_grad, mixed) = all_sum(summed, side)
     return (mixed, input_grad, *finish(mine, across_cores(mine), FF, D))
 
 

time: 85.2 us -> 81.2 us (0.953)
  waiting for transfers between devices: 30 us -> 18.4 us
  Pallas kernels: 36.7 us -> 43.8 us
    ppermute x11, waiting for transfers between devices: 25.3 us -> 13.8 us  [partners(): lax.ppermute(value, BOTH, [(i, i ^ hops[i // 2 % 2]) for i in range(count)])]
    pallas_call x1 -> x3, Pallas kernels: 29.1 us -> 36.1 us  [the longest x1 24.7 us: layer(): pl.pallas_call(functools.partial(layer_kernel, rows), out_shape=(pltpu.VM...]
  transfers between devices with their start and end apart: 13 -> 13, of which waited for: 11 -> 8; matrix products, arithmetic and copies ran while one was open for 0% -> 0% of each run, Pallas kernels for 5% -> 19%
where the time goes in v3:
time: 81.2 us; the launch traced here: 80.7 us
  Pallas kernels  43.8 us (54%)
  waiting for transfers between devices  18.4 us (23%)
  starting transfers between devices  16.2 us (20%)
  between operations  1.22 us (2%)
    pallas_call x1, Pallas kernels, layer(): pl.pallas_call(functools.partial(layer_kernel, rows), out_shape=(pltpu.VM...  24.7 us
    ppermute x11, waiting for transfers between devices, partners(): lax.ppermute(value, BOTH, [(i, i ^ hops[i // 2 % 2]) for i in range(count)])  13.8 us
    ppermute x11, starting transfers between devices, partners(): lax.ppermute(value, BOTH, [(i, i ^ hops[i // 2 % 2]) for i in range(count)])  12.5 us
    pallas_call x2, Pallas kernels, late(): pl.pallas_call(kernel, out_shape=pltpu.HBM((own, D), BF16), in_specs=[hbm...  11.4 us
    ppermute x1, waiting for transfers between devices, shards(): other = lax.ppermute(near, 'head', [(0, 1), (1, 0)])  4.64 us
    pallas_call x1, Pallas kernels, local(): pl.pallas_call(functools.partial(local_kernel, rows), out_shape=(pltpu.VM...  4.32 us
    ppermute x1, starting transfers between devices, shards(): other = lax.ppermute(near, 'head', [(0, 1), (1, 0)])  3.03 us
    pallas_call x1, Pallas kernels, finish(): pl.pallas_call(functools.partial(finish_kernel, FF, D), out_shape=tuple((...  2.22 us
  transfers between devices with their start and end apart: 13, of which 8 were waited for; matrix products, arithmetic and copies ran while one was open for 0% of the time, Pallas kernels for 19%

profile of v3, /device:TPU:0, one launch (start us, length us, event | category | flops | bytes accessed | tf_op | source)
XLA Modules:
  0.0 80.7 jit_solution(10101371557390581991)
XLA Ops:
  0.7 1.2 %pack.1 = (bf16[1408,128]{1,0:T(8,128)(2,1)S(1)}, bf16[384,128]{1,0:T(8,128)(2,1)S(1)}) custom-call(bf16[256,128]{1,0:T(8,128)(2,1)} %query_ref.5, bf16[256,128]{1,0:T(8,128)(2,1)} %key_ref.5, bf16[256,128]{1,0:T(8,128)(2,1)} %value_ref.5, bf16[128,256]{1,0:T(8,128)(2,1)} %out_ref.3, bf16[3072,256]{1,0:T(8,128)(2,1)} %x_in.3, bf16[3072,256]{1,0:T(8,128)(2,1)} %cot_in_ref.1), custom_call_target="tpu_custom_call" | custom-call | tf_op jit(solution)/shard_map/pack/pallas_call | solution.py:819
  1.9 3.0 %collective-permute-start.1 = (bf16[1408,128]{1,0:T(8,128)(2,1)S(1)}, bf16[1408,128]{1,0:T(8,128)(2,1)S(1)}, u32[]{:S(2)}, u32[]{:S(2)}) collective-permute-start(bf16[1408,128]{1,0:T(8,128)(2,1)S(1)} %get-tuple-element.75), channel_id=1, source_target_pairs={{0,1},{1,0},{2,3},{3,2},{4,5},{5,4},{6,7},{7,6},{8,9},{9,8},{10,11... | collective-permute-start | bytes 1081352 | tf_op jit(solution)/shard_map/ppermute | solution.py:983
  4.9 0.7 collective-permute-start
  5.7 4.3 %local.1 = (bf16[3072,256]{1,0:T(8,128)(2,1)S(1)}, bf16[3072,128]{1,0:T(8,128)(2,1)S(1)}, bf16[3072,128]{1,0:T(8,128)(2,1)S(1)}, bf16[3072,128]{1,0:T(8,128)(2,1...) custom-call(bf16[3072,256]{1,0:T(8,128)(2,1)S(1)} %copy-done, ...), custom_call_target="tpu_custom_call" | custom-call | tf_op jit(solution)/shard_map/local/pallas_call | solution.py:249
  10.1 4.6 %collective-permute-done.1.heads_ref = bf16[1408,128]{1,0:T(8,128)(2,1)S(1)} collective-permute-done((bf16[1408,128]{1,0:T(8,128)(2,1)S(1)}, bf16[1408,128]{1,0:T(8,128)(2,1)S(1)}, u32[]{:S(2)}, u32[]{:S(2)}) %collective-permute-start.1) | collective-permute-done | bytes 360480 | tf_op jit(solution)/shard_map/ppermute | solution.py:983
  14.7 24.7 %layer.1 = (bf16[3200,128]{1,0:T(8,128)(2,1)S(1)}, bf16[3200,128]{1,0:T(8,128)(2,1)}, bf16[3072,1024]{1,0:T(8,128)(2,1)}, bf16[3072,256]{1,0:T(8,128)(2,1)}, f32...) custom-call(bf16[384,128]{1,0:T(8,128)(2,1)S(1)} %collective-permute-done.rim, ...), custom_call_target="tpu_custom_call" | custom-call | tf_op jit(solution)/shard_map/layer/pallas_call | solution.py:670
  39.5 0.1 collective-permute-start.2
  39.6 2.5 %collective-permute-done.2 = bf16[3200,128]{1,0:T(8,128)(2,1)S(1)} collective-permute-done((bf16[3200,128]{1,0:T(8,128)(2,1)}, bf16[3200,128]{1,0:T(8,128)(2,1)S(1)}, u32[]{:S(2)}, u32[]{:S(2)}) %collective-permute-start.2) | collective-permute-done | bytes 819232 | tf_op jit(solution)/shard_map/ppermute | solution.py:908
  42.1 0.2 add_convert_fusion
  42.3 0.1 dynamic-slice_bitcast_fusion
  42.4 2.5 %collective-permute-start.3 = (bf16[800,128]{1,0:T(8,128)(2,1)S(1)}, bf16[800,128]{1,0:T(8,128)(2,1)S(1)}, u32[]{:S(2)}, u32[]{:S(2)}) collective-permute-start(bf16[800,128]{1,0:T(8,128)(2,1)S(1)} %get-tuple-element.114), channel_id=1, source_target_pairs={{0,1},{1,0},{2,10},{3,11},{4,5},{5,4},{6,14},{7,15},{8,9},{9,8},{1... | collective-permute-start | bytes 614408 | tf_op jit(solution)/shard_map/ppermute | solution.py:908
  44.9 1.5 %collective-permute-start.4 = (bf16[800,128]{1,0:T(8,128)(2,1)S(1)}, bf16[800,128]{1,0:T(8,128)(2,1)S(1)}, u32[]{:S(2)}, u32[]{:S(2)}) collective-permute-start(bf16[800,128]{1,0:T(8,128)(2,1)S(1)} %get-tuple-element.113), channel_id=1, source_target_pairs={{0,4},{1,5},{2,18},{3,19},{4,0},{5,1},{6,22},{7,23},{8,12},{9,13},... | collective-permute-start | bytes 614408 | tf_op jit(solution)/shard_map/ppermute | solution.py:908
  46.4 5.7 %input_grad.1 = bf16[3072,256]{1,0:T(8,128)(2,1)} custom-call(bf16[3072,256]{1,0:T(8,128)(2,1)} %x_in.3, f32[3072,256]{1,0:T(8,128)} %get-tuple-element.79.mid_in, bf16[3072,768]{1,0:T(8,128)(2,1)} %get-tuple-element.80.dqkv_in, bf16[256,768]{1,0:T(8,128)(2,1)} %get-tuple-element.81.wqkv_in, f32[1,256]{1,0:T(1,128)S(1)} %bitcast.39), custom_call_target="tpu_custom_call" | custom-call | tf_op jit(solution)/shard_map/input_grad/pallas_call | solution.py:774
  52.1 0.9 %collective-permute-done.5 = bf16[800,128]{1,0:T(8,128)(2,1)S(1)} collective-permute-done((bf16[800,128]{1,0:T(8,128)(2,1)S(1)}, bf16[800,128]{1,0:T(8,128)(2,1)S(1)}, u32[]{:S(2)}, u32[]{:S(2)}) %collective-permute-start.5) | collective-permute-done | bytes 204832 | tf_op jit(solution)/shard_map/ppermute | solution.py:908
  53.1 0.1 broadcast.7.clone
  53.2 0.2 bitcast_dynamic-update-slice_fusion.6
  53.3 1.6 %collective-permute-start.6 = (bf16[800,128]{1,0:T(8,128)(2,1)S(1)}, bf16[800,128]{1,0:T(8,128)(2,1)S(1)}, u32[]{:S(2)}, u32[]{:S(2)}) collective-permute-start(bf16[800,128]{1,0:T(8,128)(2,1)S(1)} %get-tuple-element.86), channel_id=1, source_target_pairs={{0,8},{1,9},{2,3},{3,2},{4,12},{5,13},{6,7},{7,6},{8,0},{9,1},{10,... | collective-permute-start | bytes 614408 | tf_op jit(solution)/shard_map/ppermute | solution.py:908
  55.0 1.9 %collective-permute-start.7 = (bf16[800,128]{1,0:T(8,128)(2,1)S(1)}, bf16[800,128]{1,0:T(8,128)(2,1)S(1)}, u32[]{:S(2)}, u32[]{:S(2)}) collective-permute-start(bf16[800,128]{1,0:T(8,128)(2,1)S(1)} %get-tuple-element.86), channel_id=1, source_target_pairs={{0,16},{1,17},{2,6},{3,7},{4,20},{5,21},{6,2},{7,3},{8,24},{9,25},... | collective-permute-start | bytes 614408 | tf_op jit(solution)/shard_map/ppermute | solution.py:908
  56.9 0.9 %collective-permute-start.8 = (bf16[800,128]{1,0:T(8,128)(2,1)S(1)}, bf16[800,128]{1,0:T(8,128)(2,1)S(1)}, u32[]{:S(2)}, u32[]{:S(2)}) collective-permute-start(bf16[800,128]{1,0:T(8,128)(2,1)S(1)} %get-tuple-element.86), channel_id=1, source_target_pairs={{0,24},{1,25},{2,7},{3,6},{4,28},{5,29},{6,3},{7,2},{8,16},{9,17},... | collective-permute-start | bytes 614408 | tf_op jit(solution)/shard_map/ppermute | solution.py:908
  57.8 5.7 %mixed.1 = bf16[3072,256]{1,0:T(8,128)(2,1)} custom-call(bf16[3072,256]{1,0:T(8,128)(2,1)} %x_in.3, bf16[3072,256]{1,0:T(8,128)(2,1)} %get-tuple-element.87.att_in, bf16[3072,1024]{1,0:T(8,128)(2,1)} %get-tuple-element.88.act_in, bf16[256,256]{1,0:T(8,128)(2,1)} %get-tuple-element.89.wout_in, bf16[1024,256]{1,0:T(8,128)(2,1)} %down_in.1, f32[1,256]{1,0:T(1,128)S(1)} %bitcast.45), custom_call_target="tpu_custom_call" | custom-call | tf_op jit(solution)/shard_map/mixed/pallas_call | solution.py:774
  63.5 2.5 %collective-permute-done.7 = bf16[800,128]{1,0:T(8,128)(2,1)S(1)} collective-permute-done((bf16[800,128]{1,0:T(8,128)(2,1)S(1)}, bf16[800,128]{1,0:T(8,128)(2,1)S(1)}, u32[]{:S(2)}, u32[]{:S(2)}) %collective-permute-start.7) | collective-permute-done | bytes 204832 | tf_op jit(solution)/shard_map/ppermute | solution.py:908
  66.1 0.1 broadcast.7
  66.2 0.1 constant_dynamic-update-slice_fusion
  66.4 1.3 %collective-permute-start.9 = (bf16[800,128]{1,0:T(8,128)(2,1)S(1)}, bf16[800,128]{1,0:T(8,128)(2,1)S(1)}, u32[]{:S(2)}, u32[]{:S(2)}) collective-permute-start(bf16[800,128]{1,0:T(8,128)(2,1)S(1)} %bitcast.50), channel_id=1, source_target_pairs={{0,1},{1,0},{2,10},{3,11},{4,5},{5,4},{6,14},{7,15},{8,9},{9,8},{1... | collective-permute-start | bytes 614408 | tf_op jit(solution)/shard_map/ppermute | solution.py:908
  67.7 1.5 %collective-permute-start.10 = (bf16[800,128]{1,0:T(8,128)(2,1)S(1)}, bf16[800,128]{1,0:T(8,128)(2,1)S(1)}, u32[]{:S(2)}, u32[]{:S(2)}) collective-permute-start(bf16[800,128]{1,0:T(8,128)(2,1)S(1)} %bitcast.51), channel_id=1, source_target_pairs={{0,4},{1,5},{2,18},{3,19},{4,0},{5,1},{6,22},{7,23},{8,12},{9,13},... | collective-permute-start | bytes 614408 | tf_op jit(solution)/shard_map/ppermute | solution.py:908
  69.2 0.7 collective-permute-start.11
  69.9 2.3 %collective-permute-done.9 = bf16[800,128]{1,0:T(8,128)(2,1)S(1)} collective-permute-done((bf16[800,128]{1,0:T(8,128)(2,1)S(1)}, bf16[800,128]{1,0:T(8,128)(2,1)S(1)}, u32[]{:S(2)}, u32[]{:S(2)}) %collective-permute-start.9) | collective-permute-done | bytes 204832 | tf_op jit(solution)/shard_map/ppermute | solution.py:908
  72.2 1.2 %collective-permute-done.10 = bf16[800,128]{1,0:T(8,128)(2,1)S(1)} collective-permute-done((bf16[800,128]{1,0:T(8,128)(2,1)S(1)}, bf16[800,128]{1,0:T(8,128)(2,1)S(1)}, u32[]{:S(2)}, u32[]{:S(2)}) %collective-permute-start.10) | collective-permute-done | bytes 204832 | tf_op jit(solution)/shard_map/ppermute | solution.py:908
  73.5 2.4 %collective-permute-done.11 = bf16[800,128]{1,0:T(8,128)(2,1)S(1)} collective-permute-done((bf16[800,128]{1,0:T(8,128)(2,1)S(1)}, bf16[800,128]{1,0:T(8,128)(2,1)S(1)}, u32[]{:S(2)}, u32[]{:S(2)}) %collective-permute-start.11) | collective-permute-done | bytes 204832 | tf_op jit(solution)/shard_map/ppermute | solution.py:908
  75.9 0.4 collective-permute-start.12
  76.3 2.0 %collective-permute-done.12.other_ref = bf16[3200,128]{1,0:T(8,128)(2,1)S(1)} collective-permute-done((bf16[3200,128]{1,0:T(8,128)(2,1)S(1)}, bf16[3200,128]{1,0:T(8,128)(2,1)S(1)}, u32[]{:S(2)}, u32[]{:S(2)}) %collective-permute-start.12) | collective-permute-done | bytes 819232 | tf_op jit(solution)/shard_map/ppermute | solution.py:908
  78.3 2.2 %finish.1 = (f32[256]{0:T(256)}, f32[256]{0:T(256)}, f32[256,128]{1,0:T(8,128)}, f32[256,128]{1,0:T(8,128)}, f32[256,128]{1,0:T(8,128)}, /*index=5*/f32[128,256]...) custom-call(bf16[3200,128]{1,0:T(8,128)(2,1)S(1)} %bitcast.36, ...), custom_call_target="tpu_custom_call" | custom-call | tf_op jit(solution)/shard_map/finish/pallas_call | solution.py:874
  (40 shorter events, 0.3 us)
Async XLA Ops:
  0.6 4.9 %copy-start = (bf16[3072,256]{1,0:T(8,128)(2,1)S(1)}, bf16[3072,256]{1,0:T(8,128)(2,1)}, u32[]{:S(2)}) copy-start(bf16[3072,256]{1,0:T(8,128)(2,1)} %x_in.3) | copy-start | bytes 4718596
  0.7 4.9 %copy-start.1 = (bf16[256,128]{1,0:T(8,128)(2,1)S(1)}, bf16[256,128]{1,0:T(8,128)(2,1)}, u32[]{:S(2)}) copy-start(bf16[256,128]{1,0:T(8,128)(2,1)} %query_ref.5) | copy-start | bytes 196612
  0.7 4.9 %copy-start.2 = (bf16[256,128]{1,0:T(8,128)(2,1)S(1)}, bf16[256,128]{1,0:T(8,128)(2,1)}, u32[]{:S(2)}) copy-start(bf16[256,128]{1,0:T(8,128)(2,1)} %key_ref.5) | copy-start | bytes 196612
  0.7 4.9 %copy-start.3 = (bf16[256,128]{1,0:T(8,128)(2,1)S(1)}, bf16[256,128]{1,0:T(8,128)(2,1)}, u32[]{:S(2)}) copy-start(bf16[256,128]{1,0:T(8,128)(2,1)} %value_ref.5) | copy-start | bytes 196612
  0.7 4.9 %copy-start.6 = (f32[256]{0:T(256)S(1)}, f32[256]{0:T(256)}, u32[]{:S(2)}) copy-start(f32[256]{0:T(256)} %param.20) | copy-start | bytes 3076
  0.7 4.9 %copy-start.7 = (f32[256]{0:T(256)S(1)}, f32[256]{0:T(256)}, u32[]{:S(2)}) copy-start(f32[256]{0:T(256)} %param.21) | copy-start | bytes 3076
  0.7 4.9 %copy-start.12 = (s32[128]{0:T(128)S(1)}, s32[128]{0:T(128)}, u32[]{:S(2)}) copy-start(s32[128]{0:T(128)} %param.18) | copy-start | bytes 1540
  0.7 4.9 %copy-start.13 = (s32[128]{0:T(128)S(1)}, s32[128]{0:T(128)}, u32[]{:S(2)}) copy-start(s32[128]{0:T(128)} %param.19) | copy-start | bytes 1540
  1.9 12.8 %collective-permute-start.1 = (bf16[1408,128]{1,0:T(8,128)(2,1)S(1)}, bf16[1408,128]{1,0:T(8,128)(2,1)S(1)}, u32[]{:S(2)}, u32[]{:S(2)}) collective-permute-start(bf16[1408,128]{1,0:T(8,128)(2,1)S(1)} %get-tuple-element.75), channel_id=1, source_target_pairs={{0,1},{1,0},{2,3},{3,2},{4,5},{5,4},{6,7},{7,6},{8,9},{9,8},{10,11... | collective-permute-start | bytes 1081352 | tf_op jit(solution)/shard_map/ppermute | solution.py:983
  4.9 5.1 %collective-permute-start = (bf16[384,128]{1,0:T(8,128)(2,1)S(1)}, bf16[384,128]{1,0:T(8,128)(2,1)S(1)}, u32[]{:S(2)}, u32[]{:S(2)}) collective-permute-start(bf16[384,128]{1,0:T(8,128)(2,1)S(1)} %get-tuple-element.61), channel_id=1, source_target_pairs={{1,2},{3,4},{5,6},{7,8},{9,10},{11,12},{13,14},{15,16},{17,18},{19... | collective-permute-start | bytes 294920 | tf_op jit(solution)/shard_map/ppermute | solution.py:985
  5.7 9.0 %copy-start.4 = (bf16[256,1024]{1,0:T(8,128)(2,1)S(1)}, bf16[256,1024]{1,0:T(8,128)(2,1)}, u32[]{:S(2)}) copy-start(bf16[256,1024]{1,0:T(8,128)(2,1)} %up_ref.1) | copy-start | bytes 1572868
  5.7 9.0 %copy-start.5 = (bf16[128,256]{1,0:T(8,128)(2,1)S(1)}, bf16[128,256]{1,0:T(8,128)(2,1)}, u32[]{:S(2)}) copy-start(bf16[128,256]{1,0:T(8,128)(2,1)} %out_ref.3) | copy-start | bytes 196612
  5.7 9.0 %copy-start.8 = (f32[1024]{0:T(1024)S(1)}, f32[1024]{0:T(1024)}, u32[]{:S(2)}) copy-start(f32[1024]{0:T(1024)} %param.29) | copy-start | bytes 12292
  5.7 9.0 %copy-start.9 = (f32[256]{0:T(256)S(1)}, f32[256]{0:T(256)}, u32[]{:S(2)}) copy-start(f32[256]{0:T(256)} %param.26) | copy-start | bytes 3076
  5.7 9.0 %copy-start.10 = (f32[256]{0:T(256)S(1)}, f32[256]{0:T(256)}, u32[]{:S(2)}) copy-start(f32[256]{0:T(256)} %param.27) | copy-start | bytes 3076
  39.5 2.6 %collective-permute-start.2 = (bf16[3200,128]{1,0:T(8,128)(2,1)}, bf16[3200,128]{1,0:T(8,128)(2,1)S(1)}, u32[]{:S(2)}, u32[]{:S(2)}) collective-permute-start(bf16[3200,128]{1,0:T(8,128)(2,1)} %get-tuple-element.77), channel_id=1, source_target_pairs={{0,2},{1,3},{2,0},{3,1},{4,6},{5,7},{6,4},{7,5},{8,10},{9,11},{10,... | collective-permute-start | bytes 2457608 | tf_op jit(solution)/shard_map/ppermute | solution.py:908
  42.4 9.8 %collective-permute-start.3 = (bf16[800,128]{1,0:T(8,128)(2,1)S(1)}, bf16[800,128]{1,0:T(8,128)(2,1)S(1)}, u32[]{:S(2)}, u32[]{:S(2)}) collective-permute-start(bf16[800,128]{1,0:T(8,128)(2,1)S(1)} %get-tuple-element.114), channel_id=1, source_target_pairs={{0,1},{1,0},{2,10},{3,11},{4,5},{5,4},{6,14},{7,15},{8,9},{9,8},{1... | collective-permute-start | bytes 614408 | tf_op jit(solution)/shard_map/ppermute | solution.py:908
  44.9 7.2 %collective-permute-start.4 = (bf16[800,128]{1,0:T(8,128)(2,1)S(1)}, bf16[800,128]{1,0:T(8,128)(2,1)S(1)}, u32[]{:S(2)}, u32[]{:S(2)}) collective-permute-start(bf16[800,128]{1,0:T(8,128)(2,1)S(1)} %get-tuple-element.113), channel_id=1, source_target_pairs={{0,4},{1,5},{2,18},{3,19},{4,0},{5,1},{6,22},{7,23},{8,12},{9,13},... | collective-permute-start | bytes 614408 | tf_op jit(solution)/shard_map/ppermute | solution.py:908
  46.4 6.7 %collective-permute-start.5 = (bf16[800,128]{1,0:T(8,128)(2,1)S(1)}, bf16[800,128]{1,0:T(8,128)(2,1)S(1)}, u32[]{:S(2)}, u32[]{:S(2)}) collective-permute-start(bf16[800,128]{1,0:T(8,128)(2,1)S(1)} %get-tuple-element.112), channel_id=1, source_target_pairs={{0,5},{1,4},{2,26},{3,27},{4,1},{5,0},{6,30},{7,31},{8,13},{9,12},... | collective-permute-start | bytes 614408 | tf_op jit(solution)/shard_map/ppermute | solution.py:908
  52.1 5.7 %copy-start.11 = (f32[256]{0:T(256)S(1)}, f32[256]{0:T(256)}, u32[]{:S(2)}) copy-start(f32[256]{0:T(256)} %param.31) | copy-start | bytes 3076
  53.3 10.2 %collective-permute-start.6 = (bf16[800,128]{1,0:T(8,128)(2,1)S(1)}, bf16[800,128]{1,0:T(8,128)(2,1)S(1)}, u32[]{:S(2)}, u32[]{:S(2)}) collective-permute-start(bf16[800,128]{1,0:T(8,128)(2,1)S(1)} %get-tuple-element.86), channel_id=1, source_target_pairs={{0,8},{1,9},{2,3},{3,2},{4,12},{5,13},{6,7},{7,6},{8,0},{9,1},{10,... | collective-permute-start | bytes 614408 | tf_op jit(solution)/shard_map/ppermute | solution.py:908
  55.0 11.0 %collective-permute-start.7 = (bf16[800,128]{1,0:T(8,128)(2,1)S(1)}, bf16[800,128]{1,0:T(8,128)(2,1)S(1)}, u32[]{:S(2)}, u32[]{:S(2)}) collective-permute-start(bf16[800,128]{1,0:T(8,128)(2,1)S(1)} %get-tuple-element.86), channel_id=1, source_target_pairs={{0,16},{1,17},{2,6},{3,7},{4,20},{5,21},{6,2},{7,3},{8,24},{9,25},... | collective-permute-start | bytes 614408 | tf_op jit(solution)/shard_map/ppermute | solution.py:908
  56.9 9.2 %collective-permute-start.8 = (bf16[800,128]{1,0:T(8,128)(2,1)S(1)}, bf16[800,128]{1,0:T(8,128)(2,1)S(1)}, u32[]{:S(2)}, u32[]{:S(2)}) collective-permute-start(bf16[800,128]{1,0:T(8,128)(2,1)S(1)} %get-tuple-element.86), channel_id=1, source_target_pairs={{0,24},{1,25},{2,7},{3,6},{4,28},{5,29},{6,3},{7,2},{8,16},{9,17},... | collective-permute-start | bytes 614408 | tf_op jit(solution)/shard_map/ppermute | solution.py:908
  66.4 5.8 %collective-permute-start.9 = (bf16[800,128]{1,0:T(8,128)(2,1)S(1)}, bf16[800,128]{1,0:T(8,128)(2,1)S(1)}, u32[]{:S(2)}, u32[]{:S(2)}) collective-permute-start(bf16[800,128]{1,0:T(8,128)(2,1)S(1)} %bitcast.50), channel_id=1, source_target_pairs={{0,1},{1,0},{2,10},{3,11},{4,5},{5,4},{6,14},{7,15},{8,9},{9,8},{1... | collective-permute-start | bytes 614408 | tf_op jit(solution)/shard_map/ppermute | solution.py:908
  67.7 5.8 %collective-permute-start.10 = (bf16[800,128]{1,0:T(8,128)(2,1)S(1)}, bf16[800,128]{1,0:T(8,128)(2,1)S(1)}, u32[]{:S(2)}, u32[]{:S(2)}) collective-permute-start(bf16[800,128]{1,0:T(8,128)(2,1)S(1)} %bitcast.51), channel_id=1, source_target_pairs={{0,4},{1,5},{2,18},{3,19},{4,0},{5,1},{6,22},{7,23},{8,12},{9,13},... | collective-permute-start | bytes 614408 | tf_op jit(solution)/shard_map/ppermute | solution.py:908
  69.2 6.7 %collective-permute-start.11 = (bf16[800,128]{1,0:T(8,128)(2,1)S(1)}, bf16[800,128]{1,0:T(8,128)(2,1)S(1)}, u32[]{:S(2)}, u32[]{:S(2)}) collective-permute-start(bf16[800,128]{1,0:T(8,128)(2,1)S(1)} %bitcast.52), channel_id=1, source_target_pairs={{0,5},{1,4},{2,26},{3,27},{4,1},{5,0},{6,30},{7,31},{8,13},{9,12},... | collective-permute-start | bytes 614408 | tf_op jit(solution)/shard_map/ppermute | solution.py:908
  75.9 2.4 %collective-permute-start.12 = (bf16[3200,128]{1,0:T(8,128)(2,1)S(1)}, bf16[3200,128]{1,0:T(8,128)(2,1)S(1)}, u32[]{:S(2)}, u32[]{:S(2)}) collective-permute-start(bf16[3200,128]{1,0:T(8,128)(2,1)S(1)} %bitcast.35), channel_id=1, source_target_pairs={{0,2},{1,3},{2,0},{3,1},{4,6},{5,7},{6,4},{7,5},{8,10},{9,11},{10,... | collective-permute-start | bytes 2457608 | tf_op jit(solution)/shard_map/ppermute | solution.py:908

commit v4 on v3

--- a/solution.py
+++ b/solution.py
@@ -79,7 +79,7 @@
     return [job for *_, job in sorted(marked, key=lambda item: item[:3])]
 
 
-VECTOR_ROWS = 128
+VECTOR_ROWS = 64
 
 
 def half_rows(FF, D):
@@ -278,7 +278,8 @@
 
 def layer_kernel(
     rows,
-    rim_ref,
+    near_rim,
+    far_rim,
     normed,
     own_q,
     own_k,
@@ -300,7 +301,8 @@
     key_ref,
     value_ref,
     out_ref,
-    heads_ref,
+    half_ref,
+    other_half_ref,
     gain2_ref,
     shift2_ref,
     up_bias_ref,
@@ -345,6 +347,7 @@
     own = rows * WINDOW
     head = lax.axis_index("head")
     place = lax.axis_index("seq") * lax.axis_size("head") + head
+    core = (place & 2) // 2
     step = CHUNK * WINDOW
     steps = rows // CHUNK
     leaving = {}
@@ -353,23 +356,28 @@
         leaving[kind, n] = pltpu.make_async_copy(source, target, out_sem.at[kind, n])
         leaving[kind, n].start()
 
+    def theirs(at, size):
+        half, at = at // (2 * D), at % (2 * D)
+        here, there = half_ref[at : at + size, :], other_half_ref[at : at + size, :]
+        return jnp.where(core == half, here, there)
+
     for part, ref in enumerate((query_ref, key_ref, value_ref)):
         wqkv[:, part * D : part * D + HEAD_DIM] = ref[...]
-        wqkv[:, part * D + HEAD_DIM : (part + 1) * D] = heads_ref[part * D : (part + 1) * D, :]
-        wother[:, part * HEAD_DIM : (part + 1) * HEAD_DIM] = heads_ref[part * D : (part + 1) * D, :]
+        wqkv[:, part * D + HEAD_DIM : (part + 1) * D] = theirs(part * D, D)
+        wother[:, part * HEAD_DIM : (part + 1) * HEAD_DIM] = theirs(part * D, D)
     wout[:HEAD_DIM, :] = out_ref[...]
     for half in range(D // HEAD_DIM):
-        wout[HEAD_DIM:, half * HEAD_DIM : (half + 1) * HEAD_DIM] = heads_ref[
-            3 * D + half * HEAD_DIM : 3 * D + (half + 1) * HEAD_DIM, :
-        ]
+        wout[HEAD_DIM:, half * HEAD_DIM : (half + 1) * HEAD_DIM] = theirs(
+            3 * D + half * HEAD_DIM, HEAD_DIM
+        )
     leave(4, 0, wqkv, wqkv_out)
     leave(4, 1, wout, wout_out)
     acc_vec[...] = jnp.zeros_like(acc_vec)
 
     for half in range(D // HEAD_DIM):
         cols = slice(half * HEAD_DIM, (half + 1) * HEAD_DIM)
-        near = heads_ref[4 * D + half * 2 * WINDOW : 4 * D + (half + 1) * 2 * WINDOW, :]
-        far = rim_ref[half * 2 * WINDOW : (half + 1) * 2 * WINDOW, :]
+        near = near_rim[half * 2 * WINDOW : (half + 1) * 2 * WINDOW, :]
+        far = far_rim[half * 2 * WINDOW : (half + 1) * 2 * WINDOW, :]
         rim_x[:WINDOW, cols] = jnp.where(head == 0, far[:WINDOW], near[:WINDOW])
         rim_x[WINDOW:, cols] = jnp.where(head == 0, near[:WINDOW], far[:WINDOW])
         rim_cot[:, cols] = jnp.where(head == 0, near[WINDOW:], far[WINDOW:])
@@ -582,7 +590,6 @@
         else:
             do([weighs[-1]] + halo + [back])
 
-    core = (place & 2) // 2
     wide = FF // 2
     halves = ((core, keep_ref), (1 - core, send_ref))
     after_down = D // HEAD_DIM * wide
@@ -658,14 +665,14 @@
             copy.wait()
 
 
-def layer(rim, made, tokens, up, gain1, shift1, weights, other, gain2, shift2, up_bias):
+def layer(rims, made, tokens, up, gain1, shift1, weights, others, gain2, shift2, up_bias):
     own, D = tokens.shape
     FF = up.shape[1]
     rows = own // WINDOW
     count = own + 2 * WINDOW
     half = half_rows(FF, D)
-    tokens, up, rim, other = in_vmem(tokens), in_vmem(up), in_vmem(rim), in_vmem(other)
-    made = [in_vmem(array) for array in made]
+    tokens, up = in_vmem(tokens), in_vmem(up)
+    rims, made, others = ([in_vmem(array) for array in arrays] for arrays in (rims, made, others))
     vmem = pl.BlockSpec(memory_space=pltpu.VMEM)
     return pl.pallas_call(
         functools.partial(layer_kernel, rows),
@@ -679,7 +686,7 @@
             pltpu.HBM((D, 3 * D), BF16),
             pltpu.HBM((D, D), BF16),
         ),
-        in_specs=[vmem] * (1 + len(made) + 2 + 2 + 4 + 1 + 3),
+        in_specs=[vmem] * (2 + len(made) + 2 + 2 + 4 + 2 + 3),
         out_specs=(vmem, vmem) + (pl.BlockSpec(memory_space=pltpu.HBM),) * 6,
         scratch_shapes=[
             pltpu.VMEM((2, CHUNK * WINDOW, FF), BF16),
@@ -712,7 +719,7 @@
         ],
         compiler_params=pltpu.CompilerParams(vmem_limit_bytes=34 * 1024 * 1024),
         name="layer",
-    )(rim, *made, tokens, up, gain1, shift1, *weights, other, gain2, shift2, up_bias)
+    )(*rims, *made, tokens, up, gain1, shift1, *weights, *others, gain2, shift2, up_bias)
 
 
 def token_chunks(streams, out_ref, buf, in_sem, out_sem, fixed, work):
@@ -787,26 +794,47 @@
     )(*[in_hbm(array) for array in arrays], small)
 
 
-def pack_kernel(query_ref, key_ref, value_ref, out_ref, tok_ref, cot_ref, near_ref, far_ref, sem):
+def pack_kernel(query_ref, key_ref, value_ref, out_ref, tok_ref, cot_ref, half_ref, near_ref, far_ref, sem):
     D = query_ref.shape[0]
     own = tok_ref.shape[0]
     head = lax.axis_index("head")
-    moves = [
-        (ref, near_ref.at[pl.ds(part * D, D)]) for part, ref in enumerate((query_ref, key_ref, value_ref))
-    ]
+    core = lax.axis_index("seq") % 2
     last = own - WINDOW
     near_from = pl.multiple_of((1 - head) * last, WINDOW)
     far_from = pl.multiple_of(head * last, WINDOW)
+    moves = []
     for half in range(D // HEAD_DIM):
         cols = pl.ds(half * HEAD_DIM, HEAD_DIM)
-        moves.append((out_ref.at[:, cols], near_ref.at[pl.ds(3 * D + half * HEAD_DIM, HEAD_DIM)]))
         for k, ref in enumerate((tok_ref, cot_ref)):
             at = (half * 2 + k) * WINDOW
-            moves.append((ref.at[pl.ds(near_from, WINDOW), cols], near_ref.at[pl.ds(4 * D + at, WINDOW)]))
+            moves.append((ref.at[pl.ds(near_from, WINDOW), cols], near_ref.at[pl.ds(at, WINDOW)]))
             moves.append((ref.at[pl.ds(far_from, WINDOW), cols], far_ref.at[pl.ds(at, WINDOW)]))
     copies = [pltpu.make_async_copy(a, b, sem.at[n]) for n, (a, b) in enumerate(moves)]
     for copy in copies:
         copy.start()
+
+    def weights(moves):
+        sent = [pltpu.make_async_copy(a, b, sem.at[len(copies) + n]) for n, (a, b) in enumerate(moves)]
+        for copy in sent:
+            copy.start()
+        for copy in sent:
+            copy.wait()
+
+    @pl.when(core == 0)
+    def _():
+        weights([(query_ref, half_ref.at[pl.ds(0, D)]), (key_ref, half_ref.at[pl.ds(D, D)])])
+
+    @pl.when(core == 1)
+    def _():
+        outs = [
+            (
+                out_ref.at[:, pl.ds(half * HEAD_DIM, HEAD_DIM)],
+                half_ref.at[pl.ds(D + half * HEAD_DIM, HEAD_DIM)],
+            )
+            for half in range(D // HEAD_DIM)
+        ]
+        weights([(value_ref, half_ref.at[pl.ds(0, D)])] + outs)
+
     for copy in copies:
         copy.wait()
 
@@ -814,76 +842,85 @@
 def pack(query_weight, key_weight, value_weight, out_weight, tokens, cotangent):
     D = query_weight.shape[0]
     rim = 2 * WINDOW * D // HEAD_DIM
-    anywhere = pl.BlockSpec(memory_space=pl.ANY)
     vmem = pl.BlockSpec(memory_space=pltpu.VMEM)
     return pl.pallas_call(
         pack_kernel,
-        out_shape=(pltpu.VMEM((4 * D + rim, HEAD_DIM), BF16), pltpu.VMEM((rim, HEAD_DIM), BF16)),
-        in_specs=[anywhere] * 6,
-        out_specs=(vmem, vmem),
-        scratch_shapes=[pltpu.SemaphoreType.DMA((3 + 5 * (D // HEAD_DIM),))],
+        out_shape=(
+            pltpu.VMEM((2 * D, HEAD_DIM), BF16),
+            pltpu.VMEM((rim, HEAD_DIM), BF16),
+            pltpu.VMEM((rim, HEAD_DIM), BF16),
+        ),
+        in_specs=[pl.BlockSpec(memory_space=pl.ANY)] * 6,
+        out_specs=(vmem, vmem, vmem),
+        scratch_shapes=[pltpu.SemaphoreType.DMA((6 * (D // HEAD_DIM) + 1,))],
         name="pack",
     )(query_weight, key_weight, value_weight, out_weight, tokens, cotangent)
 
 
-def finish_kernel(FF, D, mine_ref, other_ref, *refs):
-    outs, (down_buf, up_buf, vec_rows, sem) = refs[:12], refs[12:]
-    gain1, shift1, query, key, value, out, gain2, shift2, up, up_bias, down, down_bias = outs
+def finish_kernel(FF, D, second, mine_ref, *refs):
+    if second:
+        vectors, refs = (refs[0], refs[7:13]), refs[13:]
+    outs, (down_buf, up_buf, heads_buf, vec_rows, sem) = refs[:6], refs[6:]
+    query, key, value, out, up, down = outs
     core = lax.axis_index("seq") % 2
     head = lax.axis_index("head")
-    halves = ((core, mine_ref), (1 - core, other_ref))
+    c = 1 - core if second else core
     wide = FF // 2
-    for c, ref in halves:
-        rows = pl.ds(pl.multiple_of(c * wide, wide), wide)
-        for half in range(D // HEAD_DIM):
-            down_buf[rows, half * HEAD_DIM : (half + 1) * HEAD_DIM] = ref[
-                half * wide : (half + 1) * wide, :
-            ].astype(F32)
-    copies = [pltpu.make_async_copy(down_buf, down, sem.at[0])]
-    copies[0].start()
+    copies = []
+
+    def leave(source, target):
+        copies.append(pltpu.make_async_copy(source, target, sem.at[len(copies)]))
+        copies[-1].start()
+
+    for half in range(D // HEAD_DIM):
+        down_buf[:, half * HEAD_DIM : (half + 1) * HEAD_DIM] = mine_ref[
+            half * wide : (half + 1) * wide, :
+        ].astype(F32)
+    leave(down_buf, down.at[pl.ds(pl.multiple_of(c * wide, wide), wide)])
     start = D // HEAD_DIM * wide
-    for c, ref in halves:
-        for n, f in enumerate(range(0, wide, HEAD_DIM)):
-            at = pl.ds(pl.multiple_of(c * wide + f, HEAD_DIM), HEAD_DIM)
-            up_buf[:, at] = ref[start + n * D : start + (n + 1) * D, :].astype(F32)
-    copies.append(pltpu.make_async_copy(up_buf, up, sem.at[1]))
-    copies[1].start()
+    for n, f in enumerate(range(0, wide, HEAD_DIM)):
+        up_buf[:, f : f + HEAD_DIM] = mine_ref[start + n * D : start + (n + 1) * D, :].astype(F32)
+    leave(up_buf, up.at[:, pl.ds(pl.multiple_of(c * wide, wide), wide)])
     start += wide // HEAD_DIM * D
-    for c, ref in halves:
-        mine = pl.ds(pl.multiple_of(c * HEAD_DIM, HEAD_DIM), HEAD_DIM)
-        base = start + head * (4 * HEAD_DIM)
-        for part, made in enumerate((query, key, value)):
-            at = pl.multiple_of(base + part * HEAD_DIM, HEAD_DIM)
-            made[mine, :] = ref[pl.ds(at, HEAD_DIM), :].astype(F32)
-        at = pl.multiple_of(base + 3 * HEAD_DIM, HEAD_DIM)
-        out[:, mine] = ref[pl.ds(at, HEAD_DIM), :].astype(F32)
-        base = start + 8 * HEAD_DIM
-        vec_rows[pl.ds(pl.multiple_of(c * 16, 16), 16), :] = ref[base : base + 16, :].astype(F32)
-    vectors = (gain1, shift1, gain2, shift2, down_bias)
-    for s, (n, cols) in enumerate(vector_slots(FF, D)):
-        made = up_bias if n == 8 else vectors[n]
-        made[cols] = vec_rows[s, :]
+    own = pl.ds(pl.multiple_of(c * HEAD_DIM, HEAD_DIM), HEAD_DIM)
+    for part, made in enumerate((query, key, value, out)):
+        at = pl.multiple_of(start + (head * 4 + part) * HEAD_DIM, HEAD_DIM)
+        heads_buf[part] = mine_ref[pl.ds(at, HEAD_DIM), :].astype(F32)
+        leave(heads_buf.at[part], made.at[:, own] if part == 3 else made.at[own])
+    if second:
+        other_ref, made = vectors
+        at = start + 8 * HEAD_DIM
+        for k, ref in ((c, mine_ref), (core, other_ref)):
+            vec_rows[pl.ds(pl.multiple_of(k * 16, 16), 16), :] = ref[at : at + 16, :].astype(F32)
+        for s, (n, cols) in enumerate(vector_slots(FF, D)):
+            made[5 if n == 8 else n][cols] = vec_rows[s, :]
     for copy in copies:
         copy.wait()
 
 
-def finish(mine, other, FF, D):
+def finish(mine, FF, D, first=None):
     vmem = pl.BlockSpec(memory_space=pltpu.VMEM)
-    anywhere = pl.BlockSpec(memory_space=pl.ANY)
-    shapes = [(D,), (D,)] + [(D, HEAD_DIM)] * 3 + [(HEAD_DIM, D), (D,), (D,), (D, FF), (FF,), (FF, D), (D,)]
+    hbm = pl.BlockSpec(memory_space=pltpu.HBM)
+    arrays = [(D, HEAD_DIM)] * 3 + [(HEAD_DIM, D), (D, FF), (FF, D)]
+    vectors = [(D,)] * 5 + [(FF,)] if first else []
+    wide = FF // 2
+    given = (in_vmem(first[0]), *[in_hbm(array) for array in first[1]]) if first else ()
     return pl.pallas_call(
-        functools.partial(finish_kernel, FF, D),
-        out_shape=tuple(jax.ShapeDtypeStruct(shape, F32) for shape in shapes),
-        in_specs=[vmem, vmem],
-        out_specs=tuple(anywhere if n in (8, 10) else vmem for n in range(len(shapes))),
+        functools.partial(finish_kernel, FF, D, bool(first)),
+        out_shape=tuple(jax.ShapeDtypeStruct(shape, F32) for shape in vectors)
+        + tuple(pltpu.HBM(shape, F32) for shape in arrays),
+        in_specs=[vmem] + ([vmem] + [hbm] * 6 if first else []),
+        out_specs=(vmem,) * len(vectors) + (hbm,) * 6,
+        input_output_aliases={2 + n: 6 + n for n in range(6)} if first else {},
         scratch_shapes=[
-            pltpu.VMEM((FF, D), F32),
-            pltpu.VMEM((D, FF), F32),
+            pltpu.VMEM((wide, D), F32),
+            pltpu.VMEM((D, wide), F32),
+            pltpu.VMEM((4, HEAD_DIM, HEAD_DIM), F32),
             pltpu.VMEM((32, HEAD_DIM), F32),
-            pltpu.SemaphoreType.DMA((2,)),
+            pltpu.SemaphoreType.DMA((6,)),
         ],
-        name="finish",
-    )(in_vmem(mine), in_vmem(other))
+        name="finish_rest" if first else "finish",
+    )(in_vmem(mine), *given)
 
 
 def spans(masks):
@@ -979,22 +1016,25 @@
     own, D = tokens.shape
     FF = up_weight.shape[1]
     devices = lax.axis_size("seq") * lax.axis_size("head")
-    near, far = pack(query_weight, key_weight, value_weight, out_weight, tokens, cotangent)
-    other = lax.ppermute(near, "head", [(0, 1), (1, 0)])
+    half, near, far = pack(query_weight, key_weight, value_weight, out_weight, tokens, cotangent)
+    half = lax.ppermute(half, "head", [(0, 1), (1, 0)])
     pairs = [(i, i + 1) for i in range(1, devices - 1, 2)]
-    rim = lax.ppermute(far, BOTH, pairs + [(b, a) for a, b in pairs])
+    far = lax.ppermute(far, BOTH, pairs + [(b, a) for a, b in pairs])
+    near = lax.ppermute(near, "head", [(0, 1), (1, 0)])
     weights = (query_weight, key_weight, value_weight, out_weight)
     gain1, shift1 = first_gain[None], first_shift[None]
     made = local(tokens, cotangent, down_weight, image_rows[None], image_fill[None], gain1, shift1, weights)
+    half, near, far, mark = lax.optimization_barrier((half, near, far, made[6]))
+    made = (*made[:6], mark, *made[7:])
     keep, send, act, att, mid_grad, dqkv, wqkv, wout = layer(
-        rim,
+        (near, far),
         made,
         tokens,
         up_weight,
         gain1,
         shift1,
         weights,
-        other,
+        (half, across_cores(half)),
         second_gain[None],
         second_shift[None],
         up_bias[None],
@@ -1005,7 +1045,27 @@
     ]
     summed = (keep.astype(F32) + across_cores(send).astype(F32)).astype(BF16)
     mine, (input_grad, mixed) = all_sum(summed, side)
-    return (mixed, input_grad, *finish(mine, across_cores(mine), FF, D))
+    arrays = finish(mine, FF, D)
+    gain1_grad, shift1_grad, gain2_grad, shift2_grad, down_bias_grad, up_bias_grad, *arrays = finish(
+        across_cores(mine), FF, D, (mine, arrays)
+    )
+    query_grad, key_grad, value_grad, out_grad, up_grad, down_grad = arrays
+    return (
+        mixed,
+        input_grad,
+        gain1_grad,
+        shift1_grad,
+        query_grad,
+        key_grad,
+        value_grad,
+        out_grad,
+        gain2_grad,
+        shift2_grad,
+        up_grad,
+        up_bias_grad,
+        down_grad,
+        down_bias_grad,
+    )
 
 
 def solution(mesh):

time: 81.2 us -> 79.6 us (0.980)
  waiting for transfers between devices: 18.4 us -> 13.8 us
  starting transfers between devices: 16.2 us -> 19 us
    ppermute x2 -> x3, waiting for transfers between devices: 4.64 us -> 0.36 us  [the longest x1 0.36 us: shards(): near = lax.ppermute(near, 'head', [(0, 1), (1, 0)])]
    ppermute x11 -> x12, starting transfers between devices: 12.5 us -> 15.2 us  [partners(): lax.ppermute(value, BOTH, [(i, i ^ hops[i // 2 % 2]) for i in range(count)])]
    pallas_call x2 -> x3, Pallas kernels: 3.37 us -> 4.05 us  [the longest x2 2.86 us: finish(): pl.pallas_call(functools.partial(finish_kernel, FF, D, bool(first)), out_...]
    ppermute x11 -> x12, waiting for transfers between devices: 13.8 us -> 13.4 us  [partners(): lax.ppermute(value, BOTH, [(i, i ^ hops[i // 2 % 2]) for i in range(count)])]
    ppermute x2 -> x3, starting transfers between devices: 3.69 us -> 3.77 us  [the longest x1 3.03 us: shards(): half = lax.ppermute(half, 'head', [(0, 1), (1, 0)])]
  transfers between devices with their start and end apart: 13 -> 15, of which waited for: 8 -> 10; matrix products, arithmetic and copies ran while one was open for 0% -> 0% of each run, Pallas kernels for 19% -> 21%
where the time goes in v4:
time: 79.6 us; the launch traced here: 79.5 us
  Pallas kernels  44.5 us (56%)
  starting transfers between devices  19 us (24%)
  waiting for transfers between devices  13.8 us (17%)
  between operations  1.16 us (1%)
    pallas_call x1, Pallas kernels, layer(): pl.pallas_call(functools.partial(layer_kernel, rows), out_shape=(pltpu.VM...  24.8 us
    ppermute x12, starting transfers between devices, partners(): lax.ppermute(value, BOTH, [(i, i ^ hops[i // 2 % 2]) for i in range(count)])  15.2 us
    ppermute x12, waiting for transfers between devices, partners(): lax.ppermute(value, BOTH, [(i, i ^ hops[i // 2 % 2]) for i in range(count)])  13.4 us
    pallas_call x2, Pallas kernels, late(): pl.pallas_call(kernel, out_shape=pltpu.HBM((own, D), BF16), in_specs=[hbm...  11.4 us
    pallas_call x1, Pallas kernels, local(): pl.pallas_call(functools.partial(local_kernel, rows), out_shape=(pltpu.VM...  4.33 us
    ppermute x1, starting transfers between devices, shards(): half = lax.ppermute(half, 'head', [(0, 1), (1, 0)])  3.03 us
    pallas_call x2, Pallas kernels, finish(): pl.pallas_call(functools.partial(finish_kernel, FF, D, bool(first)), out_...  2.86 us
  transfers between devices with their start and end apart: 15, of which 10 were waited for; matrix products, arithmetic and copies ran while one was open for 0% of the time, Pallas kernels for 21%

profile of v4, /device:TPU:0, one launch (start us, length us, event | category | flops | bytes accessed | tf_op | source)
XLA Modules:
  0.0 79.5 jit_solution(2819079099957160210)
XLA Ops:
  0.7 1.2 %pack.1 = (bf16[512,128]{1,0:T(8,128)(2,1)S(1)}, bf16[384,128]{1,0:T(8,128)(2,1)S(1)}, bf16[384,128]{1,0:T(8,128)(2,1)S(1)}) custom-call(bf16[256,128]{1,0:T(8,128)(2,1)} %query_ref.5, bf16[256,128]{1,0:T(8,128)(2,1)} %key_ref.5, bf16[256,128]{1,0:T(8,128)(2,1)} %value_ref.5, bf16[128,256]{1,0:T(8,128)(2,1)} %out_ref.3, bf16[3072,256]{1,0:T(8,128)(2,1)} %x_in.3, ...), custom_call_target="tpu_custom_call" | custom-call | tf_op jit(solution)/shard_map/pack/pallas_call | solution.py:846
  1.9 3.0 %collective-permute-start = (bf16[512,128]{1,0:T(8,128)(2,1)S(1)}, bf16[512,128]{1,0:T(8,128)(2,1)S(1)}, u32[]{:S(2)}, u32[]{:S(2)}) collective-permute-start(bf16[512,128]{1,0:T(8,128)(2,1)S(1)} %get-tuple-element.72), channel_id=1, source_target_pairs={{0,1},{1,0},{2,3},{3,2},{4,5},{5,4},{6,7},{7,6},{8,9},{9,8},{10,11... | collective-permute-start | bytes 393224 | tf_op jit(solution)/shard_map/ppermute | solution.py:1020
  5.0 0.7 collective-permute-start.2
  5.8 4.3 %local.1 = (bf16[3072,256]{1,0:T(8,128)(2,1)S(1)}, bf16[3072,128]{1,0:T(8,128)(2,1)S(1)}, bf16[3072,128]{1,0:T(8,128)(2,1)S(1)}, bf16[3072,128]{1,0:T(8,128)(2,1...) custom-call(bf16[3072,256]{1,0:T(8,128)(2,1)S(1)} %copy-done, ...), custom_call_target="tpu_custom_call" | custom-call | tf_op jit(solution)/shard_map/local/pallas_call | solution.py:249
  10.2 0.4 collective-permute-done.1.near_rim
  10.5 3.0 %collective-permute-start.3 = (bf16[512,128]{1,0:T(8,128)(2,1)S(1)}, bf16[512,128]{1,0:T(8,128)(2,1)S(1)}, u32[]{:S(2)}, u32[]{:S(2)}) collective-permute-start(bf16[512,128]{1,0:T(8,128)(2,1)S(1)} %collective-permute-done.half_ref), channel_id=1, source_target_pairs={{0,2},{1,3},{2,0},{3,1},{4,6},{5,7},{6,4},{7,5},{8,10},{9,11},{10,... | collective-permute-start | bytes 393224 | tf_op jit(solution)/shard_map/ppermute | solution.py:945
  13.6 1.0 %collective-permute-done.3.other_half_ref = bf16[512,128]{1,0:T(8,128)(2,1)S(1)} collective-permute-done((bf16[512,128]{1,0:T(8,128)(2,1)S(1)}, bf16[512,128]{1,0:T(8,128)(2,1)S(1)}, u32[]{:S(2)}, u32[]{:S(2)}) %collective-permute-start.3) | collective-permute-done | bytes 131104 | tf_op jit(solution)/shard_map/ppermute | solution.py:945
  14.6 24.8 %layer.1 = (bf16[3136,128]{1,0:T(8,128)(2,1)S(1)}, bf16[3136,128]{1,0:T(8,128)(2,1)}, bf16[3072,1024]{1,0:T(8,128)(2,1)}, bf16[3072,256]{1,0:T(8,128)(2,1)}, f32...) custom-call(bf16[384,128]{1,0:T(8,128)(2,1)S(1)} %collective-permute-done.1.n, ...), custom_call_target="tpu_custom_call" | custom-call | tf_op jit(solution)/shard_map/layer/pallas_call | solution.py:677
  39.3 0.4 collective-permute-start.4
  39.8 2.2 %collective-permute-done.4 = bf16[3136,128]{1,0:T(8,128)(2,1)S(1)} collective-permute-done((bf16[3136,128]{1,0:T(8,128)(2,1)}, bf16[3136,128]{1,0:T(8,128)(2,1)S(1)}, u32[]{:S(2)}, u32[]{:S(2)}) %collective-permute-start.4) | collective-permute-done | bytes 802848 | tf_op jit(solution)/shard_map/ppermute | solution.py:945
  41.9 0.2 add_convert_fusion
  42.2 1.5 %collective-permute-start.5 = (bf16[784,128]{1,0:T(8,128)(2,1)S(1)}, bf16[784,128]{1,0:T(8,128)(2,1)S(1)}, u32[]{:S(2)}, u32[]{:S(2)}) collective-permute-start(bf16[784,128]{1,0:T(8,128)(2,1)S(1)} %get-tuple-element.136), channel_id=1, source_target_pairs={{0,1},{1,0},{2,10},{3,11},{4,5},{5,4},{6,14},{7,15},{8,9},{9,8},{1... | collective-permute-start | bytes 602120 | tf_op jit(solution)/shard_map/ppermute | solution.py:945
  43.7 1.5 %collective-permute-start.6 = (bf16[784,128]{1,0:T(8,128)(2,1)S(1)}, bf16[784,128]{1,0:T(8,128)(2,1)S(1)}, u32[]{:S(2)}, u32[]{:S(2)}) collective-permute-start(bf16[784,128]{1,0:T(8,128)(2,1)S(1)} %get-tuple-element.135), channel_id=1, source_target_pairs={{0,4},{1,5},{2,18},{3,19},{4,0},{5,1},{6,22},{7,23},{8,12},{9,13},... | collective-permute-start | bytes 602120 | tf_op jit(solution)/shard_map/ppermute | solution.py:945
  45.3 0.5 collective-permute-start.7
  45.7 5.6 %input_grad.1 = bf16[3072,256]{1,0:T(8,128)(2,1)} custom-call(bf16[3072,256]{1,0:T(8,128)(2,1)} %x_in.3, f32[3072,256]{1,0:T(8,128)} %get-tuple-element.95.mid_in, bf16[3072,768]{1,0:T(8,128)(2,1)} %get-tuple-element.96.dqkv_in, bf16[256,768]{1,0:T(8,128)(2,1)} %get-tuple-element.97.wqkv_in, f32[1,256]{1,0:T(1,128)S(1)} %bitcast.40), custom_call_target="tpu_custom_call" | custom-call | tf_op jit(solution)/shard_map/input_grad/pallas_call | solution.py:781
  51.4 0.4 collective-permute-done.7
  52.0 0.2 bitcast_dynamic-update-slice_fusion.6
  52.1 3.4 %collective-permute-start.10 = (bf16[784,128]{1,0:T(8,128)(2,1)S(1)}, bf16[784,128]{1,0:T(8,128)(2,1)S(1)}, u32[]{:S(2)}, u32[]{:S(2)}) collective-permute-start(bf16[784,128]{1,0:T(8,128)(2,1)S(1)} %get-tuple-element.102), channel_id=1, source_target_pairs={{0,24},{1,25},{2,7},{3,6},{4,28},{5,29},{6,3},{7,2},{8,16},{9,17},... | collective-permute-start | bytes 602120 | tf_op jit(solution)/shard_map/ppermute | solution.py:945
  55.5 1.1 %collective-permute-start.9 = (bf16[784,128]{1,0:T(8,128)(2,1)S(1)}, bf16[784,128]{1,0:T(8,128)(2,1)S(1)}, u32[]{:S(2)}, u32[]{:S(2)}) collective-permute-start(bf16[784,128]{1,0:T(8,128)(2,1)S(1)} %get-tuple-element.102), channel_id=1, source_target_pairs={{0,16},{1,17},{2,6},{3,7},{4,20},{5,21},{6,2},{7,3},{8,24},{9,25},... | collective-permute-start | bytes 602120 | tf_op jit(solution)/shard_map/ppermute | solution.py:945
  56.6 5.7 %mixed.1 = bf16[3072,256]{1,0:T(8,128)(2,1)} custom-call(bf16[3072,256]{1,0:T(8,128)(2,1)} %x_in.3, bf16[3072,256]{1,0:T(8,128)(2,1)} %get-tuple-element.103.att_in, bf16[3072,1024]{1,0:T(8,128)(2,1)} %get-tuple-element.104.act_in, bf16[256,256]{1,0:T(8,128)(2,1)} %get-tuple-element.105.wout_in, bf16[1024,256]{1,0:T(8,128)(2,1)} %down_in.1, ...), custom_call_target="tpu_custom_call" | custom-call | tf_op jit(solution)/shard_map/mixed/pallas_call | solution.py:781
  62.3 0.6 collective-permute-done.8
  62.9 2.5 %collective-permute-done.9 = bf16[784,128]{1,0:T(8,128)(2,1)S(1)} collective-permute-done((bf16[784,128]{1,0:T(8,128)(2,1)S(1)}, bf16[784,128]{1,0:T(8,128)(2,1)S(1)}, u32[]{:S(2)}, u32[]{:S(2)}) %collective-permute-start.9) | collective-permute-done | bytes 200736 | tf_op jit(solution)/shard_map/ppermute | solution.py:945
  65.7 1.2 %collective-permute-start.11 = (bf16[784,128]{1,0:T(8,128)(2,1)S(1)}, bf16[784,128]{1,0:T(8,128)(2,1)S(1)}, u32[]{:S(2)}, u32[]{:S(2)}) collective-permute-start(bf16[784,128]{1,0:T(8,128)(2,1)S(1)} %bitcast.51), channel_id=1, source_target_pairs={{0,1},{1,0},{2,10},{3,11},{4,5},{5,4},{6,14},{7,15},{8,9},{9,8},{1... | collective-permute-start | bytes 602120 | tf_op jit(solution)/shard_map/ppermute | solution.py:945
  67.0 1.5 %collective-permute-start.12 = (bf16[784,128]{1,0:T(8,128)(2,1)S(1)}, bf16[784,128]{1,0:T(8,128)(2,1)S(1)}, u32[]{:S(2)}, u32[]{:S(2)}) collective-permute-start(bf16[784,128]{1,0:T(8,128)(2,1)S(1)} %bitcast.52), channel_id=1, source_target_pairs={{0,4},{1,5},{2,18},{3,19},{4,0},{5,1},{6,22},{7,23},{8,12},{9,13},... | collective-permute-start | bytes 602120 | tf_op jit(solution)/shard_map/ppermute | solution.py:945
  68.5 0.8 collective-permute-start.13
  69.3 2.2 %collective-permute-done.11 = bf16[784,128]{1,0:T(8,128)(2,1)S(1)} collective-permute-done((bf16[784,128]{1,0:T(8,128)(2,1)S(1)}, bf16[784,128]{1,0:T(8,128)(2,1)S(1)}, u32[]{:S(2)}, u32[]{:S(2)}) %collective-permute-start.11) | collective-permute-done | bytes 200736 | tf_op jit(solution)/shard_map/ppermute | solution.py:945
  71.5 1.1 %collective-permute-done.12 = bf16[784,128]{1,0:T(8,128)(2,1)S(1)} collective-permute-done((bf16[784,128]{1,0:T(8,128)(2,1)S(1)}, bf16[784,128]{1,0:T(8,128)(2,1)S(1)}, u32[]{:S(2)}, u32[]{:S(2)}) %collective-permute-start.12) | collective-permute-done | bytes 200736 | tf_op jit(solution)/shard_map/ppermute | solution.py:945
  72.7 2.4 %collective-permute-done.13 = bf16[784,128]{1,0:T(8,128)(2,1)S(1)} collective-permute-done((bf16[784,128]{1,0:T(8,128)(2,1)S(1)}, bf16[784,128]{1,0:T(8,128)(2,1)S(1)}, u32[]{:S(2)}, u32[]{:S(2)}) %collective-permute-start.13) | collective-permute-done | bytes 200736 | tf_op jit(solution)/shard_map/ppermute | solution.py:945
  75.2 0.2 collective-permute-start.14
  75.4 1.1 %finish.1 = (f32[256,128]{1,0:T(8,128)}, f32[256,128]{1,0:T(8,128)}, f32[256,128]{1,0:T(8,128)}, f32[128,256]{1,0:T(8,128)}, f32[256,1024]{1,0:T(8,128)}, /*index=5*/f32[1024,256]{1,0:T(8,128)}) custom-call(bf16[3136,128]{1,0:T(8,128)(2,1)S(1)} %bitcast.36), custom_call_target="tpu_custom_call" | custom-call | tf_op jit(solution)/shard_map/finish/pallas_call | solution.py:908
  76.5 1.0 %collective-permute-done.14.mine_ref = bf16[3136,128]{1,0:T(8,128)(2,1)S(1)} collective-permute-done((bf16[3136,128]{1,0:T(8,128)(2,1)S(1)}, bf16[3136,128]{1,0:T(8,128)(2,1)S(1)}, u32[]{:S(2)}, u32[]{:S(2)}) %collective-permute-start.14) | collective-permute-done | bytes 802848 | tf_op jit(solution)/shard_map/ppermute | solution.py:945
  77.5 1.7 %finish_rest.1 = (f32[256]{0:T(256)}, f32[256]{0:T(256)}, f32[256]{0:T(256)}, f32[256]{0:T(256)}, f32[256]{0:T(256)}, /*index=5*/f32[1024]{0:T(1024)}, f32[256,1...) custom-call(bf16[3136,128]{1,0:T(8,128)(2,1)S(1)} %collective-permut, ...), custom_call_target="tpu_custom_call", output_to_operand_aliasing={{6}: (2, {}), {7}: (3, {}), {8}: (4, {}), {9}: (5, {}), {10... | custom-call | tf_op jit(solution)/shard_map/finish_rest/pallas_call | solution.py:908
  (45 shorter events, 0.7 us)
Async XLA Ops:
  0.6 5.0 %copy-start = (bf16[3072,256]{1,0:T(8,128)(2,1)S(1)}, bf16[3072,256]{1,0:T(8,128)(2,1)}, u32[]{:S(2)}) copy-start(bf16[3072,256]{1,0:T(8,128)(2,1)} %x_in.3) | copy-start | bytes 4718596
  0.7 5.0 %copy-start.1 = (bf16[256,128]{1,0:T(8,128)(2,1)S(1)}, bf16[256,128]{1,0:T(8,128)(2,1)}, u32[]{:S(2)}) copy-start(bf16[256,128]{1,0:T(8,128)(2,1)} %query_ref.5) | copy-start | bytes 196612
  0.7 5.0 %copy-start.2 = (bf16[256,128]{1,0:T(8,128)(2,1)S(1)}, bf16[256,128]{1,0:T(8,128)(2,1)}, u32[]{:S(2)}) copy-start(bf16[256,128]{1,0:T(8,128)(2,1)} %key_ref.5) | copy-start | bytes 196612
  0.7 5.0 %copy-start.3 = (bf16[256,128]{1,0:T(8,128)(2,1)S(1)}, bf16[256,128]{1,0:T(8,128)(2,1)}, u32[]{:S(2)}) copy-start(bf16[256,128]{1,0:T(8,128)(2,1)} %value_ref.5) | copy-start | bytes 196612
  0.7 5.0 %copy-start.6 = (f32[256]{0:T(256)S(1)}, f32[256]{0:T(256)}, u32[]{:S(2)}) copy-start(f32[256]{0:T(256)} %param.20) | copy-start | bytes 3076
  0.7 5.0 %copy-start.7 = (f32[256]{0:T(256)S(1)}, f32[256]{0:T(256)}, u32[]{:S(2)}) copy-start(f32[256]{0:T(256)} %param.21) | copy-start | bytes 3076
  0.7 5.0 %copy-start.12 = (s32[128]{0:T(128)S(1)}, s32[128]{0:T(128)}, u32[]{:S(2)}) copy-start(s32[128]{0:T(128)} %param.18) | copy-start | bytes 1540
  0.7 5.0 %copy-start.13 = (s32[128]{0:T(128)S(1)}, s32[128]{0:T(128)}, u32[]{:S(2)}) copy-start(s32[128]{0:T(128)} %param.19) | copy-start | bytes 1540
  1.9 8.6 %collective-permute-start = (bf16[512,128]{1,0:T(8,128)(2,1)S(1)}, bf16[512,128]{1,0:T(8,128)(2,1)S(1)}, u32[]{:S(2)}, u32[]{:S(2)}) collective-permute-start(bf16[512,128]{1,0:T(8,128)(2,1)S(1)} %get-tuple-element.72), channel_id=1, source_target_pairs={{0,1},{1,0},{2,3},{3,2},{4,5},{5,4},{6,7},{7,6},{8,9},{9,8},{10,11... | collective-permute-start | bytes 393224 | tf_op jit(solution)/shard_map/ppermute | solution.py:1020
  5.0 5.6 %collective-permute-start.1 = (bf16[384,128]{1,0:T(8,128)(2,1)S(1)}, bf16[384,128]{1,0:T(8,128)(2,1)S(1)}, u32[]{:S(2)}, u32[]{:S(2)}) collective-permute-start(bf16[384,128]{1,0:T(8,128)(2,1)S(1)} %get-tuple-element.73), channel_id=1, source_target_pairs={{0,1},{1,0},{2,3},{3,2},{4,5},{5,4},{6,7},{7,6},{8,9},{9,8},{10,11... | collective-permute-start | bytes 294920 | tf_op jit(solution)/shard_map/ppermute | solution.py:1023
  5.0 5.5 %collective-permute-start.2 = (bf16[384,128]{1,0:T(8,128)(2,1)S(1)}, bf16[384,128]{1,0:T(8,128)(2,1)S(1)}, u32[]{:S(2)}, u32[]{:S(2)}) collective-permute-start(bf16[384,128]{1,0:T(8,128)(2,1)S(1)} %get-tuple-element.74), channel_id=1, source_target_pairs={{1,2},{3,4},{5,6},{7,8},{9,10},{11,12},{13,14},{15,16},{17,18},{19... | collective-permute-start | bytes 294920 | tf_op jit(solution)/shard_map/ppermute | solution.py:1022
  5.8 8.8 %copy-start.4 = (bf16[256,1024]{1,0:T(8,128)(2,1)S(1)}, bf16[256,1024]{1,0:T(8,128)(2,1)}, u32[]{:S(2)}) copy-start(bf16[256,1024]{1,0:T(8,128)(2,1)} %up_ref.1) | copy-start | bytes 1572868
  5.8 8.8 %copy-start.5 = (bf16[128,256]{1,0:T(8,128)(2,1)S(1)}, bf16[128,256]{1,0:T(8,128)(2,1)}, u32[]{:S(2)}) copy-start(bf16[128,256]{1,0:T(8,128)(2,1)} %out_ref.3) | copy-start | bytes 196612
  5.8 8.8 %copy-start.8 = (f32[1024]{0:T(1024)S(1)}, f32[1024]{0:T(1024)}, u32[]{:S(2)}) copy-start(f32[1024]{0:T(1024)} %param.29) | copy-start | bytes 12292
  5.8 8.7 %copy-start.9 = (f32[256]{0:T(256)S(1)}, f32[256]{0:T(256)}, u32[]{:S(2)}) copy-start(f32[256]{0:T(256)} %param.26) | copy-start | bytes 3076
  5.8 8.7 %copy-start.10 = (f32[256]{0:T(256)S(1)}, f32[256]{0:T(256)}, u32[]{:S(2)}) copy-start(f32[256]{0:T(256)} %param.27) | copy-start | bytes 3076
  10.5 4.0 %collective-permute-start.3 = (bf16[512,128]{1,0:T(8,128)(2,1)S(1)}, bf16[512,128]{1,0:T(8,128)(2,1)S(1)}, u32[]{:S(2)}, u32[]{:S(2)}) collective-permute-start(bf16[512,128]{1,0:T(8,128)(2,1)S(1)} %collective-permute-done.half_ref), channel_id=1, source_target_pairs={{0,2},{1,3},{2,0},{3,1},{4,6},{5,7},{6,4},{7,5},{8,10},{9,11},{10,... | collective-permute-start | bytes 393224 | tf_op jit(solution)/shard_map/ppermute | solution.py:945
  39.3 2.6 %collective-permute-start.4 = (bf16[3136,128]{1,0:T(8,128)(2,1)}, bf16[3136,128]{1,0:T(8,128)(2,1)S(1)}, u32[]{:S(2)}, u32[]{:S(2)}) collective-permute-start(bf16[3136,128]{1,0:T(8,128)(2,1)} %get-tuple-element.93), channel_id=1, source_target_pairs={{0,2},{1,3},{2,0},{3,1},{4,6},{5,7},{6,4},{7,5},{8,10},{9,11},{10,... | collective-permute-start | bytes 2408456 | tf_op jit(solution)/shard_map/ppermute | solution.py:945
  42.2 9.2 %collective-permute-start.5 = (bf16[784,128]{1,0:T(8,128)(2,1)S(1)}, bf16[784,128]{1,0:T(8,128)(2,1)S(1)}, u32[]{:S(2)}, u32[]{:S(2)}) collective-permute-start(bf16[784,128]{1,0:T(8,128)(2,1)S(1)} %get-tuple-element.136), channel_id=1, source_target_pairs={{0,1},{1,0},{2,10},{3,11},{4,5},{5,4},{6,14},{7,15},{8,9},{9,8},{1... | collective-permute-start | bytes 602120 | tf_op jit(solution)/shard_map/ppermute | solution.py:945
  43.7 7.7 %collective-permute-start.6 = (bf16[784,128]{1,0:T(8,128)(2,1)S(1)}, bf16[784,128]{1,0:T(8,128)(2,1)S(1)}, u32[]{:S(2)}, u32[]{:S(2)}) collective-permute-start(bf16[784,128]{1,0:T(8,128)(2,1)S(1)} %get-tuple-element.135), channel_id=1, source_target_pairs={{0,4},{1,5},{2,18},{3,19},{4,0},{5,1},{6,22},{7,23},{8,12},{9,13},... | collective-permute-start | bytes 602120 | tf_op jit(solution)/shard_map/ppermute | solution.py:945
  45.3 6.6 %collective-permute-start.7 = (bf16[784,128]{1,0:T(8,128)(2,1)S(1)}, bf16[784,128]{1,0:T(8,128)(2,1)S(1)}, u32[]{:S(2)}, u32[]{:S(2)}) collective-permute-start(bf16[784,128]{1,0:T(8,128)(2,1)S(1)} %get-tuple-element.134), channel_id=1, source_target_pairs={{0,5},{1,4},{2,26},{3,27},{4,1},{5,0},{6,30},{7,31},{8,13},{9,12},... | collective-permute-start | bytes 602120 | tf_op jit(solution)/shard_map/ppermute | solution.py:945
  51.4 5.2 %copy-start.11 = (f32[256]{0:T(256)S(1)}, f32[256]{0:T(256)}, u32[]{:S(2)}) copy-start(f32[256]{0:T(256)} %param.31) | copy-start | bytes 3076
  52.1 10.2 %collective-permute-start.10 = (bf16[784,128]{1,0:T(8,128)(2,1)S(1)}, bf16[784,128]{1,0:T(8,128)(2,1)S(1)}, u32[]{:S(2)}, u32[]{:S(2)}) collective-permute-start(bf16[784,128]{1,0:T(8,128)(2,1)S(1)} %get-tuple-element.102), channel_id=1, source_target_pairs={{0,24},{1,25},{2,7},{3,6},{4,28},{5,29},{6,3},{7,2},{8,16},{9,17},... | collective-permute-start | bytes 602120 | tf_op jit(solution)/shard_map/ppermute | solution.py:945
  55.5 7.4 %collective-permute-start.8 = (bf16[784,128]{1,0:T(8,128)(2,1)S(1)}, bf16[784,128]{1,0:T(8,128)(2,1)S(1)}, u32[]{:S(2)}, u32[]{:S(2)}) collective-permute-start(bf16[784,128]{1,0:T(8,128)(2,1)S(1)} %get-tuple-element.102), channel_id=1, source_target_pairs={{0,8},{1,9},{2,3},{3,2},{4,12},{5,13},{6,7},{7,6},{8,0},{9,1},{10,... | collective-permute-start | bytes 602120 | tf_op jit(solution)/shard_map/ppermute | solution.py:945
  55.5 9.8 %collective-permute-start.9 = (bf16[784,128]{1,0:T(8,128)(2,1)S(1)}, bf16[784,128]{1,0:T(8,128)(2,1)S(1)}, u32[]{:S(2)}, u32[]{:S(2)}) collective-permute-start(bf16[784,128]{1,0:T(8,128)(2,1)S(1)} %get-tuple-element.102), channel_id=1, source_target_pairs={{0,16},{1,17},{2,6},{3,7},{4,20},{5,21},{6,2},{7,3},{8,24},{9,25},... | collective-permute-start | bytes 602120 | tf_op jit(solution)/shard_map/ppermute | solution.py:945
  65.7 5.8 %collective-permute-start.11 = (bf16[784,128]{1,0:T(8,128)(2,1)S(1)}, bf16[784,128]{1,0:T(8,128)(2,1)S(1)}, u32[]{:S(2)}, u32[]{:S(2)}) collective-permute-start(bf16[784,128]{1,0:T(8,128)(2,1)S(1)} %bitcast.51), channel_id=1, source_target_pairs={{0,1},{1,0},{2,10},{3,11},{4,5},{5,4},{6,14},{7,15},{8,9},{9,8},{1... | collective-permute-start | bytes 602120 | tf_op jit(solution)/shard_map/ppermute | solution.py:945
  67.0 5.7 %collective-permute-start.12 = (bf16[784,128]{1,0:T(8,128)(2,1)S(1)}, bf16[784,128]{1,0:T(8,128)(2,1)S(1)}, u32[]{:S(2)}, u32[]{:S(2)}) collective-permute-start(bf16[784,128]{1,0:T(8,128)(2,1)S(1)} %bitcast.52), channel_id=1, source_target_pairs={{0,4},{1,5},{2,18},{3,19},{4,0},{5,1},{6,22},{7,23},{8,12},{9,13},... | collective-permute-start | bytes 602120 | tf_op jit(solution)/shard_map/ppermute | solution.py:945
  68.5 6.6 %collective-permute-start.13 = (bf16[784,128]{1,0:T(8,128)(2,1)S(1)}, bf16[784,128]{1,0:T(8,128)(2,1)S(1)}, u32[]{:S(2)}, u32[]{:S(2)}) collective-permute-start(bf16[784,128]{1,0:T(8,128)(2,1)S(1)} %bitcast.53), channel_id=1, source_target_pairs={{0,5},{1,4},{2,26},{3,27},{4,1},{5,0},{6,30},{7,31},{8,13},{9,12},... | collective-permute-start | bytes 602120 | tf_op jit(solution)/shard_map/ppermute | solution.py:945
  75.2 2.4 %collective-permute-start.14 = (bf16[3136,128]{1,0:T(8,128)(2,1)S(1)}, bf16[3136,128]{1,0:T(8,128)(2,1)S(1)}, u32[]{:S(2)}, u32[]{:S(2)}) collective-permute-start(bf16[3136,128]{1,0:T(8,128)(2,1)S(1)} %bitcast.35), channel_id=1, source_target_pairs={{0,2},{1,3},{2,0},{3,1},{4,6},{5,7},{6,4},{7,5},{8,10},{9,11},{10,... | collective-permute-start | bytes 2408456 | tf_op jit(solution)/shard_map/ppermute | solution.py:945

commit v5 on v4

--- a/solution.py
+++ b/solution.py
@@ -79,11 +79,15 @@
     return [job for *_, job in sorted(marked, key=lambda item: item[:3])]
 
 
-VECTOR_ROWS = 64
+VECTOR_ROWS = 16
+
+
+def piece_rows(FF, D):
+    return 2 * FF * D // (8 * HEAD_DIM) + VECTOR_ROWS, 4 * D * D // (8 * HEAD_DIM)
 
 
 def half_rows(FF, D):
-    return (2 * FF * D + 4 * D * D) // (2 * HEAD_DIM) + VECTOR_ROWS
+    return 4 * sum(piece_rows(FF, D))
 
 
 def vector_slots(FF, D):
@@ -592,20 +596,25 @@
 
     wide = FF // 2
     halves = ((core, keep_ref), (1 - core, send_ref))
-    after_down = D // HEAD_DIM * wide
-    after_up = after_down + wide // HEAD_DIM * D
+    feed, heads = piece_rows(FF, D)
+    quarter = feed - VECTOR_ROWS
+
+    def spot(row):
+        return row // quarter * (feed + heads) + row % quarter
 
     def export_down(c, ref, f):
         at = pl.ds(pl.multiple_of(c * wide + f, D), D)
         block = (acc_down[:, at] * 0.5).astype(BF16).T
         for half in range(D // HEAD_DIM):
-            ref[half * wide + f : half * wide + f + D, :] = block[
+            to = spot(half * wide + f)
+            ref[to : to + D, :] = block[
                 :, half * HEAD_DIM : (half + 1) * HEAD_DIM
             ]
 
     def export_up(c, ref, n):
         at = pl.ds(pl.multiple_of(c * wide + n * HEAD_DIM, HEAD_DIM), HEAD_DIM)
-        ref[after_down + n * D : after_down + (n + 1) * D, :] = acc_up[:, at].astype(BF16)
+        to = spot(D // HEAD_DIM * wide + n * D)
+        ref[to : to + D, :] = acc_up[:, at].astype(BF16)
 
     def export_heads(c, ref, h, part):
         mine = pl.ds(pl.multiple_of(c * HEAD_DIM, HEAD_DIM), HEAD_DIM)
@@ -615,12 +624,17 @@
             block = acc_qkv[mine, at : at + HEAD_DIM]
         else:
             block = acc_out[h * HEAD_DIM : (h + 1) * HEAD_DIM, mine]
-        at = after_up + (true_head * 4 + part) * HEAD_DIM
-        ref[pl.ds(pl.multiple_of(at, HEAD_DIM), HEAD_DIM), :] = block.astype(BF16)
+        piece, shift = true_head + part // 2 * 2, part % 2 * HEAD_DIM
+        first = piece * (feed + heads) + feed + shift
+        second = part * (feed + heads) + feed + true_head * HEAD_DIM
+        at = jnp.where(c == 0, first, second)
+        ref[pl.ds(pl.multiple_of(at, 16), HEAD_DIM), :] = block.astype(BF16)
 
     def export_vectors(c, ref):
         flat = vec_rows[pl.ds(pl.multiple_of(c * 16, 16), 16), :].astype(BF16)
-        ref[after_up + 8 * HEAD_DIM :, :] = jnp.concatenate([flat] * (VECTOR_ROWS // 16))
+        for piece in range(4):
+            to = piece * (feed + heads) + quarter
+            ref[to : to + VECTOR_ROWS, :] = flat
 
     call = functools.partial
     exports = [call(export_down, c, ref, f) for c, ref in halves for f in range(0, wide, D)]
@@ -863,7 +877,6 @@
     outs, (down_buf, up_buf, heads_buf, vec_rows, sem) = refs[:6], refs[6:]
     query, key, value, out, up, down = outs
     core = lax.axis_index("seq") % 2
-    head = lax.axis_index("head")
     c = 1 - core if second else core
     wide = FF // 2
     copies = []
@@ -872,24 +885,26 @@
         copies.append(pltpu.make_async_copy(source, target, sem.at[len(copies)]))
         copies[-1].start()
 
+    feed = piece_rows(FF, D)[0]
+    quarter = feed - VECTOR_ROWS
     for half in range(D // HEAD_DIM):
-        down_buf[:, half * HEAD_DIM : (half + 1) * HEAD_DIM] = mine_ref[
-            half * wide : (half + 1) * wide, :
-        ].astype(F32)
+        at = half * wide // quarter * feed + half * wide % quarter
+        down_buf[:, half * HEAD_DIM : (half + 1) * HEAD_DIM] = mine_ref[at : at + wide, :].astype(F32)
     leave(down_buf, down.at[pl.ds(pl.multiple_of(c * wide, wide), wide)])
     start = D // HEAD_DIM * wide
     for n, f in enumerate(range(0, wide, HEAD_DIM)):
-        up_buf[:, f : f + HEAD_DIM] = mine_ref[start + n * D : start + (n + 1) * D, :].astype(F32)
+        at = (start + n * D) // quarter * feed + (start + n * D) % quarter
+        up_buf[:, f : f + HEAD_DIM] = mine_ref[at : at + D, :].astype(F32)
     leave(up_buf, up.at[:, pl.ds(pl.multiple_of(c * wide, wide), wide)])
-    start += wide // HEAD_DIM * D
+    start = 4 * feed
     own = pl.ds(pl.multiple_of(c * HEAD_DIM, HEAD_DIM), HEAD_DIM)
     for part, made in enumerate((query, key, value, out)):
-        at = pl.multiple_of(start + (head * 4 + part) * HEAD_DIM, HEAD_DIM)
-        heads_buf[part] = mine_ref[pl.ds(at, HEAD_DIM), :].astype(F32)
+        at = start + part * HEAD_DIM
+        heads_buf[part] = mine_ref[at : at + HEAD_DIM, :].astype(F32)
         leave(heads_buf.at[part], made.at[:, own] if part == 3 else made.at[own])
     if second:
         other_ref, made = vectors
-        at = start + 8 * HEAD_DIM
+        at = quarter
         for k, ref in ((c, mine_ref), (core, other_ref)):
             vec_rows[pl.ds(pl.multiple_of(k * 16, 16), 16), :] = ref[at : at + 16, :].astype(F32)
         for s, (n, cols) in enumerate(vector_slots(FF, D)):
@@ -935,7 +950,7 @@
     plane, rest = [bits[0], bits[2]], bits[3:]
     found = [plane] + [rest[i : i + 2] for i in range(0, len(rest), 2)]
     if len(found) > 1 and len(found[1]) == 2:
-        return [(found[0], found[1]), (found[1], found[0])] + [(masks, masks) for masks in found[2:]]
+        return [(found[0], found[1][::-1]), (found[1], found[0])] + [(masks, masks) for masks in found[2:]]
     return [(masks, masks) for masks in found]
 
 
@@ -945,7 +960,7 @@
     return lax.ppermute(value, BOTH, [(i, i ^ hops[i // 2 % 2]) for i in range(count)])
 
 
-def all_sum(value, side):
+def all_sum(value, side, FF, D):
     count = lax.axis_size("seq") * lax.axis_size("head")
     place = lax.axis_index("seq") * lax.axis_size("head") + lax.axis_index("head")
     width = value.shape[1]
@@ -986,9 +1001,28 @@
     for part in whole[1:]:
         total = total + part.astype(F32)
     value = total.astype(BF16)
-    for masks, code in steps[-2::-1]:
+    for masks, code in steps[-2:0:-1]:
         value = spread(value, masks, code, len(side)).reshape(-1, width)
-    return value, made
+    masks, code = steps[0]
+    feed, heads = piece_rows(FF, D)
+    head = lax.axis_index("head")
+    first_core = place & 2 == 0
+    mine, other = value[feed : feed + heads // 2], value[feed + heads // 2 :]
+    swap = jnp.logical_and(jnp.logical_not(first_core), head == 1)
+    value = jnp.concatenate([value[:feed], jnp.where(swap, other, mine), jnp.where(swap, mine, other)])
+    short = value[: feed + heads // 2]
+    found = [value, partners(short, masks, 1), partners(value, masks, 2), partners(short, masks, 3)]
+    whole = jnp.zeros((4 * feed, width), value.dtype)
+    by_half = jnp.zeros((2 * heads, width), value.dtype)
+    by_part = by_half
+    for k, part in enumerate(found):
+        whole = lax.dynamic_update_slice_in_dim(whole, part[:feed], (code ^ k) * feed, 0)
+        by_part = lax.dynamic_update_slice_in_dim(
+            by_part, part[feed : feed + heads // 2], (code ^ k) * (heads // 2), 0
+        )
+        if k % 2 == 0:
+            by_half = lax.dynamic_update_slice_in_dim(by_half, part[feed:], ((code ^ k) // 2) * heads, 0)
+    return jnp.concatenate([whole, jnp.where(first_core, by_half, by_part)]), made
 
 
 def across_cores(value):
@@ -1044,7 +1078,7 @@
         (lambda small: late(mixed_kernel, "mixed", (tokens, att, act, wout, down_weight), small), down_bias[None]),
     ]
     summed = (keep.astype(F32) + across_cores(send).astype(F32)).astype(BF16)
-    mine, (input_grad, mixed) = all_sum(summed, side)
+    mine, (input_grad, mixed) = all_sum(summed, side, FF, D)
     arrays = finish(mine, FF, D)
     gain1_grad, shift1_grad, gain2_grad, shift2_grad, down_bias_grad, up_bias_grad, *arrays = finish(
         across_cores(mine), FF, D, (mine, arrays)

time: 79.6 us -> 79.5 us (level)
  transfers between devices with their start and end apart: 15 -> 15, of which waited for: 10 -> 9; matrix products, arithmetic and copies ran while one was open for 0% -> 0% of each run, Pallas kernels for 21% -> 21%
where the time goes in v5:
time: 79.5 us; the launch traced here: 79.3 us
  Pallas kernels  44.7 us (56%)
  starting transfers between devices  18.9 us (24%)
  waiting for transfers between devices  13.2 us (17%)
  between operations  1.27 us (2%)
    pallas_call x1, Pallas kernels, layer(): pl.pallas_call(functools.partial(layer_kernel, rows), out_shape=(pltpu.VM...  25 us
    ppermute x12, starting transfers between devices, partners(): lax.ppermute(value, BOTH, [(i, i ^ hops[i // 2 % 2]) for i in range(count)])  15.1 us
    ppermute x12, waiting for transfers between devices, partners(): lax.ppermute(value, BOTH, [(i, i ^ hops[i // 2 % 2]) for i in range(count)])  12.8 us
    pallas_call x2, Pallas kernels, late(): pl.pallas_call(kernel, out_shape=pltpu.HBM((own, D), BF16), in_specs=[hbm...  11.4 us
    pallas_call x1, Pallas kernels, local(): pl.pallas_call(functools.partial(local_kernel, rows), out_shape=(pltpu.VM...  4.33 us
    ppermute x1, starting transfers between devices, shards(): half = lax.ppermute(half, 'head', [(0, 1), (1, 0)])  3.03 us
    pallas_call x2, Pallas kernels, finish(): pl.pallas_call(functools.partial(finish_kernel, FF, D, bool(first)), out_...  2.87 us
  transfers between devices with their start and end apart: 15, of which 9 were waited for; matrix products, arithmetic and copies ran while one was open for 0% of the time, Pallas kernels for 21%

profile of v5, /device:TPU:0, one launch (start us, length us, event | category | flops | bytes accessed | tf_op | source)
XLA Modules:
  0.0 79.3 jit_solution(4096585550799834881)
XLA Ops:
  0.7 1.2 %pack.1 = (bf16[512,128]{1,0:T(8,128)(2,1)S(1)}, bf16[384,128]{1,0:T(8,128)(2,1)S(1)}, bf16[384,128]{1,0:T(8,128)(2,1)S(1)}) custom-call(bf16[256,128]{1,0:T(8,128)(2,1)} %query_ref.5, bf16[256,128]{1,0:T(8,128)(2,1)} %key_ref.5, bf16[256,128]{1,0:T(8,128)(2,1)} %value_ref.5, bf16[128,256]{1,0:T(8,128)(2,1)} %out_ref.3, bf16[3072,256]{1,0:T(8,128)(2,1)} %x_in.3, ...), custom_call_target="tpu_custom_call" | custom-call | tf_op jit(solution)/shard_map/pack/pallas_call | solution.py:860
  1.9 3.0 %collective-permute-start = (bf16[512,128]{1,0:T(8,128)(2,1)S(1)}, bf16[512,128]{1,0:T(8,128)(2,1)S(1)}, u32[]{:S(2)}, u32[]{:S(2)}) collective-permute-start(bf16[512,128]{1,0:T(8,128)(2,1)S(1)} %get-tuple-element.72), channel_id=1, source_target_pairs={{0,1},{1,0},{2,3},{3,2},{4,5},{5,4},{6,7},{7,6},{8,9},{9,8},{10,11... | collective-permute-start | bytes 393224 | tf_op jit(solution)/shard_map/ppermute | solution.py:1054
  5.0 0.7 collective-permute-start.2
  5.8 4.3 %local.1 = (bf16[3072,256]{1,0:T(8,128)(2,1)S(1)}, bf16[3072,128]{1,0:T(8,128)(2,1)S(1)}, bf16[3072,128]{1,0:T(8,128)(2,1)S(1)}, bf16[3072,128]{1,0:T(8,128)(2,1...) custom-call(bf16[3072,256]{1,0:T(8,128)(2,1)S(1)} %copy-done, ...), custom_call_target="tpu_custom_call" | custom-call | tf_op jit(solution)/shard_map/local/pallas_call | solution.py:253
  10.2 0.4 collective-permute-done.1.near_rim
  10.5 3.0 %collective-permute-start.3 = (bf16[512,128]{1,0:T(8,128)(2,1)S(1)}, bf16[512,128]{1,0:T(8,128)(2,1)S(1)}, u32[]{:S(2)}, u32[]{:S(2)}) collective-permute-start(bf16[512,128]{1,0:T(8,128)(2,1)S(1)} %collective-permute-done.half_ref), channel_id=1, source_target_pairs={{0,2},{1,3},{2,0},{3,1},{4,6},{5,7},{6,4},{7,5},{8,10},{9,11},{10,... | collective-permute-start | bytes 393224 | tf_op jit(solution)/shard_map/ppermute | solution.py:960
  13.6 1.0 %collective-permute-done.3.other_half_ref = bf16[512,128]{1,0:T(8,128)(2,1)S(1)} collective-permute-done((bf16[512,128]{1,0:T(8,128)(2,1)S(1)}, bf16[512,128]{1,0:T(8,128)(2,1)S(1)}, u32[]{:S(2)}, u32[]{:S(2)}) %collective-permute-start.3) | collective-permute-done | bytes 131104 | tf_op jit(solution)/shard_map/ppermute | solution.py:960
  14.6 25.0 %layer.1 = (bf16[3136,128]{1,0:T(8,128)(2,1)S(1)}, bf16[3136,128]{1,0:T(8,128)(2,1)}, bf16[3072,1024]{1,0:T(8,128)(2,1)}, bf16[3072,256]{1,0:T(8,128)(2,1)}, f32...) custom-call(bf16[384,128]{1,0:T(8,128)(2,1)S(1)} %collective-permute-done.1.n, ...), custom_call_target="tpu_custom_call" | custom-call | tf_op jit(solution)/shard_map/layer/pallas_call | solution.py:691
  39.6 0.4 collective-permute-start.4
  40.0 2.2 %collective-permute-done.4 = bf16[3136,128]{1,0:T(8,128)(2,1)S(1)} collective-permute-done((bf16[3136,128]{1,0:T(8,128)(2,1)}, bf16[3136,128]{1,0:T(8,128)(2,1)S(1)}, u32[]{:S(2)}, u32[]{:S(2)}) %collective-permute-start.4) | collective-permute-done | bytes 802848 | tf_op jit(solution)/shard_map/ppermute | solution.py:960
  42.2 0.2 add_convert_fusion
  42.4 1.5 %collective-permute-start.5 = (bf16[784,128]{1,0:T(8,128)(2,1)S(1)}, bf16[784,128]{1,0:T(8,128)(2,1)S(1)}, u32[]{:S(2)}, u32[]{:S(2)}) collective-permute-start(bf16[784,128]{1,0:T(8,128)(2,1)S(1)} %get-tuple-element.136), channel_id=1, source_target_pairs={{0,1},{1,0},{2,18},{3,19},{4,5},{5,4},{6,22},{7,23},{8,9},{9,8},{1... | collective-permute-start | bytes 602120 | tf_op jit(solution)/shard_map/ppermute | solution.py:960
  43.9 1.5 %collective-permute-start.6 = (bf16[784,128]{1,0:T(8,128)(2,1)S(1)}, bf16[784,128]{1,0:T(8,128)(2,1)S(1)}, u32[]{:S(2)}, u32[]{:S(2)}) collective-permute-start(bf16[784,128]{1,0:T(8,128)(2,1)S(1)} %get-tuple-element.135), channel_id=1, source_target_pairs={{0,4},{1,5},{2,10},{3,11},{4,0},{5,1},{6,14},{7,15},{8,12},{9,13},... | collective-permute-start | bytes 602120 | tf_op jit(solution)/shard_map/ppermute | solution.py:960
  45.5 0.5 collective-permute-start.7
  46.0 5.7 %input_grad.1 = bf16[3072,256]{1,0:T(8,128)(2,1)} custom-call(bf16[3072,256]{1,0:T(8,128)(2,1)} %x_in.3, f32[3072,256]{1,0:T(8,128)} %get-tuple-element.95.mid_in, bf16[3072,768]{1,0:T(8,128)(2,1)} %get-tuple-element.96.dqkv_in, bf16[256,768]{1,0:T(8,128)(2,1)} %get-tuple-element.97.wqkv_in, f32[1,256]{1,0:T(1,128)S(1)} %bitcast.38), custom_call_target="tpu_custom_call" | custom-call | tf_op jit(solution)/shard_map/input_grad/pallas_call | solution.py:795
  51.7 0.4 collective-permute-done.7
  52.1 0.1 broadcast_in_dim.55
  52.2 0.2 bitcast_dynamic-update-slice_fusion.3
  52.4 3.4 %collective-permute-start.10 = (bf16[784,128]{1,0:T(8,128)(2,1)S(1)}, bf16[784,128]{1,0:T(8,128)(2,1)S(1)}, u32[]{:S(2)}, u32[]{:S(2)}) collective-permute-start(bf16[784,128]{1,0:T(8,128)(2,1)S(1)} %get-tuple-element.102), channel_id=1, source_target_pairs={{0,24},{1,25},{2,7},{3,6},{4,28},{5,29},{6,3},{7,2},{8,16},{9,17},... | collective-permute-start | bytes 602120 | tf_op jit(solution)/shard_map/ppermute | solution.py:960
  55.8 1.1 %collective-permute-start.9 = (bf16[784,128]{1,0:T(8,128)(2,1)S(1)}, bf16[784,128]{1,0:T(8,128)(2,1)S(1)}, u32[]{:S(2)}, u32[]{:S(2)}) collective-permute-start(bf16[784,128]{1,0:T(8,128)(2,1)S(1)} %get-tuple-element.102), channel_id=1, source_target_pairs={{0,16},{1,17},{2,6},{3,7},{4,20},{5,21},{6,2},{7,3},{8,24},{9,25},... | collective-permute-start | bytes 602120 | tf_op jit(solution)/shard_map/ppermute | solution.py:960
  56.8 5.7 %mixed.1 = bf16[3072,256]{1,0:T(8,128)(2,1)} custom-call(bf16[3072,256]{1,0:T(8,128)(2,1)} %x_in.3, bf16[3072,256]{1,0:T(8,128)(2,1)} %get-tuple-element.103.att_in, bf16[3072,1024]{1,0:T(8,128)(2,1)} %get-tuple-element.104.act_in, bf16[256,256]{1,0:T(8,128)(2,1)} %get-tuple-element.105.wout_in, bf16[1024,256]{1,0:T(8,128)(2,1)} %down_in.1, ...), custom_call_target="tpu_custom_call" | custom-call | tf_op jit(solution)/shard_map/mixed/pallas_call | solution.py:795
  62.5 0.6 collective-permute-done.8
  63.1 2.5 %collective-permute-done.9 = bf16[784,128]{1,0:T(8,128)(2,1)S(1)} collective-permute-done((bf16[784,128]{1,0:T(8,128)(2,1)S(1)}, bf16[784,128]{1,0:T(8,128)(2,1)S(1)}, u32[]{:S(2)}, u32[]{:S(2)}) %collective-permute-start.9) | collective-permute-done | bytes 200736 | tf_op jit(solution)/shard_map/ppermute | solution.py:960
  65.7 0.1 add_convert_fusion.1
  65.9 1.2 %collective-permute-start.11 = (bf16[656,128]{1,0:T(8,128)(2,1)S(1)}, bf16[656,128]{1,0:T(8,128)(2,1)S(1)}, u32[]{:S(2)}, u32[]{:S(2)}) collective-permute-start(bf16[656,128]{1,0:T(8,128)(2,1)S(1)} %pad_maximum_fusion.2), channel_id=1, source_target_pairs={{0,1},{1,0},{2,18},{3,19},{4,5},{5,4},{6,22},{7,23},{8,9},{9,8},{1... | collective-permute-start | bytes 503816 | tf_op jit(solution)/shard_map/ppermute | solution.py:960
  67.2 1.5 %collective-permute-start.13 = (bf16[656,128]{1,0:T(8,128)(2,1)S(1)}, bf16[656,128]{1,0:T(8,128)(2,1)S(1)}, u32[]{:S(2)}, u32[]{:S(2)}) collective-permute-start(bf16[656,128]{1,0:T(8,128)(2,1)S(1)} %pad_maximum_fusion.2), channel_id=1, source_target_pairs={{0,5},{1,4},{2,26},{3,27},{4,1},{5,0},{6,30},{7,31},{8,13},{9,12},... | collective-permute-start | bytes 503816 | tf_op jit(solution)/shard_map/ppermute | solution.py:960
  68.7 0.9 %collective-permute-start.12 = (bf16[784,128]{1,0:T(8,128)(2,1)S(1)}, bf16[784,128]{1,0:T(8,128)(2,1)S(1)}, u32[]{:S(2)}, u32[]{:S(2)}) collective-permute-start(bf16[784,128]{1,0:T(8,128)(2,1)S(1)} %pad_maximum_fusion.1), channel_id=1, source_target_pairs={{0,4},{1,5},{2,10},{3,11},{4,0},{5,1},{6,14},{7,15},{8,12},{9,13},... | collective-permute-start | bytes 602120 | tf_op jit(solution)/shard_map/ppermute | solution.py:960
  69.7 1.6 %collective-permute-done.11 = bf16[656,128]{1,0:T(8,128)(2,1)S(1)} collective-permute-done((bf16[656,128]{1,0:T(8,128)(2,1)S(1)}, bf16[656,128]{1,0:T(8,128)(2,1)S(1)}, u32[]{:S(2)}, u32[]{:S(2)}) %collective-permute-start.11) | collective-permute-done | bytes 167968 | tf_op jit(solution)/shard_map/ppermute | solution.py:960
  71.4 3.6 %collective-permute-done.12 = bf16[784,128]{1,0:T(8,128)(2,1)S(1)} collective-permute-done((bf16[784,128]{1,0:T(8,128)(2,1)S(1)}, bf16[784,128]{1,0:T(8,128)(2,1)S(1)}, u32[]{:S(2)}, u32[]{:S(2)}) %collective-permute-start.12) | collective-permute-done | bytes 200736 | tf_op jit(solution)/shard_map/ppermute | solution.py:960
  75.3 1.1 %finish.1 = (f32[256,128]{1,0:T(8,128)}, f32[256,128]{1,0:T(8,128)}, f32[256,128]{1,0:T(8,128)}, f32[128,256]{1,0:T(8,128)}, f32[256,1024]{1,0:T(8,128)}, /*index=5*/f32[1024,256]{1,0:T(8,128)}) custom-call(bf16[2624,128]{1,0:T(8,128)(2,1)S(1)} %pad_maximum_fusion.mine_ref.refs_0_), custom_call_target="tpu_custom_call" | custom-call | tf_op jit(solution)/shard_map/finish/pallas_call | solution.py:923
  76.4 1.0 %collective-permute-done.14.mine_ref = bf16[2624,128]{1,0:T(8,128)(2,1)S(1)} collective-permute-done((bf16[2624,128]{1,0:T(8,128)(2,1)S(1)}, bf16[2624,128]{1,0:T(8,128)(2,1)S(1)}, u32[]{:S(2)}, u32[]{:S(2)}) %collective-permute-start.14) | collective-permute-done | bytes 671776 | tf_op jit(solution)/shard_map/ppermute | solution.py:960
  77.4 1.7 %finish_rest.1 = (f32[256]{0:T(256)}, f32[256]{0:T(256)}, f32[256]{0:T(256)}, f32[256]{0:T(256)}, f32[256]{0:T(256)}, /*index=5*/f32[1024]{0:T(1024)}, f32[256,1...) custom-call(bf16[2624,128]{1,0:T(8,128)(2,1)S(1)} %collective-permut, ...), custom_call_target="tpu_custom_call", output_to_operand_aliasing={{6}: (2, {}), {7}: (3, {}), {8}: (4, {}), {9}: (5, {}), {10... | custom-call | tf_op jit(solution)/shard_map/finish_rest/pallas_call | solution.py:923
  (60 shorter events, 0.8 us)
Async XLA Ops:
  0.6 5.0 %copy-start = (bf16[3072,256]{1,0:T(8,128)(2,1)S(1)}, bf16[3072,256]{1,0:T(8,128)(2,1)}, u32[]{:S(2)}) copy-start(bf16[3072,256]{1,0:T(8,128)(2,1)} %x_in.3) | copy-start | bytes 4718596
  0.7 5.0 %copy-start.1 = (bf16[256,128]{1,0:T(8,128)(2,1)S(1)}, bf16[256,128]{1,0:T(8,128)(2,1)}, u32[]{:S(2)}) copy-start(bf16[256,128]{1,0:T(8,128)(2,1)} %query_ref.5) | copy-start | bytes 196612
  0.7 5.0 %copy-start.2 = (bf16[256,128]{1,0:T(8,128)(2,1)S(1)}, bf16[256,128]{1,0:T(8,128)(2,1)}, u32[]{:S(2)}) copy-start(bf16[256,128]{1,0:T(8,128)(2,1)} %key_ref.5) | copy-start | bytes 196612
  0.7 5.0 %copy-start.3 = (bf16[256,128]{1,0:T(8,128)(2,1)S(1)}, bf16[256,128]{1,0:T(8,128)(2,1)}, u32[]{:S(2)}) copy-start(bf16[256,128]{1,0:T(8,128)(2,1)} %value_ref.5) | copy-start | bytes 196612
  0.7 5.0 %copy-start.6 = (f32[256]{0:T(256)S(1)}, f32[256]{0:T(256)}, u32[]{:S(2)}) copy-start(f32[256]{0:T(256)} %param.20) | copy-start | bytes 3076
  0.7 5.0 %copy-start.7 = (f32[256]{0:T(256)S(1)}, f32[256]{0:T(256)}, u32[]{:S(2)}) copy-start(f32[256]{0:T(256)} %param.21) | copy-start | bytes 3076
  0.7 5.0 %copy-start.12 = (s32[128]{0:T(128)S(1)}, s32[128]{0:T(128)}, u32[]{:S(2)}) copy-start(s32[128]{0:T(128)} %param.18) | copy-start | bytes 1540
  0.7 5.0 %copy-start.13 = (s32[128]{0:T(128)S(1)}, s32[128]{0:T(128)}, u32[]{:S(2)}) copy-start(s32[128]{0:T(128)} %param.19) | copy-start | bytes 1540
  1.9 8.6 %collective-permute-start = (bf16[512,128]{1,0:T(8,128)(2,1)S(1)}, bf16[512,128]{1,0:T(8,128)(2,1)S(1)}, u32[]{:S(2)}, u32[]{:S(2)}) collective-permute-start(bf16[512,128]{1,0:T(8,128)(2,1)S(1)} %get-tuple-element.72), channel_id=1, source_target_pairs={{0,1},{1,0},{2,3},{3,2},{4,5},{5,4},{6,7},{7,6},{8,9},{9,8},{10,11... | collective-permute-start | bytes 393224 | tf_op jit(solution)/shard_map/ppermute | solution.py:1054
  5.0 5.6 %collective-permute-start.1 = (bf16[384,128]{1,0:T(8,128)(2,1)S(1)}, bf16[384,128]{1,0:T(8,128)(2,1)S(1)}, u32[]{:S(2)}, u32[]{:S(2)}) collective-permute-start(bf16[384,128]{1,0:T(8,128)(2,1)S(1)} %get-tuple-element.73), channel_id=1, source_target_pairs={{0,1},{1,0},{2,3},{3,2},{4,5},{5,4},{6,7},{7,6},{8,9},{9,8},{10,11... | collective-permute-start | bytes 294920 | tf_op jit(solution)/shard_map/ppermute | solution.py:1057
  5.0 5.5 %collective-permute-start.2 = (bf16[384,128]{1,0:T(8,128)(2,1)S(1)}, bf16[384,128]{1,0:T(8,128)(2,1)S(1)}, u32[]{:S(2)}, u32[]{:S(2)}) collective-permute-start(bf16[384,128]{1,0:T(8,128)(2,1)S(1)} %get-tuple-element.74), channel_id=1, source_target_pairs={{1,2},{3,4},{5,6},{7,8},{9,10},{11,12},{13,14},{15,16},{17,18},{19... | collective-permute-start | bytes 294920 | tf_op jit(solution)/shard_map/ppermute | solution.py:1056
  5.8 8.8 %copy-start.4 = (bf16[256,1024]{1,0:T(8,128)(2,1)S(1)}, bf16[256,1024]{1,0:T(8,128)(2,1)}, u32[]{:S(2)}) copy-start(bf16[256,1024]{1,0:T(8,128)(2,1)} %up_ref.1) | copy-start | bytes 1572868
  5.8 8.8 %copy-start.5 = (bf16[128,256]{1,0:T(8,128)(2,1)S(1)}, bf16[128,256]{1,0:T(8,128)(2,1)}, u32[]{:S(2)}) copy-start(bf16[128,256]{1,0:T(8,128)(2,1)} %out_ref.3) | copy-start | bytes 196612
  5.8 8.8 %copy-start.8 = (f32[1024]{0:T(1024)S(1)}, f32[1024]{0:T(1024)}, u32[]{:S(2)}) copy-start(f32[1024]{0:T(1024)} %param.29) | copy-start | bytes 12292
  5.8 8.7 %copy-start.9 = (f32[256]{0:T(256)S(1)}, f32[256]{0:T(256)}, u32[]{:S(2)}) copy-start(f32[256]{0:T(256)} %param.26) | copy-start | bytes 3076
  5.8 8.7 %copy-start.10 = (f32[256]{0:T(256)S(1)}, f32[256]{0:T(256)}, u32[]{:S(2)}) copy-start(f32[256]{0:T(256)} %param.27) | copy-start | bytes 3076
  10.5 4.0 %collective-permute-start.3 = (bf16[512,128]{1,0:T(8,128)(2,1)S(1)}, bf16[512,128]{1,0:T(8,128)(2,1)S(1)}, u32[]{:S(2)}, u32[]{:S(2)}) collective-permute-start(bf16[512,128]{1,0:T(8,128)(2,1)S(1)} %collective-permute-done.half_ref), channel_id=1, source_target_pairs={{0,2},{1,3},{2,0},{3,1},{4,6},{5,7},{6,4},{7,5},{8,10},{9,11},{10,... | collective-permute-start | bytes 393224 | tf_op jit(solution)/shard_map/ppermute | solution.py:960
  39.6 2.6 %collective-permute-start.4 = (bf16[3136,128]{1,0:T(8,128)(2,1)}, bf16[3136,128]{1,0:T(8,128)(2,1)S(1)}, u32[]{:S(2)}, u32[]{:S(2)}) collective-permute-start(bf16[3136,128]{1,0:T(8,128)(2,1)} %get-tuple-element.93), channel_id=1, source_target_pairs={{0,2},{1,3},{2,0},{3,1},{4,6},{5,7},{6,4},{7,5},{8,10},{9,11},{10,... | collective-permute-start | bytes 2408456 | tf_op jit(solution)/shard_map/ppermute | solution.py:960
  42.4 9.2 %collective-permute-start.5 = (bf16[784,128]{1,0:T(8,128)(2,1)S(1)}, bf16[784,128]{1,0:T(8,128)(2,1)S(1)}, u32[]{:S(2)}, u32[]{:S(2)}) collective-permute-start(bf16[784,128]{1,0:T(8,128)(2,1)S(1)} %get-tuple-element.136), channel_id=1, source_target_pairs={{0,1},{1,0},{2,18},{3,19},{4,5},{5,4},{6,22},{7,23},{8,9},{9,8},{1... | collective-permute-start | bytes 602120 | tf_op jit(solution)/shard_map/ppermute | solution.py:960
  43.9 7.7 %collective-permute-start.6 = (bf16[784,128]{1,0:T(8,128)(2,1)S(1)}, bf16[784,128]{1,0:T(8,128)(2,1)S(1)}, u32[]{:S(2)}, u32[]{:S(2)}) collective-permute-start(bf16[784,128]{1,0:T(8,128)(2,1)S(1)} %get-tuple-element.135), channel_id=1, source_target_pairs={{0,4},{1,5},{2,10},{3,11},{4,0},{5,1},{6,14},{7,15},{8,12},{9,13},... | collective-permute-start | bytes 602120 | tf_op jit(solution)/shard_map/ppermute | solution.py:960
  45.5 6.6 %collective-permute-start.7 = (bf16[784,128]{1,0:T(8,128)(2,1)S(1)}, bf16[784,128]{1,0:T(8,128)(2,1)S(1)}, u32[]{:S(2)}, u32[]{:S(2)}) collective-permute-start(bf16[784,128]{1,0:T(8,128)(2,1)S(1)} %get-tuple-element.134), channel_id=1, source_target_pairs={{0,5},{1,4},{2,26},{3,27},{4,1},{5,0},{6,30},{7,31},{8,13},{9,12},... | collective-permute-start | bytes 602120 | tf_op jit(solution)/shard_map/ppermute | solution.py:960
  51.6 5.2 %copy-start.11 = (f32[256]{0:T(256)S(1)}, f32[256]{0:T(256)}, u32[]{:S(2)}) copy-start(f32[256]{0:T(256)} %param.31) | copy-start | bytes 3076
  52.4 10.2 %collective-permute-start.10 = (bf16[784,128]{1,0:T(8,128)(2,1)S(1)}, bf16[784,128]{1,0:T(8,128)(2,1)S(1)}, u32[]{:S(2)}, u32[]{:S(2)}) collective-permute-start(bf16[784,128]{1,0:T(8,128)(2,1)S(1)} %get-tuple-element.102), channel_id=1, source_target_pairs={{0,24},{1,25},{2,7},{3,6},{4,28},{5,29},{6,3},{7,2},{8,16},{9,17},... | collective-permute-start | bytes 602120 | tf_op jit(solution)/shard_map/ppermute | solution.py:960
  55.7 7.4 %collective-permute-start.8 = (bf16[784,128]{1,0:T(8,128)(2,1)S(1)}, bf16[784,128]{1,0:T(8,128)(2,1)S(1)}, u32[]{:S(2)}, u32[]{:S(2)}) collective-permute-start(bf16[784,128]{1,0:T(8,128)(2,1)S(1)} %get-tuple-element.102), channel_id=1, source_target_pairs={{0,8},{1,9},{2,3},{3,2},{4,12},{5,13},{6,7},{7,6},{8,0},{9,1},{10,... | collective-permute-start | bytes 602120 | tf_op jit(solution)/shard_map/ppermute | solution.py:960
  55.8 9.8 %collective-permute-start.9 = (bf16[784,128]{1,0:T(8,128)(2,1)S(1)}, bf16[784,128]{1,0:T(8,128)(2,1)S(1)}, u32[]{:S(2)}, u32[]{:S(2)}) collective-permute-start(bf16[784,128]{1,0:T(8,128)(2,1)S(1)} %get-tuple-element.102), channel_id=1, source_target_pairs={{0,16},{1,17},{2,6},{3,7},{4,20},{5,21},{6,2},{7,3},{8,24},{9,25},... | collective-permute-start | bytes 602120 | tf_op jit(solution)/shard_map/ppermute | solution.py:960
  65.9 5.4 %collective-permute-start.11 = (bf16[656,128]{1,0:T(8,128)(2,1)S(1)}, bf16[656,128]{1,0:T(8,128)(2,1)S(1)}, u32[]{:S(2)}, u32[]{:S(2)}) collective-permute-start(bf16[656,128]{1,0:T(8,128)(2,1)S(1)} %pad_maximum_fusion.2), channel_id=1, source_target_pairs={{0,1},{1,0},{2,18},{3,19},{4,5},{5,4},{6,22},{7,23},{8,9},{9,8},{1... | collective-permute-start | bytes 503816 | tf_op jit(solution)/shard_map/ppermute | solution.py:960
  67.2 7.8 %collective-permute-start.13 = (bf16[656,128]{1,0:T(8,128)(2,1)S(1)}, bf16[656,128]{1,0:T(8,128)(2,1)S(1)}, u32[]{:S(2)}, u32[]{:S(2)}) collective-permute-start(bf16[656,128]{1,0:T(8,128)(2,1)S(1)} %pad_maximum_fusion.2), channel_id=1, source_target_pairs={{0,5},{1,4},{2,26},{3,27},{4,1},{5,0},{6,30},{7,31},{8,13},{9,12},... | collective-permute-start | bytes 503816 | tf_op jit(solution)/shard_map/ppermute | solution.py:960
  68.7 6.3 %collective-permute-start.12 = (bf16[784,128]{1,0:T(8,128)(2,1)S(1)}, bf16[784,128]{1,0:T(8,128)(2,1)S(1)}, u32[]{:S(2)}, u32[]{:S(2)}) collective-permute-start(bf16[784,128]{1,0:T(8,128)(2,1)S(1)} %pad_maximum_fusion.1), channel_id=1, source_target_pairs={{0,4},{1,5},{2,10},{3,11},{4,0},{5,1},{6,14},{7,15},{8,12},{9,13},... | collective-permute-start | bytes 602120 | tf_op jit(solution)/shard_map/ppermute | solution.py:960
  75.2 2.2 %collective-permute-start.14 = (bf16[2624,128]{1,0:T(8,128)(2,1)S(1)}, bf16[2624,128]{1,0:T(8,128)(2,1)S(1)}, u32[]{:S(2)}, u32[]{:S(2)}) collective-permute-start(bf16[2624,128]{1,0:T(8,128)(2,1)S(1)} %pad_maximum_fusion.mine_ref.refs_0_), channel_id=1, source_target_pairs={{0,2},{1,3},{2,0},{3,1},{4,6},{5,7},{6,4},{7,5},{8,10},{9,11},{10,... | collective-permute-start | bytes 2015240 | tf_op jit(solution)/shard_map/ppermute | solution.py:960

commit v6 on v5

--- a/solution.py
+++ b/solution.py
@@ -23,7 +23,7 @@
 ROWS = (((0,), (0,)), ((), ()))
 
 CHUNK = 8
-LAG = 4
+LAG = 6
 
 
 def dot(a, b):
@@ -124,12 +124,12 @@
     )
 
 
-def staggered(units, *kinds):
+def staggered(units, *kinds, lag=LAG):
     jobs = []
-    for t in range(len(units) + LAG * (len(kinds) - 1)):
+    for t in range(len(units) + lag * (len(kinds) - 1)):
         for k, kind in enumerate(kinds):
-            if 0 <= t - LAG * k < len(units):
-                jobs.append(functools.partial(kind, *units[t - LAG * k]))
+            if 0 <= t - lag * k < len(units):
+                jobs.append(functools.partial(kind, *units[t - lag * k]))
     return jobs
 
 
@@ -226,7 +226,7 @@
         values = vbuf[(r - 1) * WINDOW : (r + 1) * WINDOW, :]
         att[r * WINDOW : (r + 1) * WINDOW, :] = window_sum(held.pop(r), values, current_t).astype(BF16)
 
-    do(staggered([(r,) for r in range(1, rows)], score, soften, gather))
+    do(staggered([(r,) for r in range(1, rows)], score, soften, gather, lag=2))
     for copy in later:
         copy.wait()
     cot_t[...] = cot_ref[...].T
@@ -996,11 +996,12 @@
         for part in exchange(parts, pick, masks, number):
             total = total + part.astype(F32)
         value = total.astype(BF16)
-    whole = spread(value, *steps[-1], len(steps) - 1)
-    total = whole[0].astype(F32)
-    for part in whole[1:]:
-        total = total + part.astype(F32)
-    value = total.astype(BF16)
+    masks, _ = steps[-1]
+    parts = [value] + exchange(value, lambda v, k: v, masks, len(steps) - 1)
+    parts = [part.astype(F32) for part in parts]
+    while len(parts) > 1:
+        parts = [a + b for a, b in zip(parts[::2], parts[1::2])]
+    value = parts[0].astype(BF16)
     for masks, code in steps[-2:0:-1]:
         value = spread(value, masks, code, len(side)).reshape(-1, width)
     masks, code = steps[0]

time: 79.5 us -> 79.1 us (level)
  no operation moved by 1% of the time
where the time goes in v6:
time: 79.1 us; the launch traced here: 78.9 us
  Pallas kernels  44.5 us (56%)
  starting transfers between devices  18.9 us (24%)
  waiting for transfers between devices  13.3 us (17%)
  between operations  1.22 us (2%)
    pallas_call x1, Pallas kernels, layer(): pl.pallas_call(functools.partial(layer_kernel, rows), out_shape=(pltpu.VM...  24.8 us
    ppermute x12, starting transfers between devices, partners(): lax.ppermute(value, BOTH, [(i, i ^ hops[i // 2 % 2]) for i in range(count)])  15.1 us
    ppermute x12, waiting for transfers between devices, partners(): lax.ppermute(value, BOTH, [(i, i ^ hops[i // 2 % 2]) for i in range(count)])  12.9 us
    pallas_call x2, Pallas kernels, late(): pl.pallas_call(kernel, out_shape=pltpu.HBM((own, D), BF16), in_specs=[hbm...  11.4 us
    pallas_call x1, Pallas kernels, local(): pl.pallas_call(functools.partial(local_kernel, rows), out_shape=(pltpu.VM...  4.31 us
    ppermute x1, starting transfers between devices, shards(): half = lax.ppermute(half, 'head', [(0, 1), (1, 0)])  3.03 us
    pallas_call x2, Pallas kernels, finish(): pl.pallas_call(functools.partial(finish_kernel, FF, D, bool(first)), out_...  2.87 us
  transfers between devices with their start and end apart: 15, of which 9 were waited for; matrix products, arithmetic and copies ran while one was open for 0% of the time, Pallas kernels for 21%

profile of v6, /device:TPU:0, one launch (start us, length us, event | category | flops | bytes accessed | tf_op | source)
XLA Modules:
  0.0 78.9 jit_solution(15811585876018318773)
XLA Ops:
  0.7 1.2 %pack.1 = (bf16[512,128]{1,0:T(8,128)(2,1)S(1)}, bf16[384,128]{1,0:T(8,128)(2,1)S(1)}, bf16[384,128]{1,0:T(8,128)(2,1)S(1)}) custom-call(bf16[256,128]{1,0:T(8,128)(2,1)} %query_ref.5, bf16[256,128]{1,0:T(8,128)(2,1)} %key_ref.5, bf16[256,128]{1,0:T(8,128)(2,1)} %value_ref.5, bf16[128,256]{1,0:T(8,128)(2,1)} %out_ref.3, bf16[3072,256]{1,0:T(8,128)(2,1)} %x_in.3, ...), custom_call_target="tpu_custom_call" | custom-call | tf_op jit(solution)/shard_map/pack/pallas_call | solution.py:860
  1.9 3.0 %collective-permute-start = (bf16[512,128]{1,0:T(8,128)(2,1)S(1)}, bf16[512,128]{1,0:T(8,128)(2,1)S(1)}, u32[]{:S(2)}, u32[]{:S(2)}) collective-permute-start(bf16[512,128]{1,0:T(8,128)(2,1)S(1)} %get-tuple-element.72), channel_id=1, source_target_pairs={{0,1},{1,0},{2,3},{3,2},{4,5},{5,4},{6,7},{7,6},{8,9},{9,8},{10,11... | collective-permute-start | bytes 393224 | tf_op jit(solution)/shard_map/ppermute | solution.py:1055
  5.0 0.1 collective-permute-start.1
  5.0 0.7 collective-permute-start.2
  5.8 4.3 %local.1 = (bf16[3072,256]{1,0:T(8,128)(2,1)S(1)}, bf16[3072,128]{1,0:T(8,128)(2,1)S(1)}, bf16[3072,128]{1,0:T(8,128)(2,1)S(1)}, bf16[3072,128]{1,0:T(8,128)(2,1...) custom-call(bf16[3072,256]{1,0:T(8,128)(2,1)S(1)} %copy-done, ...), custom_call_target="tpu_custom_call" | custom-call | tf_op jit(solution)/shard_map/local/pallas_call | solution.py:253
  10.2 0.4 collective-permute-done.1.near_rim
  10.5 3.0 %collective-permute-start.3 = (bf16[512,128]{1,0:T(8,128)(2,1)S(1)}, bf16[512,128]{1,0:T(8,128)(2,1)S(1)}, u32[]{:S(2)}, u32[]{:S(2)}) collective-permute-start(bf16[512,128]{1,0:T(8,128)(2,1)S(1)} %collective-permute-done.half_ref), channel_id=1, source_target_pairs={{0,2},{1,3},{2,0},{3,1},{4,6},{5,7},{6,4},{7,5},{8,10},{9,11},{10,... | collective-permute-start | bytes 393224 | tf_op jit(solution)/shard_map/ppermute | solution.py:960
  13.5 1.0 %collective-permute-done.3.other_half_ref = bf16[512,128]{1,0:T(8,128)(2,1)S(1)} collective-permute-done((bf16[512,128]{1,0:T(8,128)(2,1)S(1)}, bf16[512,128]{1,0:T(8,128)(2,1)S(1)}, u32[]{:S(2)}, u32[]{:S(2)}) %collective-permute-start.3) | collective-permute-done | bytes 131104 | tf_op jit(solution)/shard_map/ppermute | solution.py:960
  14.5 24.8 %layer.1 = (bf16[3136,128]{1,0:T(8,128)(2,1)S(1)}, bf16[3136,128]{1,0:T(8,128)(2,1)}, bf16[3072,1024]{1,0:T(8,128)(2,1)}, bf16[3072,256]{1,0:T(8,128)(2,1)}, f32...) custom-call(bf16[384,128]{1,0:T(8,128)(2,1)S(1)} %collective-permute-done.1.n, ...), custom_call_target="tpu_custom_call" | custom-call | tf_op jit(solution)/shard_map/layer/pallas_call | solution.py:691
  39.3 0.4 collective-permute-start.4
  39.8 2.2 %collective-permute-done.4 = bf16[3136,128]{1,0:T(8,128)(2,1)S(1)} collective-permute-done((bf16[3136,128]{1,0:T(8,128)(2,1)}, bf16[3136,128]{1,0:T(8,128)(2,1)S(1)}, u32[]{:S(2)}, u32[]{:S(2)}) %collective-permute-start.4) | collective-permute-done | bytes 802848 | tf_op jit(solution)/shard_map/ppermute | solution.py:960
  41.9 0.2 add_convert_fusion
  42.2 1.5 %collective-permute-start.5 = (bf16[784,128]{1,0:T(8,128)(2,1)S(1)}, bf16[784,128]{1,0:T(8,128)(2,1)S(1)}, u32[]{:S(2)}, u32[]{:S(2)}) collective-permute-start(bf16[784,128]{1,0:T(8,128)(2,1)S(1)} %get-tuple-element.134), channel_id=1, source_target_pairs={{0,1},{1,0},{2,18},{3,19},{4,5},{5,4},{6,22},{7,23},{8,9},{9,8},{1... | collective-permute-start | bytes 602120 | tf_op jit(solution)/shard_map/ppermute | solution.py:960
  43.7 1.5 %collective-permute-start.6 = (bf16[784,128]{1,0:T(8,128)(2,1)S(1)}, bf16[784,128]{1,0:T(8,128)(2,1)S(1)}, u32[]{:S(2)}, u32[]{:S(2)}) collective-permute-start(bf16[784,128]{1,0:T(8,128)(2,1)S(1)} %get-tuple-element.133), channel_id=1, source_target_pairs={{0,4},{1,5},{2,10},{3,11},{4,0},{5,1},{6,14},{7,15},{8,12},{9,13},... | collective-permute-start | bytes 602120 | tf_op jit(solution)/shard_map/ppermute | solution.py:960
  45.3 0.5 collective-permute-start.7
  45.8 5.7 %input_grad.1 = bf16[3072,256]{1,0:T(8,128)(2,1)} custom-call(bf16[3072,256]{1,0:T(8,128)(2,1)} %x_in.3, f32[3072,256]{1,0:T(8,128)} %get-tuple-element.95.mid_in, bf16[3072,768]{1,0:T(8,128)(2,1)} %get-tuple-element.96.dqkv_in, bf16[256,768]{1,0:T(8,128)(2,1)} %get-tuple-element.97.wqkv_in, f32[1,256]{1,0:T(1,128)S(1)} %bitcast.20), custom_call_target="tpu_custom_call" | custom-call | tf_op jit(solution)/shard_map/input_grad/pallas_call | solution.py:795
  51.5 0.4 collective-permute-done.7
  51.9 0.1 fusion.2
  52.0 3.4 %collective-permute-start.10 = (bf16[784,128]{1,0:T(8,128)(2,1)S(1)}, bf16[784,128]{1,0:T(8,128)(2,1)S(1)}, u32[]{:S(2)}, u32[]{:S(2)}) collective-permute-start(bf16[784,128]{1,0:T(8,128)(2,1)S(1)} %fusion.2), channel_id=1, source_target_pairs={{0,24},{1,25},{2,7},{3,6},{4,28},{5,29},{6,3},{7,2},{8,16},{9,17},... | collective-permute-start | bytes 602120 | tf_op jit(solution)/shard_map/ppermute | solution.py:960
  55.4 1.0 %collective-permute-start.9 = (bf16[784,128]{1,0:T(8,128)(2,1)S(1)}, bf16[784,128]{1,0:T(8,128)(2,1)S(1)}, u32[]{:S(2)}, u32[]{:S(2)}) collective-permute-start(bf16[784,128]{1,0:T(8,128)(2,1)S(1)} %fusion.2), channel_id=1, source_target_pairs={{0,16},{1,17},{2,6},{3,7},{4,20},{5,21},{6,2},{7,3},{8,24},{9,25},... | collective-permute-start | bytes 602120 | tf_op jit(solution)/shard_map/ppermute | solution.py:960
  56.5 5.7 %mixed.1 = bf16[3072,256]{1,0:T(8,128)(2,1)} custom-call(bf16[3072,256]{1,0:T(8,128)(2,1)} %x_in.3, bf16[3072,256]{1,0:T(8,128)(2,1)} %get-tuple-element.103.att_in, bf16[3072,1024]{1,0:T(8,128)(2,1)} %get-tuple-element.104.act_in, bf16[256,256]{1,0:T(8,128)(2,1)} %get-tuple-element.105.wout_in, bf16[1024,256]{1,0:T(8,128)(2,1)} %down_in.1, ...), custom_call_target="tpu_custom_call" | custom-call | tf_op jit(solution)/shard_map/mixed/pallas_call | solution.py:795
  62.2 0.6 collective-permute-done.8
  62.8 2.5 %collective-permute-done.9 = bf16[784,128]{1,0:T(8,128)(2,1)S(1)} collective-permute-done((bf16[784,128]{1,0:T(8,128)(2,1)S(1)}, bf16[784,128]{1,0:T(8,128)(2,1)S(1)}, u32[]{:S(2)}, u32[]{:S(2)}) %collective-permute-start.9) | collective-permute-done | bytes 200736 | tf_op jit(solution)/shard_map/ppermute | solution.py:960
  65.2 0.1 add_convert_fusion.1
  65.6 1.2 %collective-permute-start.11 = (bf16[656,128]{1,0:T(8,128)(2,1)S(1)}, bf16[656,128]{1,0:T(8,128)(2,1)S(1)}, u32[]{:S(2)}, u32[]{:S(2)}) collective-permute-start(bf16[656,128]{1,0:T(8,128)(2,1)S(1)} %pad_maximum_fusion.2), channel_id=1, source_target_pairs={{0,1},{1,0},{2,18},{3,19},{4,5},{5,4},{6,22},{7,23},{8,9},{9,8},{1... | collective-permute-start | bytes 503816 | tf_op jit(solution)/shard_map/ppermute | solution.py:960
  66.8 1.5 %collective-permute-start.13 = (bf16[656,128]{1,0:T(8,128)(2,1)S(1)}, bf16[656,128]{1,0:T(8,128)(2,1)S(1)}, u32[]{:S(2)}, u32[]{:S(2)}) collective-permute-start(bf16[656,128]{1,0:T(8,128)(2,1)S(1)} %pad_maximum_fusion.2), channel_id=1, source_target_pairs={{0,5},{1,4},{2,26},{3,27},{4,1},{5,0},{6,30},{7,31},{8,13},{9,12},... | collective-permute-start | bytes 503816 | tf_op jit(solution)/shard_map/ppermute | solution.py:960
  68.3 0.9 %collective-permute-start.12 = (bf16[784,128]{1,0:T(8,128)(2,1)S(1)}, bf16[784,128]{1,0:T(8,128)(2,1)S(1)}, u32[]{:S(2)}, u32[]{:S(2)}) collective-permute-start(bf16[784,128]{1,0:T(8,128)(2,1)S(1)} %pad_maximum_fusion.1), channel_id=1, source_target_pairs={{0,4},{1,5},{2,10},{3,11},{4,0},{5,1},{6,14},{7,15},{8,12},{9,13},... | collective-permute-start | bytes 602120 | tf_op jit(solution)/shard_map/ppermute | solution.py:960
  69.2 1.7 %collective-permute-done.11 = bf16[656,128]{1,0:T(8,128)(2,1)S(1)} collective-permute-done((bf16[656,128]{1,0:T(8,128)(2,1)S(1)}, bf16[656,128]{1,0:T(8,128)(2,1)S(1)}, u32[]{:S(2)}, u32[]{:S(2)}) %collective-permute-start.11) | collective-permute-done | bytes 167968 | tf_op jit(solution)/shard_map/ppermute | solution.py:960
  71.0 3.6 %collective-permute-done.12 = bf16[784,128]{1,0:T(8,128)(2,1)S(1)} collective-permute-done((bf16[784,128]{1,0:T(8,128)(2,1)S(1)}, bf16[784,128]{1,0:T(8,128)(2,1)S(1)}, u32[]{:S(2)}, u32[]{:S(2)}) %collective-permute-start.12) | collective-permute-done | bytes 200736 | tf_op jit(solution)/shard_map/ppermute | solution.py:960
  74.9 1.1 %finish.1 = (f32[256,128]{1,0:T(8,128)}, f32[256,128]{1,0:T(8,128)}, f32[256,128]{1,0:T(8,128)}, f32[128,256]{1,0:T(8,128)}, f32[256,1024]{1,0:T(8,128)}, /*index=5*/f32[1024,256]{1,0:T(8,128)}) custom-call(bf16[2624,128]{1,0:T(8,128)(2,1)S(1)} %pad_maximum_fusion.mine_ref.refs_0_), custom_call_target="tpu_custom_call" | custom-call | tf_op jit(solution)/shard_map/finish/pallas_call | solution.py:923
  76.0 1.0 %collective-permute-done.14.mine_ref = bf16[2624,128]{1,0:T(8,128)(2,1)S(1)} collective-permute-done((bf16[2624,128]{1,0:T(8,128)(2,1)S(1)}, bf16[2624,128]{1,0:T(8,128)(2,1)S(1)}, u32[]{:S(2)}, u32[]{:S(2)}) %collective-permute-start.14) | collective-permute-done | bytes 671776 | tf_op jit(solution)/shard_map/ppermute | solution.py:960
  77.0 1.7 %finish_rest.1 = (f32[256]{0:T(256)}, f32[256]{0:T(256)}, f32[256]{0:T(256)}, f32[256]{0:T(256)}, f32[256]{0:T(256)}, /*index=5*/f32[1024]{0:T(1024)}, f32[256,1...) custom-call(bf16[2624,128]{1,0:T(8,128)(2,1)S(1)} %collective-permut, ...), custom_call_target="tpu_custom_call", output_to_operand_aliasing={{6}: (2, {}), {7}: (3, {}), {8}: (4, {}), {9}: (5, {}), {10... | custom-call | tf_op jit(solution)/shard_map/finish_rest/pallas_call | solution.py:923
  (54 shorter events, 0.6 us)
Async XLA Ops:
  0.6 5.0 %copy-start = (bf16[3072,256]{1,0:T(8,128)(2,1)S(1)}, bf16[3072,256]{1,0:T(8,128)(2,1)}, u32[]{:S(2)}) copy-start(bf16[3072,256]{1,0:T(8,128)(2,1)} %x_in.3) | copy-start | bytes 4718596
  0.7 5.0 %copy-start.1 = (bf16[256,128]{1,0:T(8,128)(2,1)S(1)}, bf16[256,128]{1,0:T(8,128)(2,1)}, u32[]{:S(2)}) copy-start(bf16[256,128]{1,0:T(8,128)(2,1)} %query_ref.5) | copy-start | bytes 196612
  0.7 5.0 %copy-start.2 = (bf16[256,128]{1,0:T(8,128)(2,1)S(1)}, bf16[256,128]{1,0:T(8,128)(2,1)}, u32[]{:S(2)}) copy-start(bf16[256,128]{1,0:T(8,128)(2,1)} %key_ref.5) | copy-start | bytes 196612
  0.7 5.0 %copy-start.3 = (bf16[256,128]{1,0:T(8,128)(2,1)S(1)}, bf16[256,128]{1,0:T(8,128)(2,1)}, u32[]{:S(2)}) copy-start(bf16[256,128]{1,0:T(8,128)(2,1)} %value_ref.5) | copy-start | bytes 196612
  0.7 5.0 %copy-start.6 = (f32[256]{0:T(256)S(1)}, f32[256]{0:T(256)}, u32[]{:S(2)}) copy-start(f32[256]{0:T(256)} %param.20) | copy-start | bytes 3076
  0.7 5.0 %copy-start.7 = (f32[256]{0:T(256)S(1)}, f32[256]{0:T(256)}, u32[]{:S(2)}) copy-start(f32[256]{0:T(256)} %param.21) | copy-start | bytes 3076
  0.7 5.0 %copy-start.12 = (s32[128]{0:T(128)S(1)}, s32[128]{0:T(128)}, u32[]{:S(2)}) copy-start(s32[128]{0:T(128)} %param.18) | copy-start | bytes 1540
  0.7 5.0 %copy-start.13 = (s32[128]{0:T(128)S(1)}, s32[128]{0:T(128)}, u32[]{:S(2)}) copy-start(s32[128]{0:T(128)} %param.19) | copy-start | bytes 1540
  1.9 8.6 %collective-permute-start = (bf16[512,128]{1,0:T(8,128)(2,1)S(1)}, bf16[512,128]{1,0:T(8,128)(2,1)S(1)}, u32[]{:S(2)}, u32[]{:S(2)}) collective-permute-start(bf16[512,128]{1,0:T(8,128)(2,1)S(1)} %get-tuple-element.72), channel_id=1, source_target_pairs={{0,1},{1,0},{2,3},{3,2},{4,5},{5,4},{6,7},{7,6},{8,9},{9,8},{10,11... | collective-permute-start | bytes 393224 | tf_op jit(solution)/shard_map/ppermute | solution.py:1055
  5.0 5.6 %collective-permute-start.1 = (bf16[384,128]{1,0:T(8,128)(2,1)S(1)}, bf16[384,128]{1,0:T(8,128)(2,1)S(1)}, u32[]{:S(2)}, u32[]{:S(2)}) collective-permute-start(bf16[384,128]{1,0:T(8,128)(2,1)S(1)} %get-tuple-element.73), channel_id=1, source_target_pairs={{0,1},{1,0},{2,3},{3,2},{4,5},{5,4},{6,7},{7,6},{8,9},{9,8},{10,11... | collective-permute-start | bytes 294920 | tf_op jit(solution)/shard_map/ppermute | solution.py:1058
  5.0 5.5 %collective-permute-start.2 = (bf16[384,128]{1,0:T(8,128)(2,1)S(1)}, bf16[384,128]{1,0:T(8,128)(2,1)S(1)}, u32[]{:S(2)}, u32[]{:S(2)}) collective-permute-start(bf16[384,128]{1,0:T(8,128)(2,1)S(1)} %get-tuple-element.74), channel_id=1, source_target_pairs={{1,2},{3,4},{5,6},{7,8},{9,10},{11,12},{13,14},{15,16},{17,18},{19... | collective-permute-start | bytes 294920 | tf_op jit(solution)/shard_map/ppermute | solution.py:1057
  5.8 8.8 %copy-start.4 = (bf16[256,1024]{1,0:T(8,128)(2,1)S(1)}, bf16[256,1024]{1,0:T(8,128)(2,1)}, u32[]{:S(2)}) copy-start(bf16[256,1024]{1,0:T(8,128)(2,1)} %up_ref.1) | copy-start | bytes 1572868
  5.8 8.7 %copy-start.5 = (bf16[128,256]{1,0:T(8,128)(2,1)S(1)}, bf16[128,256]{1,0:T(8,128)(2,1)}, u32[]{:S(2)}) copy-start(bf16[128,256]{1,0:T(8,128)(2,1)} %out_ref.3) | copy-start | bytes 196612
  5.8 8.7 %copy-start.8 = (f32[1024]{0:T(1024)S(1)}, f32[1024]{0:T(1024)}, u32[]{:S(2)}) copy-start(f32[1024]{0:T(1024)} %param.29) | copy-start | bytes 12292
  5.8 8.7 %copy-start.9 = (f32[256]{0:T(256)S(1)}, f32[256]{0:T(256)}, u32[]{:S(2)}) copy-start(f32[256]{0:T(256)} %param.26) | copy-start | bytes 3076
  5.8 8.7 %copy-start.10 = (f32[256]{0:T(256)S(1)}, f32[256]{0:T(256)}, u32[]{:S(2)}) copy-start(f32[256]{0:T(256)} %param.27) | copy-start | bytes 3076
  10.5 4.0 %collective-permute-start.3 = (bf16[512,128]{1,0:T(8,128)(2,1)S(1)}, bf16[512,128]{1,0:T(8,128)(2,1)S(1)}, u32[]{:S(2)}, u32[]{:S(2)}) collective-permute-start(bf16[512,128]{1,0:T(8,128)(2,1)S(1)} %collective-permute-done.half_ref), channel_id=1, source_target_pairs={{0,2},{1,3},{2,0},{3,1},{4,6},{5,7},{6,4},{7,5},{8,10},{9,11},{10,... | collective-permute-start | bytes 393224 | tf_op jit(solution)/shard_map/ppermute | solution.py:960
  39.3 2.6 %collective-permute-start.4 = (bf16[3136,128]{1,0:T(8,128)(2,1)}, bf16[3136,128]{1,0:T(8,128)(2,1)S(1)}, u32[]{:S(2)}, u32[]{:S(2)}) collective-permute-start(bf16[3136,128]{1,0:T(8,128)(2,1)} %get-tuple-element.93), channel_id=1, source_target_pairs={{0,2},{1,3},{2,0},{3,1},{4,6},{5,7},{6,4},{7,5},{8,10},{9,11},{10,... | collective-permute-start | bytes 2408456 | tf_op jit(solution)/shard_map/ppermute | solution.py:960
  42.2 9.2 %collective-permute-start.5 = (bf16[784,128]{1,0:T(8,128)(2,1)S(1)}, bf16[784,128]{1,0:T(8,128)(2,1)S(1)}, u32[]{:S(2)}, u32[]{:S(2)}) collective-permute-start(bf16[784,128]{1,0:T(8,128)(2,1)S(1)} %get-tuple-element.134), channel_id=1, source_target_pairs={{0,1},{1,0},{2,18},{3,19},{4,5},{5,4},{6,22},{7,23},{8,9},{9,8},{1... | collective-permute-start | bytes 602120 | tf_op jit(solution)/shard_map/ppermute | solution.py:960
  43.7 7.7 %collective-permute-start.6 = (bf16[784,128]{1,0:T(8,128)(2,1)S(1)}, bf16[784,128]{1,0:T(8,128)(2,1)S(1)}, u32[]{:S(2)}, u32[]{:S(2)}) collective-permute-start(bf16[784,128]{1,0:T(8,128)(2,1)S(1)} %get-tuple-element.133), channel_id=1, source_target_pairs={{0,4},{1,5},{2,10},{3,11},{4,0},{5,1},{6,14},{7,15},{8,12},{9,13},... | collective-permute-start | bytes 602120 | tf_op jit(solution)/shard_map/ppermute | solution.py:960
  45.3 6.6 %collective-permute-start.7 = (bf16[784,128]{1,0:T(8,128)(2,1)S(1)}, bf16[784,128]{1,0:T(8,128)(2,1)S(1)}, u32[]{:S(2)}, u32[]{:S(2)}) collective-permute-start(bf16[784,128]{1,0:T(8,128)(2,1)S(1)} %get-tuple-element.132), channel_id=1, source_target_pairs={{0,5},{1,4},{2,26},{3,27},{4,1},{5,0},{6,30},{7,31},{8,13},{9,12},... | collective-permute-start | bytes 602120 | tf_op jit(solution)/shard_map/ppermute | solution.py:960
  45.8 10.7 %copy-start.11 = (f32[256]{0:T(256)S(1)}, f32[256]{0:T(256)}, u32[]{:S(2)}) copy-start(f32[256]{0:T(256)} %param.31) | copy-start | bytes 3076
  52.0 10.2 %collective-permute-start.10 = (bf16[784,128]{1,0:T(8,128)(2,1)S(1)}, bf16[784,128]{1,0:T(8,128)(2,1)S(1)}, u32[]{:S(2)}, u32[]{:S(2)}) collective-permute-start(bf16[784,128]{1,0:T(8,128)(2,1)S(1)} %fusion.2), channel_id=1, source_target_pairs={{0,24},{1,25},{2,7},{3,6},{4,28},{5,29},{6,3},{7,2},{8,16},{9,17},... | collective-permute-start | bytes 602120 | tf_op jit(solution)/shard_map/ppermute | solution.py:960
  55.4 7.3 %collective-permute-start.8 = (bf16[784,128]{1,0:T(8,128)(2,1)S(1)}, bf16[784,128]{1,0:T(8,128)(2,1)S(1)}, u32[]{:S(2)}, u32[]{:S(2)}) collective-permute-start(bf16[784,128]{1,0:T(8,128)(2,1)S(1)} %fusion.2), channel_id=1, source_target_pairs={{0,8},{1,9},{2,3},{3,2},{4,12},{5,13},{6,7},{7,6},{8,0},{9,1},{10,... | collective-permute-start | bytes 602120 | tf_op jit(solution)/shard_map/ppermute | solution.py:960
  55.4 9.8 %collective-permute-start.9 = (bf16[784,128]{1,0:T(8,128)(2,1)S(1)}, bf16[784,128]{1,0:T(8,128)(2,1)S(1)}, u32[]{:S(2)}, u32[]{:S(2)}) collective-permute-start(bf16[784,128]{1,0:T(8,128)(2,1)S(1)} %fusion.2), channel_id=1, source_target_pairs={{0,16},{1,17},{2,6},{3,7},{4,20},{5,21},{6,2},{7,3},{8,24},{9,25},... | collective-permute-start | bytes 602120 | tf_op jit(solution)/shard_map/ppermute | solution.py:960
  65.6 5.4 %collective-permute-start.11 = (bf16[656,128]{1,0:T(8,128)(2,1)S(1)}, bf16[656,128]{1,0:T(8,128)(2,1)S(1)}, u32[]{:S(2)}, u32[]{:S(2)}) collective-permute-start(bf16[656,128]{1,0:T(8,128)(2,1)S(1)} %pad_maximum_fusion.2), channel_id=1, source_target_pairs={{0,1},{1,0},{2,18},{3,19},{4,5},{5,4},{6,22},{7,23},{8,9},{9,8},{1... | collective-permute-start | bytes 503816 | tf_op jit(solution)/shard_map/ppermute | solution.py:960
  66.8 7.9 %collective-permute-start.13 = (bf16[656,128]{1,0:T(8,128)(2,1)S(1)}, bf16[656,128]{1,0:T(8,128)(2,1)S(1)}, u32[]{:S(2)}, u32[]{:S(2)}) collective-permute-start(bf16[656,128]{1,0:T(8,128)(2,1)S(1)} %pad_maximum_fusion.2), channel_id=1, source_target_pairs={{0,5},{1,4},{2,26},{3,27},{4,1},{5,0},{6,30},{7,31},{8,13},{9,12},... | collective-permute-start | bytes 503816 | tf_op jit(solution)/shard_map/ppermute | solution.py:960
  68.3 6.3 %collective-permute-start.12 = (bf16[784,128]{1,0:T(8,128)(2,1)S(1)}, bf16[784,128]{1,0:T(8,128)(2,1)S(1)}, u32[]{:S(2)}, u32[]{:S(2)}) collective-permute-start(bf16[784,128]{1,0:T(8,128)(2,1)S(1)} %pad_maximum_fusion.1), channel_id=1, source_target_pairs={{0,4},{1,5},{2,10},{3,11},{4,0},{5,1},{6,14},{7,15},{8,12},{9,13},... | collective-permute-start | bytes 602120 | tf_op jit(solution)/shard_map/ppermute | solution.py:960
  74.8 2.2 %collective-permute-start.14 = (bf16[2624,128]{1,0:T(8,128)(2,1)S(1)}, bf16[2624,128]{1,0:T(8,128)(2,1)S(1)}, u32[]{:S(2)}, u32[]{:S(2)}) collective-permute-start(bf16[2624,128]{1,0:T(8,128)(2,1)S(1)} %pad_maximum_fusion.mine_ref.refs_0_), channel_id=1, source_target_pairs={{0,2},{1,3},{2,0},{3,1},{4,6},{5,7},{6,4},{7,5},{8,10},{9,11},{10,... | collective-permute-start | bytes 2015240 | tf_op jit(solution)/shard_map/ppermute | solution.py:960
